TPU v7x, 128 devices: a whole 4x4x4 slice. The times are simulated.
128 devices in a mesh: dp: 8 (over y, core), mp: 16 (over x, z).
Axes of the slice: x: 4, y: 4, z: 4, core: 2. Of those that a mesh axis runs over, the one named last changes fastest.
Arguments:
- activations: bfloat16 [2, 2048, 4096], P(None, 'dp'), may hold values from -6 to 6
- cotangents: bfloat16 [2, 2048, 24576], P(None, 'dp', 'mp'), may hold values from -0.3125 to 0.3125
- left_root: bfloat16 [8, 16, 8, 512, 512], P('dp', 'mp')
- right_root: bfloat16 [8, 16, 8, 512, 512], P('dp', 'mp')
- block_owner: int32 [8, 16, 6], P('dp', 'mp'), may hold values from 0 to 15, as said below
- owned_sources: int32 [8, 16, 8], P('dp', 'mp'), may hold values from -1 to 15, as said below
- owner_counts: int32 [8, 16], P('dp', 'mp'), may hold values from 5 to 8, as said below
Outputs:
- precond: bfloat16 [2, 4096, 24576], P(None, 'dp', 'mp')
- left_stats: bfloat16 [8, 16, 8, 512, 512], P('dp', 'mp')
- right_stats: bfloat16 [8, 16, 8, 512, 512], P('dp', 'mp')
Inputs may be any that keep to these rules, and one draw needn't show every extreme that they name: In each group g no holder names one owner for two of its blocks; block_owner, owned_sources and owner_counts describe one assignment of the group's 6 x mp blocks. owned_sources[g, o, s] is the holder of owner o's s-th block, holders ascending, for s < owner_counts[g, o], and -1 after. `owner_counts`: in each group one owner holds exactly 8 blocks.
All inputs are finite; a program needn't handle non-finite values.
Results may differ from a plain program's by a relative error of at most 0.02.
Values may be sent and summed in bfloat16 or wider, within the bound.
No kernel may reach another device: no remote copies, remote signals or barrier semaphores. Data moves between devices by JAX's collectives and lax.ppermute only.
A program may use at most 192 MiB of HBM per device.

v0:
```python
import jax
import jax.numpy as jnp
from jax import lax
from jax.sharding import PartitionSpec as P


def on_device(
    activations, cotangents, left_root, right_root, block_owner, owned_sources, owner_counts
):
    group_count = lax.axis_size("dp")
    owner_total = lax.axis_size("mp")
    layer_count = activations.shape[0]
    row_count = activations.shape[2] // group_count
    block_size = left_root.shape[-1]
    col_width = cotangents.shape[2]
    col_blocks = col_width // block_size
    row_blocks = row_count // block_size
    summed = lax.psum_scatter(
        jnp.einsum(
            "ltd,ltc->dlc", activations, cotangents, preferred_element_type=jnp.float32
        ).astype(jnp.bfloat16),
        "dp",
        scatter_dimension=0,
        tiled=True,
    )
    my_blocks = (
        summed.reshape(row_blocks, block_size, layer_count, col_blocks, block_size)
        .transpose(2, 0, 3, 1, 4)
        .reshape(layer_count * row_blocks * col_blocks, block_size, block_size)
    )
    owners_of = block_owner.reshape(-1)
    owner_range = jnp.arange(owner_total, dtype=jnp.int32)
    send_route = (owners_of[:, None] == owner_range[None, :]).astype(jnp.bfloat16)
    outgoing = jnp.einsum(
        "tn,tab->nab", send_route, my_blocks, preferred_element_type=jnp.float32
    ).astype(jnp.bfloat16)
    arrived = lax.all_to_all(outgoing, "mp", split_axis=0, concat_axis=0, tiled=True)
    sources = owned_sources.reshape(-1)
    slot_total = sources.shape[0]
    live_slots = jnp.arange(slot_total, dtype=jnp.int32) < owner_counts.reshape(())
    slot_blocks = jnp.take(arrived, jnp.maximum(sources, 0), axis=0)
    left_gram = (
        jnp.einsum("sab,scb->sac", slot_blocks, slot_blocks, preferred_element_type=jnp.float32)
        / block_size
    )
    right_gram = (
        jnp.einsum("sba,sbc->sac", slot_blocks, slot_blocks, preferred_element_type=jnp.float32)
        / block_size
    )
    left_stats = jnp.where(live_slots[:, None, None], left_gram, 0.0).astype(jnp.bfloat16)
    right_stats = jnp.where(live_slots[:, None, None], right_gram, 0.0).astype(jnp.bfloat16)
    left_roots = left_root.reshape(slot_total, block_size, block_size)
    right_roots = right_root.reshape(slot_total, block_size, block_size)
    inner_prod = jnp.einsum(
        "sab,sbc->sac", left_roots, slot_blocks, preferred_element_type=jnp.float32
    ).astype(jnp.bfloat16)
    precond_slots = jnp.einsum(
        "sab,sbc->sac", inner_prod, right_roots, preferred_element_type=jnp.float32
    ).astype(jnp.bfloat16)
    back_route = (sources[:, None] == owner_range[None, :]).astype(jnp.bfloat16)
    returning = jnp.einsum(
        "sn,sab->nab", back_route, precond_slots, preferred_element_type=jnp.float32
    ).astype(jnp.bfloat16)
    returned = lax.all_to_all(returning, "mp", split_axis=0, concat_axis=0, tiled=True)
    mine_back = jnp.take(returned, owners_of, axis=0)
    precond = (
        mine_back.reshape(layer_count, row_blocks, col_blocks, block_size, block_size)
        .transpose(0, 1, 3, 2, 4)
        .reshape(layer_count, row_count, col_blocks * block_size)
    )
    stat_shape = (1, 1, slot_total, block_size, block_size)
    return (precond, left_stats.reshape(stat_shape), right_stats.reshape(stat_shape))


def solution(mesh):
    placed = (
        P(None, "dp", None),
        P(None, "dp", "mp"),
        P("dp", "mp", None, None, None),
        P("dp", "mp", None, None, None),
        P("dp", "mp", None),
        P("dp", "mp", None),
        P("dp", "mp"),
    )
    return jax.shard_map(
        on_device,
        mesh=mesh,
        in_specs=placed,
        out_specs=(
            P(None, "dp", "mp"),
            P("dp", "mp", None, None, None),
            P("dp", "mp", None, None, None),
        ),
        check_vma=False,
    )
```

profile of v0, /device:TPU:116, one launch (start us, length us, event | category | flops | bytes accessed | tf_op | source)
XLA Modules:
  0.0 561.5 jit_solution(15114663695529569358)
XLA Ops:
  7.2 0.0 copy-start
  7.2 0.0 reduce-scatter.2.cloned.1.call-start
  7.2 1.4 copy-done
  8.6 13.9 %convert_bitcast_fusion = bf16[4096,2,1536]{0,2,1:T(8,128)(2,1)} fusion(bf16[2,256,1536]{2,1,0:T(8,128)(2,1)S(1)} %copy-done, bf16[2,256,4096]{2,1,0:T(8,128)(2,1)} %param.7), kind=kOutput, calls=%fused_computation.2 | convolution fusion | flops 6455033856 | bytes 30932992 | tf_op jit(solution)/shard_map/ltd,ltc->dlc/dot_general | solution.py:19
  22.5 0.0 reduce-scatter.2.cloned.1.call-update
  22.5 0.0 copy-start.4
  22.6 130.4 %reduce-scatter.2.cloned.1.call-done = bf16[512,2,1536]{0,2,1:T(8,128)(2,1)} async-done(((bf16[4096,2,1536]{0,2,1:T(8,128)(2,1)}), bf16[512,2,1536]{0,2,1:T(8,128)(2,1)}) %reduce-scatter.2.cloned.1.call-update) | async-done | bytes 3145744 | tf_op jit(solution)/shard_map/reduce_scatter | solution.py:18
  152.9 7.7 %copy.27 = bf16[6,512,512]{2,0,1:T(8,128)(2,1)} copy(bf16[6,512,512]{1,2,0:T(8,128)(2,1)} %bitcast.49) | data formatting | bytes 6291456 | tf_op jit(solution)/shard_map/reshape | solution.py:29
  160.6 0.0 copy-done.4
  160.6 6.4 %convolution_convert_fusion.1 = bf16[16,512,512]{2,0,1:T(8,128)(2,1)} fusion(bf16[6,512,512]{2,0,1:T(8,128)(2,1)} %copy.27, s32[6]{0:T(128)S(1)} %bitcast.51), kind=kOutput, calls=%fused_computation.6 | convolution fusion | flops 54526048 | bytes 11534360 | tf_op jit(solution)/shard_map/tn,tab->nab/dot_general | solution.py:34
  167.1 11.4 %copy.28 = bf16[16,512,512]{2,1,0:T(8,128)(2,1)} copy(bf16[16,512,512]{2,0,1:T(8,128)(2,1)} %convolution_convert_fusion.1) | data formatting | bytes 16777216 | tf_op jit(solution)/shard_map/convert_element_type | solution.py:36
  178.4 0.0 copy-start.3
  178.4 7.3 %all-to-all-start = ((bf16[16,512,512]{2,1,0:T(8,128)(2,1)}), bf16[16,512,512]{2,1,0:T(8,128)(2,1)}, u32[]{:S(2)}, u32[]{:S(2)}) async-start(bf16[16,512,512]{2,1,0:T(8,128)(2,1)} %copy.28), calls=%async_computation.1 | async-start | bytes 16777216 | tf_op jit(solution)/shard_map/all_to_all | solution.py:37
  186.3 0.0 copy-done.3
  186.4 156.6 %all-to-all-done = bf16[16,512,512]{2,1,0:T(8,128)(2,1)} async-done(((bf16[16,512,512]{2,1,0:T(8,128)(2,1)}), bf16[16,512,512]{2,1,0:T(8,128)(2,1)}, u32[]{:S(2)}, u32[]{:S(2)}) %all-to-all-start) | async-done | bytes 8388640 | tf_op jit(solution)/shard_map/all_to_all | solution.py:37
  343.0 6.2 %gather_fusion = bf16[8,512,512]{2,1,0:T(8,128)(2,1)} fusion(bf16[16,512,512]{2,1,0:T(8,128)(2,1)} %all-to-all-done, s32[1024]{0:T(1024)S(1)} %pad_clamp_fusion.1), kind=kCustom, calls=%fused_computation | custom fusion | bytes 8388640 | tf_op jit(solution)/shard_map/jit(_take)/gather | solution.py:41
  349.2 11.5 %fusion.8 = bf16[8,512,512]{2,1,0:T(8,128)(2,1)} fusion(bf16[1,1,8,512,512]{4,3,2,1,0:T(8,128)(2,1)} %param.10, bf16[1,1,8,512,512]{4,3,2,1,0:T(8,128)(2,1)} %param.9, bf16[8,512,512]{2,1,0:T(8,128)(2,1)} %gather_fusion, pred[8]{0:T(512)(128)(4,1)S(1)} %get-tuple-element.10), kind=kOutput, calls=%fused_computation.17 | convolution fusion | flops 4301258752 | bytes 16777224 | tf_op jit(solution)/shard_map/sab,sbc->sac/dot_general | solution.py:57
  360.6 7.3 %convolution_convert_fusion = bf16[16,512,512]{2,0,1:T(8,128)(2,1)} fusion(bf16[8,512,512]{2,1,0:T(8,128)(2,1)} %fusion.8, s32[8]{0:T(128)S(1)} %bitcast.50), kind=kOutput, calls=%fused_computation.5 | convolution fusion | flops 71303296 | bytes 12582944 | tf_op jit(solution)/shard_map/sn,sab->nab/dot_general | solution.py:61
  368.0 11.4 %copy.32 = bf16[16,512,512]{2,1,0:T(8,128)(2,1)} copy(bf16[16,512,512]{2,0,1:T(8,128)(2,1)} %convolution_convert_fusion) | data formatting | bytes 16777216 | tf_op jit(solution)/shard_map/convert_element_type | solution.py:63
  379.3 7.2 %all-to-all-start.1 = ((bf16[16,512,512]{2,1,0:T(8,128)(2,1)}), bf16[16,512,512]{2,1,0:T(8,128)(2,1)}, u32[]{:S(2)}, u32[]{:S(2)}) async-start(bf16[16,512,512]{2,1,0:T(8,128)(2,1)} %copy.32), calls=%async_computation.2 | async-start | bytes 16777216 | tf_op jit(solution)/shard_map/all_to_all | solution.py:64
  386.5 0.5 broadcast.110
  387.0 0.7 reduce.3
  387.7 0.1 reshape.111
  387.8 0.0 copy-start.2
  387.8 8.6 %fusion.1 = bf16[1,1,8,512,512]{4,3,2,1,0:T(8,128)(2,1)} fusion(pred[8]{0:T(512)(128)(4,1)S(1)} %get-tuple-element.9, bf16[8,512,512]{2,1,0:T(8,128)(2,1)} %gather_fusion, pred[8]{0:T(512)(128)(4,1)S(1)} %get-tuple-element.10), kind=kOutput, calls=%fused_computation.8 | convolution fusion | flops 2155872256 | bytes 8388624 | tf_op jit(solution)/shard_map/sba,sbc->sac/dot_general | solution.py:47
  396.4 0.0 copy-done.2
  396.4 4.5 fusion
  400.9 134.5 %all-to-all-done.1 = bf16[16,512,512]{2,1,0:T(8,128)(2,1)} async-done(((bf16[16,512,512]{2,1,0:T(8,128)(2,1)}), bf16[16,512,512]{2,1,0:T(8,128)(2,1)}, u32[]{:S(2)}, u32[]{:S(2)}) %all-to-all-start.1) | async-done | bytes 8388640 | tf_op jit(solution)/shard_map/all_to_all | solution.py:64
  535.4 5.9 %gather_fusion.1 = bf16[6,512,512]{2,1,0:T(8,128)(2,1)} fusion(bf16[16,512,512]{2,1,0:T(8,128)(2,1)} %all-to-all-done.1, s32[1024]{0:T(1024)S(1)} %pad_clamp_fusion), kind=kCustom, calls=%fused_computation.1 | custom fusion | bytes 6291480 | tf_op jit(solution)/shard_map/jit(_take)/gather | solution.py:65
  541.3 3.9 select_bitcast_fusion
  545.2 0.0 copy-start.1
  545.2 4.8 copy.33
  550.0 4.6 copy.35
  554.6 0.0 copy-done.1
  (6 shorter events, 0.0 us)
Async XLA Ops:
  7.2 1.4 copy-start
  7.2 145.7 %reduce-scatter.2.cloned.1.call-start = ((), (), s32[]{:S(2)}) async-start(), calls=%async_computation.3 | async-start | bytes 28311552 | tf_op jit(solution)/shard_map/reduce_scatter | solution.py:18
  22.5 138.1 %copy-start.4 = (s32[1,1,6]{2,1,0:T(1,128)S(1)}, s32[1,1,6]{2,1,0:T(1,128)}, u32[]{:S(2)}) copy-start(s32[1,1,6]{2,1,0:T(1,128)} %param.11) | copy-start | bytes 76
  178.4 7.9 %copy-start.3 = (s32[1,1,8]{2,1,0:T(1,128)S(1)}, s32[1,1,8]{2,1,0:T(1,128)}, u32[]{:S(2)}) copy-start(s32[1,1,8]{2,1,0:T(1,128)} %param.12) | copy-start | bytes 100
  178.4 164.6 %all-to-all-start = ((bf16[16,512,512]{2,1,0:T(8,128)(2,1)}), bf16[16,512,512]{2,1,0:T(8,128)(2,1)}, u32[]{:S(2)}, u32[]{:S(2)}) async-start(bf16[16,512,512]{2,1,0:T(8,128)(2,1)} %copy.28), calls=%async_computation.1 | async-start | bytes 16777216 | tf_op jit(solution)/shard_map/all_to_all | solution.py:37
  379.3 156.1 %all-to-all-start.1 = ((bf16[16,512,512]{2,1,0:T(8,128)(2,1)}), bf16[16,512,512]{2,1,0:T(8,128)(2,1)}, u32[]{:S(2)}, u32[]{:S(2)}) async-start(bf16[16,512,512]{2,1,0:T(8,128)(2,1)} %copy.32), calls=%async_computation.2 | async-start | bytes 16777216 | tf_op jit(solution)/shard_map/all_to_all | solution.py:64
  387.8 8.7 %copy-start.2 = (bf16[8,512,512]{2,1,0:T(8,128)(2,1)S(1)}, bf16[8,512,512]{2,1,0:T(8,128)(2,1)}, u32[]{:S(2)}) copy-start(bf16[8,512,512]{2,1,0:T(8,128)(2,1)} %gather_fusion) | copy-start | bytes 12582916
  545.2 9.4 %copy-start.1 = (bf16[2,256,1536]{2,1,0:T(8,128)(2,1)S(1)}, bf16[2,256,1536]{2,1,0:T(8,128)(2,1)}, u32[]{:S(2)}) copy-start(bf16[2,256,1536]{2,1,0:T(8,128)(2,1)} %param.8) | copy-start | bytes 4718596
Sparse Core Ops, SparseCore 0:
  22.7 130.2 reduce-scatter.1
where the time goes:
time: 562 us; the launch traced here: 561 us
  waiting for transfers between devices  421 us (75%)
  local copies, waits for them, and re-layouts  53.9 us (10%)
  matrix products  52.3 us (9%)
  between operations  14.8 us (3%)
  starting transfers between devices  14.5 us (3%)
    all_to_all x1, waiting for transfers between devices, on_device(): lax.all_to_all(outgoing, 'mp', split_axis=0, concat_axis=0, tiled=True)  157 us
    all_to_all x1, waiting for transfers between devices, on_device(): lax.all_to_all(returning, 'mp', split_axis=0, concat_axis=0, tiled=True)  134 us
    reduce_scatter x1, waiting for transfers between devices, on_device(): lax.psum_scatter(jnp.einsum('ltd,ltc->dlc', activations, cotangents, pref...  130 us
    dot_general x1, matrix products, on_device(): jnp.einsum('ltd,ltc->dlc', activations, cotangents, preferred_element_typ...  13.9 us
    dot_general x1, matrix products, on_device(): jnp.einsum('sab,sbc->sac', inner_prod, right_roots, preferred_element_typ...  11.5 us
    convert_element_type x1, local copies, waits for them, and re-layouts, on_device(): outgoing = jnp.einsum('tn,tab->nab', send_route, my_blocks, preferred_ele...  11.4 us
    convert_element_type x1, local copies, waits for them, and re-layouts, on_device(): returning = jnp.einsum('sn,sab->nab', back_route, precond_slots, preferre...  11.4 us
  transfers between devices with their start and end apart: 3, of which 3 were waited for; matrix products, arithmetic and copies ran while one was open for 3% of the time, Pallas kernels for 0%

commit v1 on v0

v1 whole, which is shorter than its diff:
```python
import functools

import jax
import jax.numpy as jnp
from jax import lax
from jax.experimental import pallas as pl
from jax.experimental.pallas import tpu as pltpu
from jax.sharding import PartitionSpec as P

CHUNKS = 2
SIDE = 4
CORES = 2
TABLE_ROWS = 16
MIB = 1024 * 1024

NT = (((1,), (1,)), ((), ()))
NN = (((1,), (0,)), ((), ()))
TN = (((0,), (0,)), ((), ()))


def dot(a, b, dims):
    return lax.dot_general(a, b, dims, preferred_element_type=jnp.float32)


def along_y(value, hops):
    pairs = [
        (y * CORES + c, (y + hops) % SIDE * CORES + c) for y in range(SIDE) for c in range(CORES)
    ]
    return lax.ppermute(value, "dp", pairs)


def other_core(value):
    pairs = [(y * CORES + c, y * CORES + 1 - c) for y in range(SIDE) for c in range(CORES)]
    return lax.ppermute(value, "dp", pairs)


def along_x(value, hops):
    pairs = [(x * SIDE + z, (x + hops) % SIDE * SIDE + z) for x in range(SIDE) for z in range(SIDE)]
    return lax.ppermute(value, "mp", pairs)


def along_z(value, hops):
    pairs = [(x * SIDE + z, x * SIDE + (z + hops) % SIDE) for x in range(SIDE) for z in range(SIDE)]
    return lax.ppermute(value, "mp", pairs)


def ring(value, move):
    return (value, move(value, 1), move(value, -1), move(value, 2))


def exchange(value):
    return lax.all_to_all(value, "mp", split_axis=0, concat_axis=0, tiled=True)


def after(value, *needed):
    return lax.optimization_barrier((value,) + needed)[0]


def split_kernel(owner_ref, cot_ref, out_ref):
    layers, tokens, width = cot_ref.shape
    parts, piece = out_ref.shape[0], TABLE_ROWS
    size = parts * piece * CHUNKS
    cols = width // size
    for layer in range(layers):
        for col in range(cols):
            turned = cot_ref[layer, :, col * size : (col + 1) * size].T
            for q in range(CHUNKS):
                row = ((q * layers + layer) * cols + col) * piece
                half = turned[q * parts * piece : (q + 1) * parts * piece]
                out_ref[:, row : row + piece, :] = half.reshape(parts, piece, tokens)
    rows = lax.broadcasted_iota(jnp.int32, (TABLE_ROWS, tokens), 0)
    table = jnp.zeros((TABLE_ROWS, tokens), jnp.float32)
    for t in range(layers * cols):
        table = jnp.where(rows == t, owner_ref[t].astype(jnp.float32), table)
    base = CHUNKS * layers * cols * piece
    for part in range(parts):
        out_ref[part, base : base + TABLE_ROWS, :] = table.astype(out_ref.dtype)


def split_cotangents(owners, cotangents, owner_total):
    layers, tokens, width = cotangents.shape
    rows = width * layers // owner_total
    return pl.pallas_call(
        split_kernel,
        in_specs=[
            pl.BlockSpec(memory_space=pltpu.SMEM),
            pl.BlockSpec(memory_space=pltpu.VMEM),
        ],
        out_specs=pl.BlockSpec(memory_space=pltpu.VMEM),
        out_shape=jax.ShapeDtypeStruct((owner_total, rows + TABLE_ROWS, tokens), cotangents.dtype),
        compiler_params=pltpu.CompilerParams(vmem_limit_bytes=12 * MIB),
        cost_estimate=pl.CostEstimate(
            flops=0, bytes_accessed=4 * cotangents.size, transcendentals=0
        ),
        name="split_cotangents",
    )(owners, cotangents)


def lay_kernel(place_ref, *refs):
    out_ref = refs[-1]
    rows = refs[0].shape[2]
    half = out_ref.shape[2] // 2
    for u in range(2):
        for hops, piece in zip((0, SIDE - 1, 1, 2), refs[4 * u : 4 * u + 4]):
            start = u * half + lax.rem(place_ref[u] + hops, SIDE) * rows
            out_ref[:, :, pl.ds(pl.multiple_of(start, rows), rows), :] = piece[...]


def lay_activations(place, pieces):
    chips, layers, rows, width = pieces[0].shape
    shape = (chips, layers, 2 * SIDE * rows, width)
    return pl.pallas_call(
        lay_kernel,
        in_specs=[pl.BlockSpec(memory_space=pltpu.SMEM)]
        + [pl.BlockSpec(memory_space=pltpu.VMEM)] * len(pieces),
        out_specs=pl.BlockSpec(memory_space=pltpu.VMEM),
        out_shape=jax.ShapeDtypeStruct(shape, pieces[0].dtype),
        compiler_params=pltpu.CompilerParams(vmem_limit_bytes=14 * MIB),
        cost_estimate=pl.CostEstimate(
            flops=0, bytes_accessed=16 * 2 * SIDE * pieces[0].size, transcendentals=0
        ),
        name="lay_activations",
    )(place, *pieces)


def partial_kernel(core_ref, act_ref, *refs):
    parts, (kept_ref, given_ref) = refs[:-2], refs[-2:]
    holders, rows, tokens = parts[0].shape
    width = kept_ref.shape[-1]
    flat = [part[...].reshape(holders * rows, tokens) for part in parts]
    for out_ref, which in ((kept_ref, core_ref[0]), (given_ref, 1 - core_ref[0])):
        columns = pl.ds(pl.multiple_of(which * width, width), width)
        total = dot(flat[0], act_ref[0, 0, :, columns], NN)
        for n in range(1, len(flat)):
            total += dot(flat[n], act_ref[n, 0, :, columns], NN)
        out_ref[...] = total.astype(out_ref.dtype).reshape(out_ref.shape)


def gradient_partials(core, acts, parts):
    chips, layers, tokens, width = acts.shape
    holders, all_rows, _ = parts[0].shape
    rows, size = all_rows // layers, width // CORES
    shape = jax.ShapeDtypeStruct((holders, all_rows, size), acts.dtype)
    return pl.pallas_call(
        partial_kernel,
        grid_spec=pltpu.PrefetchScalarGridSpec(
            num_scalar_prefetch=1,
            grid=(layers, 2),
            in_specs=[pl.BlockSpec((chips, 1, tokens, width), lambda l, h, s: (0, l, 0, 0))]
            + [pl.BlockSpec((holders // 2, rows, tokens), lambda l, h, s: (h, l, 0))] * len(parts),
            out_specs=[pl.BlockSpec((holders // 2, rows, size), lambda l, h, s: (h, l, 0))] * 2,
        ),
        out_shape=[shape, shape],
        compiler_params=pltpu.CompilerParams(vmem_limit_bytes=24 * MIB),
        cost_estimate=pl.CostEstimate(
            flops=2 * holders * all_rows * chips * tokens * width,
            bytes_accessed=2 * (acts.size + chips * parts[0].size + 2 * holders * all_rows * size),
            transcendentals=0,
        ),
        name="gradient_partials",
    )(core, acts, *parts)


def deal_kernel(slot_ref, kept_ref, got_ref, out_ref):
    layer, half = pl.program_id(0), pl.program_id(1)
    holders, rows, _ = kept_ref.shape
    piece = out_ref.shape[1]
    cols = rows // piece
    for holder in range(holders):
        total = kept_ref[holder].astype(jnp.float32) + got_ref[holder].astype(jnp.float32)
        total = total.astype(out_ref.dtype)
        for col in range(cols):
            slot = slot_ref[((half * holders + holder) * 2 + layer) * cols + col]
            out_ref[slot] = total[col * piece : (col + 1) * piece]


def deal_to_slots(slots, kept, got, slot_total):
    holders, all_rows, size = kept.shape
    layers = 2
    rows = all_rows // layers
    shape = (holders * slot_total, TABLE_ROWS, size)
    return pl.pallas_call(
        deal_kernel,
        grid_spec=pltpu.PrefetchScalarGridSpec(
            num_scalar_prefetch=1,
            grid=(layers, 2),
            in_specs=[pl.BlockSpec((holders // 2, rows, size), lambda l, h, s: (h, l, 0))] * 2,
            out_specs=pl.BlockSpec(shape, lambda l, h, s: (0, 0, 0)),
        ),
        out_shape=jax.ShapeDtypeStruct(shape, kept.dtype),
        compiler_params=pltpu.CompilerParams(vmem_limit_bytes=16 * MIB),
        cost_estimate=pl.CostEstimate(
            flops=kept.size, bytes_accessed=8 * kept.size, transcendentals=0
        ),
        name="deal_to_slots",
    )(slots, kept, got)


def turned_block(slice_refs):
    width = slice_refs[0].shape[-1]
    return jnp.concatenate([ref[...].reshape(-1, width) for ref in slice_refs], axis=0)


def slot_kernel(source_ref, count_ref, left_ref, right_ref, *refs):
    slice_refs, (out_ref, left_stat_ref, right_stat_ref) = refs[:-3], refs[-3:]
    is_live = pl.program_id(0) < count_ref[0]

    @pl.when(is_live)
    def _():
        turned = turned_block(slice_refs)
        inner = dot(left_ref[0], turned, NT).astype(out_ref.dtype)
        out_ref[0] = dot(inner, right_ref[0], NN).astype(out_ref.dtype)
        scale = 1.0 / turned.shape[0]
        left_stat_ref[0] = (dot(turned, turned, TN) * scale).astype(left_stat_ref.dtype)
        right_stat_ref[0] = (dot(turned, turned, NT) * scale).astype(right_stat_ref.dtype)

    @pl.when(jnp.logical_not(is_live))
    def _():
        left_stat_ref[...] = jnp.zeros_like(left_stat_ref)
        right_stat_ref[...] = jnp.zeros_like(right_stat_ref)


def work_on_slots(sources, counts, left_roots, right_roots, arrived, owner_total):
    slot_total, size, _ = left_roots.shape

    def out_place(s, source, count):
        return (source[jnp.minimum(s, count[0] - 1)], 0, 0)

    def live(s, source, count):
        return (s, 0, 0)

    def slice_spec(a):
        return pl.BlockSpec((a.shape[0], 1) + a.shape[2:], lambda s, *_: (0, s, 0, 0))

    stats = jax.ShapeDtypeStruct((slot_total, size, size), left_roots.dtype)
    return pl.pallas_call(
        slot_kernel,
        grid_spec=pltpu.PrefetchScalarGridSpec(
            num_scalar_prefetch=2,
            grid=(slot_total,),
            in_specs=[pl.BlockSpec((1, size, size), live)] * 2 + [slice_spec(a) for a in arrived],
            out_specs=[
                pl.BlockSpec((1, size, size), out_place),
                pl.BlockSpec((1, size, size), live),
                pl.BlockSpec((1, size, size), live),
            ],
        ),
        out_shape=[jax.ShapeDtypeStruct((owner_total, size, size), left_roots.dtype), stats, stats],
        compiler_params=pltpu.CompilerParams(vmem_limit_bytes=24 * MIB),
        cost_estimate=pl.CostEstimate(
            flops=8 * slot_total * size**3,
            bytes_accessed=12 * slot_total * size * size,
            transcendentals=0,
        ),
        name="work_on_slots",
    )(sources, counts, left_roots, right_roots, *arrived)


def place_kernel(owner_ref, returned_ref, out_ref, held, in_sems, out_sems):
    layers, size, width = out_ref.shape
    cols = width // size
    blocks = [(l, c, l * cols + c) for l in range(layers) for c in range(cols)]
    fetches = [
        pltpu.make_async_copy(returned_ref.at[owner_ref[t]], held.at[t], in_sems.at[t])
        for _, _, t in blocks
    ]
    stores = [
        pltpu.make_async_copy(
            held.at[t], out_ref.at[l, :, pl.ds(c * size, size)], out_sems.at[t]
        )
        for l, c, t in blocks
    ]
    for fetch in fetches:
        fetch.start()
    for fetch, store in zip(fetches, stores):
        fetch.wait()
        store.start()
    for store in stores:
        store.wait()


def place_blocks(owners, returned, layers, cols):
    _, size, _ = returned.shape
    return pl.pallas_call(
        place_kernel,
        in_specs=[
            pl.BlockSpec(memory_space=pltpu.SMEM),
            pl.BlockSpec(memory_space=pl.ANY),
        ],
        out_specs=pl.BlockSpec(memory_space=pl.ANY),
        out_shape=jax.ShapeDtypeStruct((layers, size, cols * size), returned.dtype),
        scratch_shapes=[
            pltpu.VMEM((layers * cols, size, size), returned.dtype),
            pltpu.SemaphoreType.DMA((layers * cols,)),
            pltpu.SemaphoreType.DMA((layers * cols,)),
        ],
        compiler_params=pltpu.CompilerParams(vmem_limit_bytes=8 * MIB),
        cost_estimate=pl.CostEstimate(
            flops=0, bytes_accessed=4 * layers * cols * size * size, transcendentals=0
        ),
        name="place_blocks",
    )(owners, returned)


def activations_for_chips(activations, chip_y, place):
    layers, tokens, width = activations.shape
    rows = tokens // 2 // SIDE
    pair_width = width // SIDE
    mine = jnp.stack(
        [
            lax.dynamic_slice(
                activations, (0, u * (tokens // 2) + place[u] * rows, 0), (layers, rows, width)
            )
            for u in range(2)
        ]
    )
    return [
        lax.dynamic_slice(
            mine,
            (0, 0, 0, lax.rem(chip_y + hops, SIDE) * pair_width),
            mine.shape[:3] + (pair_width,),
        )
        for hops in (0, 1, SIDE - 1, 2)
    ]


def on_device(
    activations, cotangents, left_root, right_root, block_owner, owned_sources, owner_counts
):
    owner_total = lax.axis_size("mp")
    layers, _, width = cotangents.shape
    slot_total, size = left_root.shape[2], left_root.shape[-1]
    cols = width // size
    blocks = layers * cols
    owners = block_owner.reshape(-1)
    group, holder = lax.axis_index("dp"), lax.axis_index("mp")
    chip_y, core = group // CORES, lax.rem(group, CORES)
    place = (lax.rem(holder, SIDE), holder // SIDE)

    for_chips = activations_for_chips(activations, chip_y, place)
    from_chips = [for_chips[0]] + [
        along_y(piece, hops) for piece, hops in zip(for_chips[1:], (1, -1, 2))
    ]
    spread = exchange(split_cotangents(owners, after(cotangents, *for_chips), owner_total))
    base = spread.shape[1] - TABLE_ROWS
    chunk = base // CHUNKS

    own_piece = after(from_chips[0], spread)
    halves = [jnp.stack([own_piece[u]] + [piece[u] for piece in from_chips[1:]]) for u in range(2)]
    first_parts = ring(spread[:, :chunk], along_y)
    pieces = ring(halves[0], along_z) + ring(halves[1], along_x)
    moved = lax.optimization_barrier(first_parts + pieces)
    first_parts, pieces = moved[:SIDE], moved[SIDE:]
    acts = lay_activations(jnp.stack(place).astype(jnp.int32), pieces)
    second_parts = ring(after(spread[:, chunk:base], *first_parts), along_y)

    owner_of = spread[:, base : base + blocks, 0].astype(jnp.int32)
    all_owners = jnp.arange(owner_total, dtype=jnp.int32)
    named = (owner_of[:, :, None] == all_owners).astype(jnp.int32)
    given = jnp.sum(named, axis=1)
    earlier = (all_owners[:, None] > all_owners[None, :]).astype(jnp.int32)
    slot_of = jnp.sum(earlier[:, :, None] * given[None, :, :], axis=1)
    slots = (owner_of * slot_total + jnp.sum(named * slot_of[:, None, :], axis=-1)).reshape(-1)

    def sliced_slots(core, parts):
        kept, given = gradient_partials(core, acts, parts)
        return exchange(deal_to_slots(slots, kept, other_core(given), slot_total))

    core = core.reshape(1).astype(jnp.int32)
    arrived = sliced_slots(after(core, slots), first_parts)
    more = sliced_slots(after(core, arrived), second_parts)

    def by_slot(value):
        return value.reshape((owner_total, slot_total) + value.shape[1:])

    returning, left_stats, right_stats = work_on_slots(
        owned_sources.reshape(-1),
        owner_counts.reshape(-1),
        left_root.reshape(slot_total, size, size),
        right_root.reshape(slot_total, size, size),
        (by_slot(arrived), by_slot(more)),
        owner_total,
    )
    precond = place_blocks(owners, exchange(returning), layers, cols)
    stat_shape = (1, 1, slot_total, size, size)
    return (precond, left_stats.reshape(stat_shape), right_stats.reshape(stat_shape))


def solution(mesh):
    placed = (
        P(None, "dp", None),
        P(None, "dp", "mp"),
        P("dp", "mp", None, None, None),
        P("dp", "mp", None, None, None),
        P("dp", "mp", None),
        P("dp", "mp", None),
        P("dp", "mp"),
    )
    return jax.shard_map(
        on_device,
        mesh=mesh,
        in_specs=placed,
        out_specs=(
            P(None, "dp", "mp"),
            P("dp", "mp", None, None, None),
            P("dp", "mp", None, None, None),
        ),
        check_vma=False,
    )
```

time: 562 us -> 313 us (0.56)
  the two profiles are of different devices: /device:TPU:116 before, /device:TPU:0 now
where the time goes in v1:
time: 313 us; the launch traced here: 312 us
  waiting for transfers between devices  115 us (37%)
  blocking collectives  98.6 us (32%)
  starting transfers between devices  47.7 us (15%)
  Pallas kernels  35.7 us (11%)
  local copies, waits for them, and re-layouts  11.8 us (4%)
    all_to_all x1, blocking collectives, exchange(): return lax.all_to_all(value, 'mp', split_axis=0, concat_axis=0, tiled=True)  98.6 us
    all_to_all x3, waiting for transfers between devices, exchange(): return lax.all_to_all(value, 'mp', split_axis=0, concat_axis=0, tiled=True)  67.8 us
    all_to_all x3, starting transfers between devices, exchange(): return lax.all_to_all(value, 'mp', split_axis=0, concat_axis=0, tiled=True)  21.8 us
    ppermute x9, starting transfers between devices, along_y(): return lax.ppermute(value, 'dp', pairs)  18.3 us
    ppermute x9, waiting for transfers between devices, along_y(): return lax.ppermute(value, 'dp', pairs)  18.3 us
    pallas_call x2, Pallas kernels, gradient_partials(): pl.pallas_call(partial_kernel, grid_spec=pltpu.PrefetchScalarGridSpec(num...  12.2 us
    pallas_call x1, Pallas kernels, work_on_slots(): pl.pallas_call(slot_kernel, grid_spec=pltpu.PrefetchScalarGridSpec(num_sc...  11.8 us
    ppermute x3, waiting for transfers between devices, along_x(): return lax.ppermute(value, 'mp', pairs)  11.2 us
  transfers between devices with their start and end apart: 20, of which 16 were waited for; matrix products, arithmetic and copies ran while one was open for 1% of the time, Pallas kernels for 0%

profile of v1, /device:TPU:0, one launch (start us, length us, event | category | flops | bytes accessed | tf_op | source)
XLA Modules:
  0.0 311.8 jit_solution(1471825814652771814)
XLA Ops:
  0.7 1.4 dynamic-slice_bitcast_fusion
  2.4 2.2 split_cotangents.1
  4.6 8.0 %all-to-all-start = ((bf16[16,208,256]{2,1,0:T(8,128)(2,1)}), bf16[16,208,256]{2,1,0:T(8,128)(2,1)S(1)}, u32[]{:S(2)}, u32[]{:S(2)}) async-start(bf16[16,208,256]{2,1,0:T(8,128)(2,1)} %split_cotangents.1), calls=%async_computation | async-start | bytes 3407872 | tf_op jit(solution)/shard_map/all_to_all | solution.py:52
  12.6 3.3 %collective-permute-start.5 = (bf16[2,2,32,1024]{3,2,1,0:T(8,128)(2,1)S(1)}, bf16[2,2,32,1024]{3,2,1,0:T(8,128)(2,1)S(1)}, u32[]{:S(2)}, u32[]{:S(2)}) collective-permute-start(bf16[2,2,32,1024]{3,2,1,0:T(8,128)(2,1)S(1)} %get-tuple-element.55), channel_id=1, source_target_pairs={{0,64},{16,80},{32,96},{48,112},{64,0},{80,16},{96,32},{112,48},{1... | collective-permute-start | bytes 786440 | tf_op jit(solution)/shard_map/ppermute | solution.py:29
  15.9 0.7 collective-permute-start.3
  16.6 2.6 collective-permute-start.4
  19.1 4.3 %collective-permute-done.5 = bf16[2,2,32,1024]{3,2,1,0:T(8,128)(2,1)S(1)} collective-permute-done((bf16[2,2,32,1024]{3,2,1,0:T(8,128)(2,1)S(1)}, bf16[2,2,32,1024]{3,2,1,0:T(8,128)(2,1)S(1)}, u32[]{:S(2)}, u32[]{:S(2)}) %collective-permute-start.5) | collective-permute-done | bytes 262176 | tf_op jit(solution)/shard_map/ppermute | solution.py:29
  23.4 4.1 %collective-permute-done.3 = bf16[2,2,32,1024]{3,2,1,0:T(8,128)(2,1)S(1)} collective-permute-done((bf16[2,2,32,1024]{3,2,1,0:T(8,128)(2,1)S(1)}, bf16[2,2,32,1024]{3,2,1,0:T(8,128)(2,1)S(1)}, u32[]{:S(2)}, u32[]{:S(2)}) %collective-permute-start.3) | collective-permute-done | bytes 262176 | tf_op jit(solution)/shard_map/ppermute | solution.py:29
  27.9 10.0 %all-to-all-done = bf16[16,208,256]{2,1,0:T(8,128)(2,1)S(1)} async-done(((bf16[16,208,256]{2,1,0:T(8,128)(2,1)}), bf16[16,208,256]{2,1,0:T(8,128)(2,1)S(1)}, u32[]{:S(2)}, u32[]{:S(2)}) %all-to-all-start) | async-done | bytes 1703968 | tf_op jit(solution)/shard_map/all_to_all | solution.py:52
  38.0 1.2 copy-done.9
  39.7 2.9 collective-permute-start.7
  42.6 1.9 collective-permute-start.11
  44.8 3.3 %collective-permute-start.2 = (bf16[16,96,256]{2,1,0:T(8,128)(2,1)S(1)}, bf16[16,96,256]{2,1,0:T(8,128)(2,1)}, u32[]{:S(2)}, u32[]{:S(2)}) collective-permute-start(bf16[16,96,256]{2,1,0:T(8,128)(2,1)S(1)} %get-tuple-element.38.refs_0_), channel_id=1, source_target_pairs={{0,64},{16,80},{32,96},{48,112},{64,0},{80,16},{96,32},{112,48},{1... | collective-permute-start | bytes 2359304 | tf_op jit(solution)/shard_map/ppermute | solution.py:29
  48.0 7.7 %collective-permute-done.8.refs_3_ = bf16[4,2,32,1024]{3,2,1,0:T(8,128)(2,1)S(1)} collective-permute-done((bf16[4,2,32,1024]{3,2,1,0:T(8,128)(2,1)S(1)}, bf16[4,2,32,1024]{3,2,1,0:T(8,128)(2,1)S(1)}, u32[]{:S(2)}, u32[]{:S(2)}) %collective-permute-start.8) | collective-permute-done | bytes 524320 | tf_op jit(solution)/shard_map/ppermute | solution.py:44
  55.7 3.0 collective-permute-start.1
  58.7 2.8 collective-permute-done.7.refs_2_
  61.5 0.8 copy-done.3
  62.3 1.6 collective-permute-start
  64.4 0.8 collective-permute-start.10
  65.2 1.3 collective-permute-start.9
  66.5 0.8 slice_convert_fusion
  68.1 9.0 %collective-permute-done.10.refs_6_ = bf16[4,2,32,1024]{3,2,1,0:T(8,128)(2,1)} collective-permute-done((bf16[4,2,32,1024]{3,2,1,0:T(8,128)(2,1)S(1)}, bf16[4,2,32,1024]{3,2,1,0:T(8,128)(2,1)}, u32[]{:S(2)}, u32[]{:S(2)}) %collective-permute-start.10) | collective-permute-done | bytes 524320 | tf_op jit(solution)/shard_map/ppermute | solution.py:39
  77.1 2.1 collective-permute-done.9.refs_5_
  79.2 0.8 collective-permute-done.1.refs_2_
  80.1 2.0 collective-permute-done.refs_1_
  82.1 1.0 copy-done.4
  83.1 1.8 lay_activations.1.act_ref
  85.0 6.5 %gradient_partials.2 = (bf16[16,96,512]{2,1,0:T(8,128)(2,1)S(1)}, bf16[16,96,512]{2,1,0:T(8,128)(2,1)S(1)}) custom-call(s32[1]{0:T(128)} %bitcast.8.core_ref, bf16[4,2,256,1024]{3,2,1,0:T(8,128)(2,1)S(1)} %lay_activations.1.act_ref, bf16[16,96,256]{2,1,0:T(8,128)(2,1)S(1)} %get-tuple-element.38.refs_0_, bf16[16,96,256]{2,1,0:T(8,128)(2,1)} %collective-permute-done.refs_1_, ...), custom_call_target="tpu_custom_call" | custom-call | flops 3221225472 | bytes 10485760 | tf_op jit(solution)/shard_map/gradient_partials/pallas_call | solution.py:144
  91.6 3.4 %collective-permute-done.12.got_ref = bf16[16,96,512]{2,1,0:T(8,128)(2,1)S(1)} collective-permute-done((bf16[16,96,512]{2,1,0:T(8,128)(2,1)S(1)}, bf16[16,96,512]{2,1,0:T(8,128)(2,1)S(1)}, u32[]{:S(2)}, u32[]{:S(2)}) %collective-permute-start.12) | collective-permute-done | bytes 1572896 | tf_op jit(solution)/shard_map/ppermute | solution.py:34
  95.0 2.6 deal_to_slots.2
  97.5 6.8 %all-to-all-start.1 = ((bf16[128,16,512]{2,1,0:T(8,128)(2,1)}), bf16[128,16,512]{2,1,0:T(8,128)(2,1)S(1)}, u32[]{:S(2)}, u32[]{:S(2)}) async-start(bf16[128,16,512]{2,1,0:T(8,128)(2,1)} %deal_to_slots.2), calls=%async_computation.1 | async-start | bytes 4194304 | tf_op jit(solution)/shard_map/all_to_all | solution.py:52
  104.4 1.9 collective-permute-start.15
  106.3 1.1 collective-permute-start.14
  107.3 1.0 collective-permute-start.13
  108.3 27.2 %all-to-all-done.1 = bf16[128,16,512]{2,1,0:T(8,128)(2,1)S(1)} async-done(((bf16[128,16,512]{2,1,0:T(8,128)(2,1)}), bf16[128,16,512]{2,1,0:T(8,128)(2,1)S(1)}, u32[]{:S(2)}, u32[]{:S(2)}) %all-to-all-start.1) | async-done | bytes 2097184 | tf_op jit(solution)/shard_map/all_to_all | solution.py:52
  135.5 5.8 %collective-permute-done.14.refs_2_ = bf16[16,96,256]{2,1,0:T(8,128)(2,1)} collective-permute-done((bf16[16,96,256]{2,1,0:T(8,128)(2,1)S(1)}, bf16[16,96,256]{2,1,0:T(8,128)(2,1)}, u32[]{:S(2)}, u32[]{:S(2)}) %collective-permute-start.14) | collective-permute-done | bytes 786464 | tf_op jit(solution)/shard_map/ppermute | solution.py:29
  141.3 0.9 collective-permute-done.13.refs_1_
  142.2 2.2 copy-done.1
  144.4 5.8 %gradient_partials.3 = (bf16[16,96,512]{2,1,0:T(8,128)(2,1)S(1)}, bf16[16,96,512]{2,1,0:T(8,128)(2,1)S(1)}) custom-call(s32[1]{0:T(128)} %bitcast.8.core_ref, bf16[4,2,256,1024]{3,2,1,0:T(8,128)(2,1)S(1)} %copy-done.1, bf16[16,96,256]{2,1,0:T(8,128)(2,1)S(1)} %get-tuple-element.45.refs_0_, bf16[16,96,256]{2,1,0:T(8,128)(2,1)} %collective-permute-done.13.refs_1_, ...), custom_call_target="tpu_custom_call" | custom-call | flops 3221225472 | bytes 10485760 | tf_op jit(solution)/shard_map/gradient_partials/pallas_call | solution.py:144
  150.2 3.4 %collective-permute-done.16.got_ref = bf16[16,96,512]{2,1,0:T(8,128)(2,1)S(1)} collective-permute-done((bf16[16,96,512]{2,1,0:T(8,128)(2,1)S(1)}, bf16[16,96,512]{2,1,0:T(8,128)(2,1)S(1)}, u32[]{:S(2)}, u32[]{:S(2)}) %collective-permute-start.16) | collective-permute-done | bytes 1572896 | tf_op jit(solution)/shard_map/ppermute | solution.py:34
  153.6 2.6 deal_to_slots.3
  156.2 7.0 %all-to-all-start.2 = ((bf16[128,16,512]{2,1,0:T(8,128)(2,1)}), bf16[128,16,512]{2,1,0:T(8,128)(2,1)}, u32[]{:S(2)}, u32[]{:S(2)}) async-start(bf16[128,16,512]{2,1,0:T(8,128)(2,1)} %deal_to_slots.3), calls=%async_computation.2 | async-start | bytes 4194304 | tf_op jit(solution)/shard_map/all_to_all | solution.py:52
  163.9 30.6 %all-to-all-done.2 = bf16[128,16,512]{2,1,0:T(8,128)(2,1)} async-done(((bf16[128,16,512]{2,1,0:T(8,128)(2,1)}), bf16[128,16,512]{2,1,0:T(8,128)(2,1)}, u32[]{:S(2)}, u32[]{:S(2)}) %all-to-all-start.2) | async-done | bytes 2097184 | tf_op jit(solution)/shard_map/all_to_all | solution.py:52
  194.5 2.2 copy-done.6
  196.7 2.2 copy-done.7
  198.8 11.8 %work_on_slots.1 = (bf16[16,512,512]{2,1,0:T(8,128)(2,1)S(1)}, bf16[8,512,512]{2,1,0:T(8,128)(2,1)}, bf16[8,512,512]{2,1,0:T(8,128)(2,1)}) custom-call(s32[8]{0:T(128)S(1)} %bitcast.23, s32[1]{0:T(128)} %bitcast.17.count_ref, bf16[8,512,512]{2,1,0:T(8,128)(2,1)S(1)} %bitcast.21, bf16[8,512,512]{2,1,0:T(8,128)(2,1)S(1)} %bitcast.22, ...), custom_call_target="tpu_custom_call" | custom-call | flops 8589934592 | bytes 25165824 | tf_op jit(solution)/shard_map/work_on_slots/pallas_call | solution.py:236
  210.7 98.6 %all_to_all.20.returned_ref = bf16[16,512,512]{2,1,0:T(8,128)(2,1)S(1)} all-to-all(bf16[16,512,512]{2,1,0:T(8,128)(2,1)S(1)} %get-tuple-element.48), channel_id=1, replica_groups=mesh['dp'=8,'mp'=16] {'mp'}, dimensions={0} | all-to-all | bytes 16777216 | tf_op jit(solution)/shard_map/all_to_all | solution.py:52
  309.3 2.5 place_blocks.1
  (44 shorter events, 3.0 us)
Async XLA Ops:
  0.7 1.7 copy-start.2
  0.7 1.7 copy-start.5
  4.6 33.3 %all-to-all-start = ((bf16[16,208,256]{2,1,0:T(8,128)(2,1)}), bf16[16,208,256]{2,1,0:T(8,128)(2,1)S(1)}, u32[]{:S(2)}, u32[]{:S(2)}) async-start(bf16[16,208,256]{2,1,0:T(8,128)(2,1)} %split_cotangents.1), calls=%async_computation | async-start | bytes 3407872 | tf_op jit(solution)/shard_map/all_to_all | solution.py:52
  12.6 10.8 %collective-permute-start.5 = (bf16[2,2,32,1024]{3,2,1,0:T(8,128)(2,1)S(1)}, bf16[2,2,32,1024]{3,2,1,0:T(8,128)(2,1)S(1)}, u32[]{:S(2)}, u32[]{:S(2)}) collective-permute-start(bf16[2,2,32,1024]{3,2,1,0:T(8,128)(2,1)S(1)} %get-tuple-element.55), channel_id=1, source_target_pairs={{0,64},{16,80},{32,96},{48,112},{64,0},{80,16},{96,32},{112,48},{1... | collective-permute-start | bytes 786440 | tf_op jit(solution)/shard_map/ppermute | solution.py:29
  15.9 11.7 %collective-permute-start.3 = (bf16[2,2,32,1024]{3,2,1,0:T(8,128)(2,1)S(1)}, bf16[2,2,32,1024]{3,2,1,0:T(8,128)(2,1)S(1)}, u32[]{:S(2)}, u32[]{:S(2)}) collective-permute-start(bf16[2,2,32,1024]{3,2,1,0:T(8,128)(2,1)S(1)} %get-tuple-element.57), channel_id=1, source_target_pairs={{0,32},{16,48},{32,64},{48,80},{64,96},{80,112},{96,0},{112,16},{1... | collective-permute-start | bytes 786440 | tf_op jit(solution)/shard_map/ppermute | solution.py:29
  16.6 11.4 %collective-permute-start.4 = (bf16[2,2,32,1024]{3,2,1,0:T(8,128)(2,1)S(1)}, bf16[2,2,32,1024]{3,2,1,0:T(8,128)(2,1)S(1)}, u32[]{:S(2)}, u32[]{:S(2)}) collective-permute-start(bf16[2,2,32,1024]{3,2,1,0:T(8,128)(2,1)S(1)} %get-tuple-element.58), channel_id=1, source_target_pairs={{0,96},{16,112},{32,0},{48,16},{64,32},{80,48},{96,64},{112,80},{1... | collective-permute-start | bytes 786440 | tf_op jit(solution)/shard_map/ppermute | solution.py:29
  38.0 1.2 copy-start.9
  39.2 5.4 %copy-start.10 = (bf16[16,208,256]{2,1,0:T(8,128)(2,1)S(1)}, bf16[16,208,256]{2,1,0:T(8,128)(2,1)}, u32[]{:S(2)}) copy-start(bf16[16,208,256]{2,1,0:T(8,128)(2,1)} %copy-done.9) | copy-start | bytes 5111812
  39.2 16.4 %collective-permute-start.8 = (bf16[4,2,32,1024]{3,2,1,0:T(8,128)(2,1)S(1)}, bf16[4,2,32,1024]{3,2,1,0:T(8,128)(2,1)S(1)}, u32[]{:S(2)}, u32[]{:S(2)}) collective-permute-start(bf16[4,2,32,1024]{3,2,1,0:T(8,128)(2,1)S(1)} %pad_maximum_fusion.refs_0_), channel_id=1, source_target_pairs={{0,2},{1,3},{2,0},{3,1},{4,6},{5,7},{6,4},{7,5},{8,10},{9,11},{10,... | collective-permute-start | bytes 1572872 | tf_op jit(solution)/shard_map/ppermute | solution.py:44
  39.7 21.8 %collective-permute-start.7 = (bf16[4,2,32,1024]{3,2,1,0:T(8,128)(2,1)S(1)}, bf16[4,2,32,1024]{3,2,1,0:T(8,128)(2,1)S(1)}, u32[]{:S(2)}, u32[]{:S(2)}) collective-permute-start(bf16[4,2,32,1024]{3,2,1,0:T(8,128)(2,1)S(1)} %pad_maximum_fusion.refs_0_), channel_id=1, source_target_pairs={{0,3},{1,0},{2,1},{3,2},{4,7},{5,4},{6,5},{7,6},{8,11},{9,8},{10,9... | collective-permute-start | bytes 1572872 | tf_op jit(solution)/shard_map/ppermute | solution.py:44
  42.6 21.9 %collective-permute-start.6 = (bf16[4,2,32,1024]{3,2,1,0:T(8,128)(2,1)S(1)}, bf16[4,2,32,1024]{3,2,1,0:T(8,128)(2,1)}, u32[]{:S(2)}, u32[]{:S(2)}) collective-permute-start(bf16[4,2,32,1024]{3,2,1,0:T(8,128)(2,1)S(1)} %pad_maximum_fusion.refs_0_), channel_id=1, source_target_pairs={{0,1},{1,2},{2,3},{3,0},{4,5},{5,6},{6,7},{7,4},{8,9},{9,10},{10,1... | collective-permute-start | bytes 1572872 | tf_op jit(solution)/shard_map/ppermute | solution.py:44
  42.6 22.6 %collective-permute-start.11 = (bf16[4,2,32,1024]{3,2,1,0:T(8,128)(2,1)S(1)}, bf16[4,2,32,1024]{3,2,1,0:T(8,128)(2,1)}, u32[]{:S(2)}, u32[]{:S(2)}) collective-permute-start(bf16[4,2,32,1024]{3,2,1,0:T(8,128)(2,1)S(1)} %pad_maximum_fusion.1.refs_4_), channel_id=1, source_target_pairs={{0,8},{1,9},{2,10},{3,11},{4,12},{5,13},{6,14},{7,15},{8,0},{9,1},... | collective-permute-start | bytes 1572872 | tf_op jit(solution)/shard_map/ppermute | solution.py:39
  44.8 34.5 %collective-permute-start.2 = (bf16[16,96,256]{2,1,0:T(8,128)(2,1)S(1)}, bf16[16,96,256]{2,1,0:T(8,128)(2,1)}, u32[]{:S(2)}, u32[]{:S(2)}) collective-permute-start(bf16[16,96,256]{2,1,0:T(8,128)(2,1)S(1)} %get-tuple-element.38.refs_0_), channel_id=1, source_target_pairs={{0,64},{16,80},{32,96},{48,112},{64,0},{80,16},{96,32},{112,48},{1... | collective-permute-start | bytes 2359304 | tf_op jit(solution)/shard_map/ppermute | solution.py:29
  55.7 24.4 %collective-permute-start.1 = (bf16[16,96,256]{2,1,0:T(8,128)(2,1)S(1)}, bf16[16,96,256]{2,1,0:T(8,128)(2,1)}, u32[]{:S(2)}, u32[]{:S(2)}) collective-permute-start(bf16[16,96,256]{2,1,0:T(8,128)(2,1)S(1)} %get-tuple-element.38.refs_0_), channel_id=1, source_target_pairs={{0,96},{16,112},{32,0},{48,16},{64,32},{80,48},{96,64},{112,80},{1... | collective-permute-start | bytes 2359304 | tf_op jit(solution)/shard_map/ppermute | solution.py:29
  61.5 0.8 copy-start.3
  62.3 19.8 %collective-permute-start = (bf16[16,96,256]{2,1,0:T(8,128)(2,1)S(1)}, bf16[16,96,256]{2,1,0:T(8,128)(2,1)}, u32[]{:S(2)}, u32[]{:S(2)}) collective-permute-start(bf16[16,96,256]{2,1,0:T(8,128)(2,1)S(1)} %get-tuple-element.38.refs_0_), channel_id=1, source_target_pairs={{0,32},{16,48},{32,64},{48,80},{64,96},{80,112},{96,0},{112,16},{1... | collective-permute-start | bytes 2359304 | tf_op jit(solution)/shard_map/ppermute | solution.py:29
  64.4 12.7 %collective-permute-start.10 = (bf16[4,2,32,1024]{3,2,1,0:T(8,128)(2,1)S(1)}, bf16[4,2,32,1024]{3,2,1,0:T(8,128)(2,1)}, u32[]{:S(2)}, u32[]{:S(2)}) collective-permute-start(bf16[4,2,32,1024]{3,2,1,0:T(8,128)(2,1)S(1)} %pad_maximum_fusion.1.refs_4_), channel_id=1, source_target_pairs={{0,12},{1,13},{2,14},{3,15},{4,0},{5,1},{6,2},{7,3},{8,4},{9,5},{1... | collective-permute-start | bytes 1572872 | tf_op jit(solution)/shard_map/ppermute | solution.py:39
  65.2 14.0 %collective-permute-start.9 = (bf16[4,2,32,1024]{3,2,1,0:T(8,128)(2,1)S(1)}, bf16[4,2,32,1024]{3,2,1,0:T(8,128)(2,1)}, u32[]{:S(2)}, u32[]{:S(2)}) collective-permute-start(bf16[4,2,32,1024]{3,2,1,0:T(8,128)(2,1)S(1)} %pad_maximum_fusion.1.refs_4_), channel_id=1, source_target_pairs={{0,4},{1,5},{2,6},{3,7},{4,8},{5,9},{6,10},{7,11},{8,12},{9,13},{1... | collective-permute-start | bytes 1572872 | tf_op jit(solution)/shard_map/ppermute | solution.py:39
  82.1 1.0 copy-start.4
  84.9 6.5 %copy-start = (bf16[4,2,256,1024]{3,2,1,0:T(8,128)(2,1)}, bf16[4,2,256,1024]{3,2,1,0:T(8,128)(2,1)S(1)}, u32[]{:S(2)}) copy-start(bf16[4,2,256,1024]{3,2,1,0:T(8,128)(2,1)S(1)} %lay_activations.1.act_ref) | copy-start | bytes 12582916
  91.5 3.5 %collective-permute-start.12 = (bf16[16,96,512]{2,1,0:T(8,128)(2,1)S(1)}, bf16[16,96,512]{2,1,0:T(8,128)(2,1)S(1)}, u32[]{:S(2)}, u32[]{:S(2)}) collective-permute-start(bf16[16,96,512]{2,1,0:T(8,128)(2,1)S(1)} %get-tuple-element.43), channel_id=1, source_target_pairs={{0,16},{16,0},{32,48},{48,32},{64,80},{80,64},{96,112},{112,96},{1... | collective-permute-start | bytes 4718600 | tf_op jit(solution)/shard_map/ppermute | solution.py:34
  97.5 38.0 %all-to-all-start.1 = ((bf16[128,16,512]{2,1,0:T(8,128)(2,1)}), bf16[128,16,512]{2,1,0:T(8,128)(2,1)S(1)}, u32[]{:S(2)}, u32[]{:S(2)}) async-start(bf16[128,16,512]{2,1,0:T(8,128)(2,1)} %deal_to_slots.2), calls=%async_computation.1 | async-start | bytes 4194304 | tf_op jit(solution)/shard_map/all_to_all | solution.py:52
  104.4 31.2 %collective-permute-start.15 = (bf16[16,96,256]{2,1,0:T(8,128)(2,1)S(1)}, bf16[16,96,256]{2,1,0:T(8,128)(2,1)}, u32[]{:S(2)}, u32[]{:S(2)}) collective-permute-start(bf16[16,96,256]{2,1,0:T(8,128)(2,1)S(1)} %get-tuple-element.45.refs_0_), channel_id=1, source_target_pairs={{0,64},{16,80},{32,96},{48,112},{64,0},{80,16},{96,32},{112,48},{1... | collective-permute-start | bytes 2359304 | tf_op jit(solution)/shard_map/ppermute | solution.py:29
  106.3 35.1 %collective-permute-start.14 = (bf16[16,96,256]{2,1,0:T(8,128)(2,1)S(1)}, bf16[16,96,256]{2,1,0:T(8,128)(2,1)}, u32[]{:S(2)}, u32[]{:S(2)}) collective-permute-start(bf16[16,96,256]{2,1,0:T(8,128)(2,1)S(1)} %get-tuple-element.45.refs_0_), channel_id=1, source_target_pairs={{0,96},{16,112},{32,0},{48,16},{64,32},{80,48},{96,64},{112,80},{1... | collective-permute-start | bytes 2359304 | tf_op jit(solution)/shard_map/ppermute | solution.py:29
  107.3 34.9 %collective-permute-start.13 = (bf16[16,96,256]{2,1,0:T(8,128)(2,1)S(1)}, bf16[16,96,256]{2,1,0:T(8,128)(2,1)}, u32[]{:S(2)}, u32[]{:S(2)}) collective-permute-start(bf16[16,96,256]{2,1,0:T(8,128)(2,1)S(1)} %get-tuple-element.45.refs_0_), channel_id=1, source_target_pairs={{0,32},{16,48},{32,64},{48,80},{64,96},{80,112},{96,0},{112,16},{1... | collective-permute-start | bytes 2359304 | tf_op jit(solution)/shard_map/ppermute | solution.py:29
  142.2 2.2 copy-start.1
  150.2 3.5 %collective-permute-start.16 = (bf16[16,96,512]{2,1,0:T(8,128)(2,1)S(1)}, bf16[16,96,512]{2,1,0:T(8,128)(2,1)S(1)}, u32[]{:S(2)}, u32[]{:S(2)}) collective-permute-start(bf16[16,96,512]{2,1,0:T(8,128)(2,1)S(1)} %get-tuple-element.47), channel_id=1, source_target_pairs={{0,16},{16,0},{32,48},{48,32},{64,80},{80,64},{96,112},{112,96},{1... | collective-permute-start | bytes 4718600 | tf_op jit(solution)/shard_map/ppermute | solution.py:34
  156.2 38.3 %copy-start.8 = (s32[1,1,8]{2,1,0:T(1,128)S(1)}, s32[1,1,8]{2,1,0:T(1,128)}, u32[]{:S(2)}) copy-start(s32[1,1,8]{2,1,0:T(1,128)} %param.12) | copy-start | bytes 100
  156.2 38.3 %all-to-all-start.2 = ((bf16[128,16,512]{2,1,0:T(8,128)(2,1)}), bf16[128,16,512]{2,1,0:T(8,128)(2,1)}, u32[]{:S(2)}, u32[]{:S(2)}) async-start(bf16[128,16,512]{2,1,0:T(8,128)(2,1)} %deal_to_slots.3), calls=%async_computation.2 | async-start | bytes 4194304 | tf_op jit(solution)/shard_map/all_to_all | solution.py:52
  194.5 2.2 copy-start.6
  196.7 2.2 copy-start.7

commit v2 on v1

v2 whole, which is shorter than its diff:
```python
import functools

import jax
import jax.numpy as jnp
from jax import lax
from jax.experimental import pallas as pl
from jax.experimental.pallas import tpu as pltpu
from jax.sharding import PartitionSpec as P

CHUNKS = 2
SIDE = 4
CORES = 2
TABLE_ROWS = 16
MIB = 1024 * 1024

NT = (((1,), (1,)), ((), ()))
NN = (((1,), (0,)), ((), ()))
TN = (((0,), (0,)), ((), ()))


def dot(a, b, dims):
    return lax.dot_general(a, b, dims, preferred_element_type=jnp.float32)


def along_y(value, hops):
    pairs = [
        (y * CORES + c, (y + hops) % SIDE * CORES + c) for y in range(SIDE) for c in range(CORES)
    ]
    return lax.ppermute(value, "dp", pairs)


def other_core(value):
    pairs = [(y * CORES + c, y * CORES + 1 - c) for y in range(SIDE) for c in range(CORES)]
    return lax.ppermute(value, "dp", pairs)


def along_z(value, hops):
    pairs = [(x * SIDE + z, x * SIDE + (z + hops) % SIDE) for x in range(SIDE) for z in range(SIDE)]
    return lax.ppermute(value, "mp", pairs)


def ring_in_two(value, move):
    half = value.shape[0] // 2
    before, behind = move(value, 1), move(value, -1)
    return (value, before, behind, move(before[:half], 1), move(behind[half:], -1))


def exchange(value):
    return lax.all_to_all(value, "mp", split_axis=0, concat_axis=0, tiled=True)


def after(value, *needed):
    return lax.optimization_barrier((value,) + needed)[0]


def split_kernel(owner_ref, cot_ref, out_ref):
    layers, tokens, width = cot_ref.shape
    parts, piece = out_ref.shape[0], TABLE_ROWS
    size = parts * piece * CHUNKS
    cols = width // size
    for layer in range(layers):
        for col in range(cols):
            turned = cot_ref[layer, :, col * size : (col + 1) * size].T
            for q in range(CHUNKS):
                row = ((q * layers + layer) * cols + col) * piece
                half = turned[q * parts * piece : (q + 1) * parts * piece]
                out_ref[:, row : row + piece, :] = half.reshape(parts, piece, tokens)
    rows = lax.broadcasted_iota(jnp.int32, (TABLE_ROWS, tokens), 0)
    table = jnp.zeros((TABLE_ROWS, tokens), jnp.float32)
    for t in range(layers * cols):
        table = jnp.where(rows == t, owner_ref[t].astype(jnp.float32), table)
    base = CHUNKS * layers * cols * piece
    for part in range(parts):
        out_ref[part, base : base + TABLE_ROWS, :] = table.astype(out_ref.dtype)


def split_cotangents(owners, cotangents, owner_total):
    layers, tokens, width = cotangents.shape
    rows = width * layers // owner_total
    return pl.pallas_call(
        split_kernel,
        in_specs=[
            pl.BlockSpec(memory_space=pltpu.SMEM),
            pl.BlockSpec(memory_space=pltpu.VMEM),
        ],
        out_specs=pl.BlockSpec(memory_space=pltpu.VMEM),
        out_shape=jax.ShapeDtypeStruct((owner_total, rows + TABLE_ROWS, tokens), cotangents.dtype),
        compiler_params=pltpu.CompilerParams(vmem_limit_bytes=6 * MIB),
        cost_estimate=pl.CostEstimate(
            flops=0, bytes_accessed=4 * cotangents.size, transcendentals=0
        ),
        name="split_cotangents",
    )(owners, cotangents)


def partial_kernel(here_ref, *refs):
    pieces, parts, (kept_ref, given_ref, acts, held, sems) = refs[:4], refs[4:-5], refs[-5:]
    _, layers, count, _ = pieces[0].shape
    _, holders, all_rows, tokens = held.shape
    width = kept_ref.shape[-1]
    rows, half = all_rows // layers, holders // 2

    def fetches(layer):
        moves = []
        for n, part in enumerate(parts):
            to = held.at[min(n, 3)]
            if part.shape[0] == half:
                to = to.at[pl.ds((n - 3) * half, half)]
            mine = pl.ds(layer * rows, rows)
            moves.append((part.at[:, mine, :], to.at[:, mine, :]))
        for n, piece in enumerate(pieces):
            first = here_ref[1] if n < 2 else 1 - here_ref[1]
            start = pl.multiple_of((first * 2 + n % 2) * count, count)
            moves.append((piece.at[:, layer], acts.at[layer, :, pl.ds(start, count), :]))
        return [pltpu.make_async_copy(*move, sems.at[layer, n]) for n, move in enumerate(moves)]

    for layer in range(layers):
        for fetch in fetches(layer):
            fetch.start()
    for layer in range(layers):
        for fetch in fetches(layer):
            fetch.wait()
        mine = slice(layer * rows, (layer + 1) * rows)
        for side in range(2):
            some = slice(side * half, (side + 1) * half)
            flat = [held[n, some, mine, :].reshape(half * rows, tokens) for n in range(4)]
            for out_ref, which in ((kept_ref, here_ref[0]), (given_ref, 1 - here_ref[0])):
                columns = pl.ds(pl.multiple_of(which * width, width), width)
                total = dot(flat[0], acts[layer, 0, :, columns], NN)
                for n in range(1, SIDE):
                    total += dot(flat[n], acts[layer, n, :, columns], NN)
                out_ref[some, mine, :] = total.astype(out_ref.dtype).reshape(half, rows, width)


def gradient_partials(here, pieces, parts):
    chips, layers, _, width = pieces[0].shape
    holders, all_rows, tokens = parts[0].shape
    kind = parts[0].dtype
    shape = jax.ShapeDtypeStruct((holders, all_rows, width // CORES), kind)
    inputs = len(pieces) + len(parts)
    return pl.pallas_call(
        partial_kernel,
        in_specs=[pl.BlockSpec(memory_space=pltpu.SMEM)]
        + [pl.BlockSpec(memory_space=pl.ANY)] * inputs,
        out_specs=[pl.BlockSpec(memory_space=pltpu.VMEM)] * 2,
        scratch_shapes=[
            pltpu.VMEM((layers, chips, tokens, width), kind),
            pltpu.VMEM((SIDE, holders, all_rows, tokens), kind),
            pltpu.SemaphoreType.DMA((layers, inputs)),
        ],
        out_shape=[shape, shape],
        compiler_params=pltpu.CompilerParams(vmem_limit_bytes=50 * MIB),
        cost_estimate=pl.CostEstimate(flops=0, bytes_accessed=1024, transcendentals=0),
        name="gradient_partials",
    )(here, *pieces, *parts)


def deal_kernel(slot_ref, kept_ref, got_ref, out_ref):
    layer, half = pl.program_id(0), pl.program_id(1)
    holders, rows, _ = kept_ref.shape
    piece = out_ref.shape[1]
    cols = rows // piece
    for holder in range(holders):
        total = kept_ref[holder].astype(jnp.float32) + got_ref[holder].astype(jnp.float32)
        total = total.astype(out_ref.dtype)
        for col in range(cols):
            slot = slot_ref[((half * holders + holder) * 2 + layer) * cols + col]
            out_ref[slot] = total[col * piece : (col + 1) * piece]


def deal_to_slots(slots, kept, got, slot_total):
    holders, all_rows, size = kept.shape
    layers = 2
    rows = all_rows // layers
    shape = (holders * slot_total, TABLE_ROWS, size)
    return pl.pallas_call(
        deal_kernel,
        grid_spec=pltpu.PrefetchScalarGridSpec(
            num_scalar_prefetch=1,
            grid=(layers, 2),
            in_specs=[pl.BlockSpec((holders // 2, rows, size), lambda l, h, s: (h, l, 0))] * 2,
            out_specs=pl.BlockSpec(shape, lambda l, h, s: (0, 0, 0)),
        ),
        out_shape=jax.ShapeDtypeStruct(shape, kept.dtype),
        compiler_params=pltpu.CompilerParams(vmem_limit_bytes=6 * MIB),
        cost_estimate=pl.CostEstimate(flops=0, bytes_accessed=1024, transcendentals=0),
        name="deal_to_slots",
    )(slots, kept, got)


def slot_kernel(source_ref, left_ref, right_ref, first_ref, second_ref, *refs):
    out_ref, left_stat_ref, right_stat_ref, lefts, rights, turns, sems = refs
    slot = pl.program_id(0)
    slot_total, size, _ = lefts.shape

    def fetches(s):
        moves = [(left_ref.at[s], lefts.at[s]), (right_ref.at[s], rights.at[s])]
        moves += [(ref.at[:, s], turns.at[s, q]) for q, ref in enumerate((first_ref, second_ref))]
        return [pltpu.make_async_copy(*move, sems.at[s, n]) for n, move in enumerate(moves)]

    @pl.when(slot == 0)
    def _():
        for s in range(slot_total):
            for fetch in fetches(s):
                fetch.start()

    for fetch in fetches(slot):
        fetch.wait()
    is_live = source_ref[slot] >= 0

    @pl.when(is_live)
    def _():
        turned = turns[slot].reshape(size, size)
        inner = dot(lefts[slot], turned, NT).astype(out_ref.dtype)
        out_ref[0] = dot(inner, rights[slot], NN).astype(out_ref.dtype)
        scale = 1.0 / size
        left_stat_ref[0] = (dot(turned, turned, TN) * scale).astype(left_stat_ref.dtype)
        right_stat_ref[0] = (dot(turned, turned, NT) * scale).astype(right_stat_ref.dtype)

    @pl.when(jnp.logical_not(is_live))
    def _():
        left_stat_ref[...] = jnp.zeros_like(left_stat_ref)
        right_stat_ref[...] = jnp.zeros_like(right_stat_ref)


def work_on_slots(sources, left_roots, right_roots, arrived, owner_total):
    slot_total, size, _ = left_roots.shape
    kind = left_roots.dtype
    slices = arrived[0].shape

    def out_place(s, source):
        place = source[s]
        for back in range(1, slot_total):
            place = jnp.where(place >= 0, place, source[jnp.maximum(s - back, 0)])
        return (place, 0, 0)

    def live(s, source):
        return (s, 0, 0)

    stats = jax.ShapeDtypeStruct((slot_total, size, size), kind)
    return pl.pallas_call(
        slot_kernel,
        grid_spec=pltpu.PrefetchScalarGridSpec(
            num_scalar_prefetch=1,
            grid=(slot_total,),
            in_specs=[pl.BlockSpec(memory_space=pl.ANY)] * 4,
            out_specs=[
                pl.BlockSpec((1, size, size), out_place),
                pl.BlockSpec((1, size, size), live),
                pl.BlockSpec((1, size, size), live),
            ],
            scratch_shapes=[
                pltpu.VMEM((slot_total, size, size), kind),
                pltpu.VMEM((slot_total, size, size), kind),
                pltpu.VMEM((slot_total, CHUNKS, slices[0], slices[2], size), kind),
                pltpu.SemaphoreType.DMA((slot_total, 4)),
            ],
        ),
        out_shape=[jax.ShapeDtypeStruct((owner_total, size, size), kind), stats, stats],
        compiler_params=pltpu.CompilerParams(vmem_limit_bytes=50 * MIB),
        cost_estimate=pl.CostEstimate(
            flops=8 * slot_total * size**3,
            bytes_accessed=12 * slot_total * size * size,
            transcendentals=0,
        ),
        name="work_on_slots",
    )(sources, left_roots, right_roots, *arrived)


def place_kernel(owner_ref, returned_ref, out_ref, held, in_sems, out_sems):
    layers, size, width = out_ref.shape
    cols = width // size
    blocks = [(l, c, l * cols + c) for l in range(layers) for c in range(cols)]
    fetches = [
        pltpu.make_async_copy(returned_ref.at[owner_ref[t]], held.at[t], in_sems.at[t])
        for _, _, t in blocks
    ]
    stores = [
        pltpu.make_async_copy(
            held.at[t], out_ref.at[l, :, pl.ds(c * size, size)], out_sems.at[t]
        )
        for l, c, t in blocks
    ]
    for fetch in fetches:
        fetch.start()
    for fetch, store in zip(fetches, stores):
        fetch.wait()
        store.start()
    for store in stores:
        store.wait()


def place_blocks(owners, returned, layers, cols):
    _, size, _ = returned.shape
    return pl.pallas_call(
        place_kernel,
        in_specs=[
            pl.BlockSpec(memory_space=pltpu.SMEM),
            pl.BlockSpec(memory_space=pl.ANY),
        ],
        out_specs=pl.BlockSpec(memory_space=pl.ANY),
        out_shape=jax.ShapeDtypeStruct((layers, size, cols * size), returned.dtype),
        scratch_shapes=[
            pltpu.VMEM((layers * cols, size, size), returned.dtype),
            pltpu.SemaphoreType.DMA((layers * cols,)),
            pltpu.SemaphoreType.DMA((layers * cols,)),
        ],
        compiler_params=pltpu.CompilerParams(vmem_limit_bytes=8 * MIB),
        cost_estimate=pl.CostEstimate(
            flops=0, bytes_accessed=4 * layers * cols * size * size, transcendentals=0
        ),
        name="place_blocks",
    )(owners, returned)


def activations_for_chips(activations, chip_y, parity):
    layers, tokens, width = activations.shape
    rows, pair_width = tokens // 4, width // SIDE
    return [
        jnp.stack(
            [
                lax.dynamic_slice(
                    activations,
                    (0, (parity * 2 + u) * rows, lax.rem(chip_y + hops, SIDE) * pair_width),
                    (layers, rows, pair_width),
                )
                for u in range(2)
            ]
        )
        for hops in (0, 1, SIDE - 1, 2)
    ]


def on_device(
    activations, cotangents, left_root, right_root, block_owner, owned_sources, owner_counts
):
    owner_total = lax.axis_size("mp")
    layers, _, width = cotangents.shape
    slot_total, size = left_root.shape[2], left_root.shape[-1]
    cols = width // size
    blocks = layers * cols
    owners = block_owner.reshape(-1)
    group, holder = lax.axis_index("dp"), lax.axis_index("mp")
    chip_y, core = group // CORES, lax.rem(group, CORES)
    parity = lax.rem(holder, 2)

    split = split_cotangents(owners, cotangents, owner_total)
    spread = exchange(split)
    for_chips = activations_for_chips(after(activations, split), chip_y, parity)
    from_chips = [for_chips[0]] + [
        along_y(piece, hops) for piece, hops in zip(for_chips[1:], (1, -1, 2))
    ]
    base = spread.shape[1] - TABLE_ROWS
    chunk = base // CHUNKS

    halves = [jnp.stack([piece[u] for piece in from_chips]) for u in range(2)]
    first_parts = ring_in_two(spread[:, :chunk], along_y)
    pieces = (halves[0], halves[1], along_z(halves[0], 1), along_z(halves[1], -1))
    second = after(spread[:, chunk:base], *first_parts)
    second_parts = (second, along_y(second, 1), along_y(second, -1), along_y(second, 2))

    owner_of = spread[:, base : base + blocks, 0].astype(jnp.int32)
    all_owners = jnp.arange(owner_total, dtype=jnp.int32)
    named = (owner_of[:, :, None] == all_owners).astype(jnp.int32)
    given = jnp.sum(named, axis=1)
    earlier = (all_owners[:, None] > all_owners[None, :]).astype(jnp.int32)
    slot_of = jnp.sum(earlier[:, :, None] * given[None, :, :], axis=1)
    slots = (owner_of * slot_total + jnp.sum(named * slot_of[:, None, :], axis=-1)).reshape(-1)

    def sliced_slots(here, parts):
        kept, given = gradient_partials(here, pieces, parts)
        return deal_to_slots(slots, kept, other_core(given), slot_total)

    slot_range = jnp.arange(slot_total, dtype=jnp.int32)
    sources = jnp.where(slot_range < owner_counts.reshape(()), owned_sources.reshape(-1), -1)
    here = jnp.stack((core, parity)).astype(jnp.int32)
    here, slots, sources = lax.optimization_barrier((here, slots, sources))
    dealt = sliced_slots(here, first_parts)
    arrived = exchange(dealt)
    dealt = sliced_slots(after(here, dealt), second_parts)
    dealt, arrived = lax.optimization_barrier((dealt, arrived))
    more = exchange(dealt)

    def by_slot(value):
        return value.reshape((owner_total, slot_total) + value.shape[1:])

    returning, left_stats, right_stats = work_on_slots(
        sources,
        left_root.reshape(slot_total, size, size),
        right_root.reshape(slot_total, size, size),
        (by_slot(arrived), by_slot(more)),
        owner_total,
    )
    precond = place_blocks(owners, exchange(returning), layers, cols)
    stat_shape = (1, 1, slot_total, size, size)
    return (precond, left_stats.reshape(stat_shape), right_stats.reshape(stat_shape))


def solution(mesh):
    placed = (
        P(None, "dp", None),
        P(None, "dp", "mp"),
        P("dp", "mp", None, None, None),
        P("dp", "mp", None, None, None),
        P("dp", "mp", None),
        P("dp", "mp", None),
        P("dp", "mp"),
    )
    return jax.shard_map(
        on_device,
        mesh=mesh,
        in_specs=placed,
        out_specs=(
            P(None, "dp", "mp"),
            P("dp", "mp", None, None, None),
            P("dp", "mp", None, None, None),
        ),
        check_vma=False,
    )
```

time: 313 us -> 287 us (0.917)
  waiting for transfers between devices: 115 us -> 59.3 us
  blocking collectives: 98.6 us -> 134 us
  starting transfers between devices: 47.7 us -> 31 us
  other arithmetic: 1.88 us -> 9.08 us
  local copies, waits for them, and re-layouts: 11.8 us -> 15.4 us
    all_to_all x3 -> x2, waiting for transfers between devices: 67.8 us -> 0.01 us  [exchange(): return lax.all_to_all(value, 'mp', split_axis=0, concat_axis=0, tiled=True)]
    ppermute x9 -> x10, waiting for transfers between devices: 18.3 us -> 54.5 us  [along_y(): return lax.ppermute(value, 'dp', pairs)]
    all_to_all x1 -> x2, blocking collectives: 98.6 us -> 134 us  [exchange(): return lax.all_to_all(value, 'mp', split_axis=0, concat_axis=0, tiled=True)]
    ppermute x3 -> x0, waiting for transfers between devices: 11.2 us -> none  [along_x(): return lax.ppermute(value, 'mp', pairs)]
    ppermute x3 -> x2, waiting for transfers between devices: 10.5 us -> 0.01 us  [along_z(): return lax.ppermute(value, 'mp', pairs)]
    all_to_all x3 -> x2, starting transfers between devices: 21.8 us -> 14.5 us  [exchange(): return lax.all_to_all(value, 'mp', split_axis=0, concat_axis=0, tiled=True)]
    ppermute x9 -> x10, starting transfers between devices: 18.3 us -> 13 us  [along_y(): return lax.ppermute(value, 'dp', pairs)]
    ppermute x3 -> x0, starting transfers between devices: 4.02 us -> none  [along_x(): return lax.ppermute(value, 'mp', pairs)]
  transfers between devices with their start and end apart: 20 -> 16, of which waited for: 16 -> 10; matrix products, arithmetic and copies ran while one was open for 1% -> 6% of each run, Pallas kernels for 0% -> 4%
where the time goes in v2:
time: 287 us
  blocking collectives  134 us (47%)
  waiting for transfers between devices  59.3 us (21%)
  Pallas kernels  35.8 us (12%)
  starting transfers between devices  31 us (11%)
  local copies, waits for them, and re-layouts  15.4 us (5%)
  other arithmetic  9.08 us (3%)
    all_to_all x2, blocking collectives, exchange(): return lax.all_to_all(value, 'mp', split_axis=0, concat_axis=0, tiled=True)  134 us
    ppermute x10, waiting for transfers between devices, along_y(): return lax.ppermute(value, 'dp', pairs)  54.5 us
    pallas_call x2, Pallas kernels, gradient_partials(): pl.pallas_call(partial_kernel, in_specs=[pl.BlockSpec(memory_space=pltpu....  14.6 us
    all_to_all x2, starting transfers between devices, exchange(): return lax.all_to_all(value, 'mp', split_axis=0, concat_axis=0, tiled=True)  14.5 us
    ppermute x10, starting transfers between devices, along_y(): return lax.ppermute(value, 'dp', pairs)  13 us
    pallas_call x1, Pallas kernels, work_on_slots(): pl.pallas_call(slot_kernel, grid_spec=pltpu.PrefetchScalarGridSpec(num_sc...  12.8 us
    unnamed x14, local copies, waits for them, and re-layouts  5.87 us
  transfers between devices with their start and end apart: 16, of which 10 were waited for; matrix products, arithmetic and copies ran while one was open for 6% of the time, Pallas kernels for 4%

profile of v2, /device:TPU:0, one launch (start us, length us, event | category | flops | bytes accessed | tf_op | source)
XLA Modules:
  0.0 286.7 jit_solution(5834992354285185961)
XLA Ops:
  0.6 1.4 copy-done
  2.7 2.2 split_cotangents.1
  4.9 8.0 %all-to-all-start = ((bf16[16,208,256]{2,1,0:T(8,128)(2,1)}), bf16[16,208,256]{2,1,0:T(8,128)(2,1)S(1)}, u32[]{:S(2)}, u32[]{:S(2)}) async-start(bf16[16,208,256]{2,1,0:T(8,128)(2,1)} %split_cotangents.1), calls=%async_computation | async-start | bytes 3407872 | tf_op jit(solution)/shard_map/all_to_all | solution.py:49
  12.9 1.8 dynamic-slice_bitcast_fusion
  14.8 1.6 collective-permute-start
  16.5 1.7 collective-permute-start.1
  18.2 2.1 collective-permute-start.2
  20.3 9.5 %collective-permute-done = bf16[2,2,64,1024]{3,2,1,0:T(8,128)(2,1)S(1)} collective-permute-done((bf16[2,2,64,1024]{3,2,1,0:T(8,128)(2,1)S(1)}, bf16[2,2,64,1024]{3,2,1,0:T(8,128)(2,1)S(1)}, u32[]{:S(2)}, u32[]{:S(2)}) %collective-permute-start) | collective-permute-done | bytes 524320 | tf_op jit(solution)/shard_map/ppermute | solution.py:29
  29.8 0.7 fusion.2
  30.5 0.9 collective-permute-done.1
  31.4 0.7 fusion.3
  32.1 9.8 %collective-permute-done.2 = bf16[2,2,64,1024]{3,2,1,0:T(8,128)(2,1)S(1)} collective-permute-done((bf16[2,2,64,1024]{3,2,1,0:T(8,128)(2,1)S(1)}, bf16[2,2,64,1024]{3,2,1,0:T(8,128)(2,1)S(1)}, u32[]{:S(2)}, u32[]{:S(2)}) %collective-permute-start.2) | collective-permute-done | bytes 524320 | tf_op jit(solution)/shard_map/ppermute | solution.py:29
  41.9 0.7 fusion.4
  42.6 1.1 pad_maximum_fusion.refs_0_
  43.8 1.5 collective-permute-start.3
  45.5 1.0 copy-done.5
  46.5 2.7 collective-permute-start.6
  49.2 2.2 pad_maximum_fusion.1.refs_1_
  51.4 1.7 collective-permute-start.4
  54.4 1.4 slice_convert_fusion
  55.8 8.2 %collective-permute-done.6.refs_6_ = bf16[16,96,256]{2,1,0:T(8,128)(2,1)S(1)} collective-permute-done((bf16[16,96,256]{2,1,0:T(8,128)(2,1)S(1)}, bf16[16,96,256]{2,1,0:T(8,128)(2,1)S(1)}, u32[]{:S(2)}, u32[]{:S(2)}) %collective-permute-start.6) | collective-permute-done | bytes 786464 | tf_op jit(solution)/shard_map/ppermute | solution.py:29
  64.0 0.8 slice.53
  64.8 2.6 collective-permute-start.8
  67.4 0.8 slice.52
  68.2 1.7 multiply_reduce_fusion.1
  69.9 1.4 mul.34
  71.3 1.0 copy.14
  72.3 0.8 multiply_reduce_fusion
  74.1 0.8 reduce_sum.32
  75.6 1.9 collective-permute-done.7.refs_7_
  77.5 7.3 %gradient_partials.2 = (bf16[16,96,512]{2,1,0:T(8,128)(2,1)}, bf16[16,96,512]{2,1,0:T(8,128)(2,1)}) custom-call(s32[2]{0:T(128)S(1)} %pad_add_fusion.here_ref, bf16[4,2,64,1024]{3,2,1,0:T(8,128)(2,1)} %pad_maximum_fusion.refs_0_, bf16[4,2,64,1024]{3,2,1,0:T(8,128)(2,1)} %pad_maximum_fusion.1.refs_1_, ...), custom_call_target="tpu_custom_call" | custom-call | bytes 1024 | tf_op jit(solution)/shard_map/gradient_partials/pallas_call | solution.py:141
  85.0 1.5 collective-permute-start.11
  86.5 0.7 collective-permute-start.10
  87.2 1.4 collective-permute-done.9.got_ref
  88.5 1.4 copy-done.1
  89.9 2.6 deal_to_slots.2
  92.5 6.5 %all-to-all-start.1 = ((bf16[128,16,512]{2,1,0:T(8,128)(2,1)}), bf16[128,16,512]{2,1,0:T(8,128)(2,1)}, u32[]{:S(2)}, u32[]{:S(2)}) async-start(bf16[128,16,512]{2,1,0:T(8,128)(2,1)} %deal_to_slots.2), calls=%async_computation.1 | async-start | bytes 4194304 | tf_op jit(solution)/shard_map/all_to_all | solution.py:49
  99.0 7.9 %collective-permute-done.12.refs_7_ = bf16[16,96,256]{2,1,0:T(8,128)(2,1)S(1)} collective-permute-done((bf16[16,96,256]{2,1,0:T(8,128)(2,1)S(1)}, bf16[16,96,256]{2,1,0:T(8,128)(2,1)S(1)}, u32[]{:S(2)}, u32[]{:S(2)}) %collective-permute-start.12) | collective-permute-done | bytes 786464 | tf_op jit(solution)/shard_map/ppermute | solution.py:29
  106.9 15.0 %collective-permute-done.11.refs_6_ = bf16[16,96,256]{2,1,0:T(8,128)(2,1)S(1)} collective-permute-done((bf16[16,96,256]{2,1,0:T(8,128)(2,1)S(1)}, bf16[16,96,256]{2,1,0:T(8,128)(2,1)S(1)}, u32[]{:S(2)}, u32[]{:S(2)}) %collective-permute-start.11) | collective-permute-done | bytes 786464 | tf_op jit(solution)/shard_map/ppermute | solution.py:29
  121.9 1.3 collective-permute-done.10.refs_5_
  123.2 7.2 %gradient_partials.3 = (bf16[16,96,512]{2,1,0:T(8,128)(2,1)}, bf16[16,96,512]{2,1,0:T(8,128)(2,1)}) custom-call(s32[2]{0:T(128)S(1)} %pad_add_fusion.here_ref, bf16[4,2,64,1024]{3,2,1,0:T(8,128)(2,1)} %pad_maximum_fusion.refs_0_, bf16[4,2,64,1024]{3,2,1,0:T(8,128)(2,1)} %pad_maximum_fusion.1.refs_1_, ...), custom_call_target="tpu_custom_call" | custom-call | bytes 1024 | tf_op jit(solution)/shard_map/gradient_partials/pallas_call | solution.py:141
  130.7 3.5 %collective-permute-done.13.got_ref = bf16[16,96,512]{2,1,0:T(8,128)(2,1)S(1)} collective-permute-done((bf16[16,96,512]{2,1,0:T(8,128)(2,1)}, bf16[16,96,512]{2,1,0:T(8,128)(2,1)S(1)}, u32[]{:S(2)}, u32[]{:S(2)}) %collective-permute-start.13) | collective-permute-done | bytes 1572896 | tf_op jit(solution)/shard_map/ppermute | solution.py:34
  134.2 1.4 copy-done.2
  135.6 1.2 deal_to_slots.3
  136.9 35.0 %all_to_all.20 = bf16[128,16,512]{2,1,0:T(8,128)(2,1)} all-to-all(bf16[128,16,512]{2,1,0:T(8,128)(2,1)S(1)} %deal_to_slots.3), channel_id=1, replica_groups=mesh['dp'=8,'mp'=16] {'mp'}, dimensions={0} | all-to-all | bytes 4194304 | tf_op jit(solution)/shard_map/all_to_all | solution.py:49
  171.9 12.8 %work_on_slots.1 = (bf16[16,512,512]{2,1,0:T(8,128)(2,1)}, bf16[8,512,512]{2,1,0:T(8,128)(2,1)}, bf16[8,512,512]{2,1,0:T(8,128)(2,1)}) custom-call(s32[8]{0:T(128)S(1)} %compare_select_fusion.source_ref, bf16[8,512,512]{2,1,0:T(8,128)(2,1)} %bitcast.35, bf16[8,512,512]{2,1,0:T(8,128)(2,1)} %bitcast.36, bf16[16,8,16,512]{3,2,1,0:T(8,128)(2,1)} %bitcast.16.first_ref, ...), custom_call_target="tpu_custom_call" | custom-call | flops 8589934592 | bytes 25165824 | tf_op jit(solution)/shard_map/work_on_slots/pallas_call | solution.py:241
  184.7 99.3 %all_to_all.21.returned_ref = bf16[16,512,512]{2,1,0:T(8,128)(2,1)S(1)} all-to-all(bf16[16,512,512]{2,1,0:T(8,128)(2,1)} %get-tuple-element.30), channel_id=1, replica_groups=mesh['dp'=8,'mp'=16] {'mp'}, dimensions={0} | all-to-all | bytes 16777216 | tf_op jit(solution)/shard_map/all_to_all | solution.py:49
  284.0 2.5 place_blocks.1
  (32 shorter events, 3.8 us)
Async XLA Ops:
  0.6 1.4 copy-start
  2.0 0.7 copy-start.3
  4.9 40.4 %all-to-all-start = ((bf16[16,208,256]{2,1,0:T(8,128)(2,1)}), bf16[16,208,256]{2,1,0:T(8,128)(2,1)S(1)}, u32[]{:S(2)}, u32[]{:S(2)}) async-start(bf16[16,208,256]{2,1,0:T(8,128)(2,1)} %split_cotangents.1), calls=%async_computation | async-start | bytes 3407872 | tf_op jit(solution)/shard_map/all_to_all | solution.py:49
  14.8 15.0 %collective-permute-start = (bf16[2,2,64,1024]{3,2,1,0:T(8,128)(2,1)S(1)}, bf16[2,2,64,1024]{3,2,1,0:T(8,128)(2,1)S(1)}, u32[]{:S(2)}, u32[]{:S(2)}) collective-permute-start(bf16[2,2,64,1024]{3,2,1,0:T(8,128)(2,1)S(1)} %pad_maximum_fusion.2), channel_id=1, source_target_pairs={{0,32},{16,48},{32,64},{48,80},{64,96},{80,112},{96,0},{112,16},{1... | collective-permute-start | bytes 1572872 | tf_op jit(solution)/shard_map/ppermute | solution.py:29
  16.5 14.9 %collective-permute-start.1 = (bf16[2,2,64,1024]{3,2,1,0:T(8,128)(2,1)S(1)}, bf16[2,2,64,1024]{3,2,1,0:T(8,128)(2,1)S(1)}, u32[]{:S(2)}, u32[]{:S(2)}) collective-permute-start(bf16[2,2,64,1024]{3,2,1,0:T(8,128)(2,1)S(1)} %pad_maximum_fusion.3), channel_id=1, source_target_pairs={{0,96},{16,112},{32,0},{48,16},{64,32},{80,48},{96,64},{112,80},{1... | collective-permute-start | bytes 1572872 | tf_op jit(solution)/shard_map/ppermute | solution.py:29
  18.2 23.7 %collective-permute-start.2 = (bf16[2,2,64,1024]{3,2,1,0:T(8,128)(2,1)S(1)}, bf16[2,2,64,1024]{3,2,1,0:T(8,128)(2,1)S(1)}, u32[]{:S(2)}, u32[]{:S(2)}) collective-permute-start(bf16[2,2,64,1024]{3,2,1,0:T(8,128)(2,1)S(1)} %pad_maximum_fusion.4), channel_id=1, source_target_pairs={{0,64},{16,80},{32,96},{48,112},{64,0},{80,16},{96,32},{112,48},{1... | collective-permute-start | bytes 1572872 | tf_op jit(solution)/shard_map/ppermute | solution.py:29
  43.8 10.7 %copy-start.6 = (s32[1,1,8]{2,1,0:T(1,128)S(1)}, s32[1,1,8]{2,1,0:T(1,128)}, u32[]{:S(2)}) copy-start(s32[1,1,8]{2,1,0:T(1,128)} %param.12) | copy-start | bytes 100
  43.8 31.8 %collective-permute-start.3 = (bf16[4,2,64,1024]{3,2,1,0:T(8,128)(2,1)}, bf16[4,2,64,1024]{3,2,1,0:T(8,128)(2,1)}, u32[]{:S(2)}, u32[]{:S(2)}) collective-permute-start(bf16[4,2,64,1024]{3,2,1,0:T(8,128)(2,1)} %pad_maximum_fusion.refs_0_), channel_id=1, source_target_pairs={{0,1},{1,2},{2,3},{3,0},{4,5},{5,6},{6,7},{7,4},{8,9},{9,10},{10,1... | collective-permute-start | bytes 3145736 | tf_op jit(solution)/shard_map/ppermute | solution.py:39
  45.3 1.2 copy-start.5
  46.5 17.5 %collective-permute-start.6 = (bf16[16,96,256]{2,1,0:T(8,128)(2,1)S(1)}, bf16[16,96,256]{2,1,0:T(8,128)(2,1)S(1)}, u32[]{:S(2)}, u32[]{:S(2)}) collective-permute-start(bf16[16,96,256]{2,1,0:T(8,128)(2,1)S(1)} %get-tuple-element.42.refs_4_), channel_id=1, source_target_pairs={{0,96},{16,112},{32,0},{48,16},{64,32},{80,48},{96,64},{112,80},{1... | collective-permute-start | bytes 2359304 | tf_op jit(solution)/shard_map/ppermute | solution.py:29
  49.2 18.2 %collective-permute-start.5 = (bf16[16,96,256]{2,1,0:T(8,128)(2,1)S(1)}, bf16[16,96,256]{2,1,0:T(8,128)(2,1)S(1)}, u32[]{:S(2)}, u32[]{:S(2)}) collective-permute-start(bf16[16,96,256]{2,1,0:T(8,128)(2,1)S(1)} %get-tuple-element.42.refs_4_), channel_id=1, source_target_pairs={{0,32},{16,48},{32,64},{48,80},{64,96},{80,112},{96,0},{112,16},{1... | collective-permute-start | bytes 2359304 | tf_op jit(solution)/shard_map/ppermute | solution.py:29
  51.4 24.2 %collective-permute-start.4 = (bf16[4,2,64,1024]{3,2,1,0:T(8,128)(2,1)}, bf16[4,2,64,1024]{3,2,1,0:T(8,128)(2,1)}, u32[]{:S(2)}, u32[]{:S(2)}) collective-permute-start(bf16[4,2,64,1024]{3,2,1,0:T(8,128)(2,1)} %pad_maximum_fusion.1.refs_1_), channel_id=1, source_target_pairs={{0,3},{1,0},{2,1},{3,2},{4,7},{5,4},{6,5},{7,6},{8,11},{9,8},{10,9... | collective-permute-start | bytes 3145736 | tf_op jit(solution)/shard_map/ppermute | solution.py:39
  64.8 10.8 %collective-permute-start.8 = (bf16[8,96,256]{2,1,0:T(8,128)(2,1)}, bf16[8,96,256]{2,1,0:T(8,128)(2,1)S(1)}, u32[]{:S(2)}, u32[]{:S(2)}) collective-permute-start(bf16[8,96,256]{2,1,0:T(8,128)(2,1)} %slice.53), channel_id=1, source_target_pairs={{0,96},{16,112},{32,0},{48,16},{64,32},{80,48},{96,64},{112,80},{1... | collective-permute-start | bytes 1179656 | tf_op jit(solution)/shard_map/ppermute | solution.py:29
  68.2 9.3 %collective-permute-start.7 = (bf16[8,96,256]{2,1,0:T(8,128)(2,1)}, bf16[8,96,256]{2,1,0:T(8,128)(2,1)}, u32[]{:S(2)}, u32[]{:S(2)}) collective-permute-start(bf16[8,96,256]{2,1,0:T(8,128)(2,1)} %slice.52), channel_id=1, source_target_pairs={{0,32},{16,48},{32,64},{48,80},{64,96},{80,112},{96,0},{112,16},{1... | collective-permute-start | bytes 1179656 | tf_op jit(solution)/shard_map/ppermute | solution.py:29
  84.8 3.7 %collective-permute-start.9 = (bf16[16,96,512]{2,1,0:T(8,128)(2,1)}, bf16[16,96,512]{2,1,0:T(8,128)(2,1)S(1)}, u32[]{:S(2)}, u32[]{:S(2)}) collective-permute-start(bf16[16,96,512]{2,1,0:T(8,128)(2,1)} %get-tuple-element.23), channel_id=1, source_target_pairs={{0,16},{16,0},{32,48},{48,32},{64,80},{80,64},{96,112},{112,96},{1... | collective-permute-start | bytes 4718600 | tf_op jit(solution)/shard_map/ppermute | solution.py:34
  84.9 22.0 %collective-permute-start.12 = (bf16[16,96,256]{2,1,0:T(8,128)(2,1)S(1)}, bf16[16,96,256]{2,1,0:T(8,128)(2,1)S(1)}, u32[]{:S(2)}, u32[]{:S(2)}) collective-permute-start(bf16[16,96,256]{2,1,0:T(8,128)(2,1)S(1)} %get-tuple-element.25.refs_4_), channel_id=1, source_target_pairs={{0,64},{16,80},{32,96},{48,112},{64,0},{80,16},{96,32},{112,48},{1... | collective-permute-start | bytes 2359304 | tf_op jit(solution)/shard_map/ppermute | solution.py:29
  85.0 36.9 %collective-permute-start.11 = (bf16[16,96,256]{2,1,0:T(8,128)(2,1)S(1)}, bf16[16,96,256]{2,1,0:T(8,128)(2,1)S(1)}, u32[]{:S(2)}, u32[]{:S(2)}) collective-permute-start(bf16[16,96,256]{2,1,0:T(8,128)(2,1)S(1)} %get-tuple-element.25.refs_4_), channel_id=1, source_target_pairs={{0,96},{16,112},{32,0},{48,16},{64,32},{80,48},{96,64},{112,80},{1... | collective-permute-start | bytes 2359304 | tf_op jit(solution)/shard_map/ppermute | solution.py:29
  86.5 36.8 %collective-permute-start.10 = (bf16[16,96,256]{2,1,0:T(8,128)(2,1)S(1)}, bf16[16,96,256]{2,1,0:T(8,128)(2,1)S(1)}, u32[]{:S(2)}, u32[]{:S(2)}) collective-permute-start(bf16[16,96,256]{2,1,0:T(8,128)(2,1)S(1)} %get-tuple-element.25.refs_4_), channel_id=1, source_target_pairs={{0,32},{16,48},{32,64},{48,80},{64,96},{80,112},{96,0},{112,16},{1... | collective-permute-start | bytes 2359304 | tf_op jit(solution)/shard_map/ppermute | solution.py:29
  88.5 1.4 copy-start.1
  92.5 44.4 %all-to-all-start.1 = ((bf16[128,16,512]{2,1,0:T(8,128)(2,1)}), bf16[128,16,512]{2,1,0:T(8,128)(2,1)}, u32[]{:S(2)}, u32[]{:S(2)}) async-start(bf16[128,16,512]{2,1,0:T(8,128)(2,1)} %deal_to_slots.2), calls=%async_computation.1 | async-start | bytes 4194304 | tf_op jit(solution)/shard_map/all_to_all | solution.py:49
  130.5 3.7 %collective-permute-start.13 = (bf16[16,96,512]{2,1,0:T(8,128)(2,1)}, bf16[16,96,512]{2,1,0:T(8,128)(2,1)S(1)}, u32[]{:S(2)}, u32[]{:S(2)}) collective-permute-start(bf16[16,96,512]{2,1,0:T(8,128)(2,1)} %get-tuple-element.27), channel_id=1, source_target_pairs={{0,16},{16,0},{32,48},{48,32},{64,80},{80,64},{96,112},{112,96},{1... | collective-permute-start | bytes 4718600 | tf_op jit(solution)/shard_map/ppermute | solution.py:34
  134.2 1.4 copy-start.2
  184.7 99.3 %copy-start.4 = (s32[1,1,6]{2,1,0:T(1,128)S(1)}, s32[1,1,6]{2,1,0:T(1,128)}, u32[]{:S(2)}) copy-start(s32[1,1,6]{2,1,0:T(1,128)} %param.11) | copy-start | bytes 76

commit v3 on v2

--- a/solution.py
+++ b/solution.py
@@ -53,38 +53,41 @@
     return lax.optimization_barrier((value,) + needed)[0]
 
 
-def split_kernel(owner_ref, cot_ref, out_ref):
+def split_kernel(owner_ref, cot_ref, *out_refs):
     layers, tokens, width = cot_ref.shape
-    parts, piece = out_ref.shape[0], TABLE_ROWS
+    parts, piece = out_refs[0].shape[0], TABLE_ROWS
     size = parts * piece * CHUNKS
     cols = width // size
     for layer in range(layers):
         for col in range(cols):
             turned = cot_ref[layer, :, col * size : (col + 1) * size].T
-            for q in range(CHUNKS):
-                row = ((q * layers + layer) * cols + col) * piece
+            row = (layer * cols + col) * piece
+            for q, out_ref in enumerate(out_refs):
                 half = turned[q * parts * piece : (q + 1) * parts * piece]
                 out_ref[:, row : row + piece, :] = half.reshape(parts, piece, tokens)
     rows = lax.broadcasted_iota(jnp.int32, (TABLE_ROWS, tokens), 0)
     table = jnp.zeros((TABLE_ROWS, tokens), jnp.float32)
     for t in range(layers * cols):
         table = jnp.where(rows == t, owner_ref[t].astype(jnp.float32), table)
-    base = CHUNKS * layers * cols * piece
+    base, out_ref = layers * cols * piece, out_refs[-1]
     for part in range(parts):
         out_ref[part, base : base + TABLE_ROWS, :] = table.astype(out_ref.dtype)
 
 
 def split_cotangents(owners, cotangents, owner_total):
     layers, tokens, width = cotangents.shape
-    rows = width * layers // owner_total
+    rows = width * layers // owner_total // CHUNKS
     return pl.pallas_call(
         split_kernel,
         in_specs=[
             pl.BlockSpec(memory_space=pltpu.SMEM),
             pl.BlockSpec(memory_space=pltpu.VMEM),
         ],
-        out_specs=pl.BlockSpec(memory_space=pltpu.VMEM),
-        out_shape=jax.ShapeDtypeStruct((owner_total, rows + TABLE_ROWS, tokens), cotangents.dtype),
+        out_specs=[pl.BlockSpec(memory_space=pltpu.VMEM)] * 2,
+        out_shape=[
+            jax.ShapeDtypeStruct((owner_total, rows, tokens), cotangents.dtype),
+            jax.ShapeDtypeStruct((owner_total, rows + TABLE_ROWS, tokens), cotangents.dtype),
+        ],
         compiler_params=pltpu.CompilerParams(vmem_limit_bytes=6 * MIB),
         cost_estimate=pl.CostEstimate(
             flops=0, bytes_accessed=4 * cotangents.size, transcendentals=0
@@ -344,22 +347,22 @@
     chip_y, core = group // CORES, lax.rem(group, CORES)
     parity = lax.rem(holder, 2)
 
-    split = split_cotangents(owners, cotangents, owner_total)
-    spread = exchange(split)
-    for_chips = activations_for_chips(after(activations, split), chip_y, parity)
+    for_chips = activations_for_chips(activations, chip_y, parity)
     from_chips = [for_chips[0]] + [
         along_y(piece, hops) for piece, hops in zip(for_chips[1:], (1, -1, 2))
     ]
-    base = spread.shape[1] - TABLE_ROWS
-    chunk = base // CHUNKS
+    first, second = split_cotangents(owners, after(cotangents, *for_chips), owner_total)
+    first = exchange(first)
+    second = exchange(after(second, first))
+    base = first.shape[1]
 
     halves = [jnp.stack([piece[u] for piece in from_chips]) for u in range(2)]
-    first_parts = ring_in_two(spread[:, :chunk], along_y)
+    first_parts = ring_in_two(first, along_y)
     pieces = (halves[0], halves[1], along_z(halves[0], 1), along_z(halves[1], -1))
-    second = after(spread[:, chunk:base], *first_parts)
+    owner_of = second[:, base : base + blocks, 0].astype(jnp.int32)
+    second = after(second[:, :base], *first_parts)
     second_parts = (second, along_y(second, 1), along_y(second, -1), along_y(second, 2))
 
-    owner_of = spread[:, base : base + blocks, 0].astype(jnp.int32)
     all_owners = jnp.arange(owner_total, dtype=jnp.int32)
     named = (owner_of[:, :, None] == all_owners).astype(jnp.int32)
     given = jnp.sum(named, axis=1)

time: 287 us -> 280 us (0.976)
  waiting for transfers between devices: 59.3 us -> 51 us
  starting transfers between devices: 31 us -> 34.9 us
    ppermute x10, waiting for transfers between devices: 54.5 us -> 33.6 us  [along_y(): return lax.ppermute(value, 'dp', pairs)]
    all_to_all x2 -> x3, waiting for transfers between devices: 0.01 us -> 10.2 us  [exchange(): return lax.all_to_all(value, 'mp', split_axis=0, concat_axis=0, tiled=True)]
    unnamed x14 -> x10, local copies, waits for them, and re-layouts: 5.87 us -> 1.43 us
    ppermute x2, waiting for transfers between devices: 0.01 us -> 3.62 us  [along_z(): return lax.ppermute(value, 'mp', pairs)]
    all_to_all x2 -> x3, starting transfers between devices: 14.5 us -> 16.9 us  [exchange(): return lax.all_to_all(value, 'mp', split_axis=0, concat_axis=0, tiled=True)]
  transfers between devices with their start and end apart: 16 -> 17, of which waited for: 10 -> 7; matrix products, arithmetic and copies ran while one was open for 6% -> 7% of each run, Pallas kernels for 4% -> 5%
where the time goes in v3:
time: 280 us; the launch traced here: 279 us
  blocking collectives  132 us (47%)
  waiting for transfers between devices  51 us (18%)
  Pallas kernels  35.8 us (13%)
  starting transfers between devices  34.9 us (12%)
  local copies, waits for them, and re-layouts  12.8 us (5%)
  other arithmetic  11.2 us (4%)
    all_to_all x2, blocking collectives, exchange(): return lax.all_to_all(value, 'mp', split_axis=0, concat_axis=0, tiled=True)  132 us
    ppermute x10, waiting for transfers between devices, along_y(): return lax.ppermute(value, 'dp', pairs)  33.6 us
    all_to_all x3, starting transfers between devices, exchange(): return lax.all_to_all(value, 'mp', split_axis=0, concat_axis=0, tiled=True)  16.9 us
    pallas_call x2, Pallas kernels, gradient_partials(): pl.pallas_call(partial_kernel, in_specs=[pl.BlockSpec(memory_space=pltpu....  14.5 us
    ppermute x10, starting transfers between devices, along_y(): return lax.ppermute(value, 'dp', pairs)  14.5 us
    pallas_call x1, Pallas kernels, work_on_slots(): pl.pallas_call(slot_kernel, grid_spec=pltpu.PrefetchScalarGridSpec(num_sc...  12.8 us
    all_to_all x3, waiting for transfers between devices, exchange(): return lax.all_to_all(value, 'mp', split_axis=0, concat_axis=0, tiled=True)  10.2 us
  transfers between devices with their start and end apart: 17, of which 7 were waited for; matrix products, arithmetic and copies ran while one was open for 7% of the time, Pallas kernels for 5%

profile of v3, /device:TPU:0, one launch (start us, length us, event | category | flops | bytes accessed | tf_op | source)
XLA Modules:
  0.0 279.2 jit_solution(10354811514354635204)
XLA Ops:
  0.7 1.8 dynamic-slice_bitcast_fusion
  2.5 0.8 pad_maximum_fusion.2
  3.3 1.7 collective-permute-start
  5.0 1.6 collective-permute-start.1
  6.7 0.8 pad_maximum_fusion.4
  7.5 2.2 split_cotangents.1
  9.7 8.0 %all-to-all-start = ((bf16[16,96,256]{2,1,0:T(8,128)(2,1)}), bf16[16,96,256]{2,1,0:T(8,128)(2,1)S(1)}, u32[]{:S(2)}, u32[]{:S(2)}) async-start(bf16[16,96,256]{2,1,0:T(8,128)(2,1)} %get-tuple-element.23), calls=%async_computation | async-start | bytes 1572864 | tf_op jit(solution)/shard_map/all_to_all | solution.py:49
  17.7 2.1 collective-permute-start.2
  19.7 0.7 fusion.1
  20.5 0.7 fusion.2
  21.2 10.2 %all-to-all-done.refs_4_ = bf16[16,96,256]{2,1,0:T(8,128)(2,1)S(1)} async-done(((bf16[16,96,256]{2,1,0:T(8,128)(2,1)}), bf16[16,96,256]{2,1,0:T(8,128)(2,1)S(1)}, u32[]{:S(2)}, u32[]{:S(2)}) %all-to-all-start) | async-done | bytes 786464 | tf_op jit(solution)/shard_map/all_to_all | solution.py:49
  31.5 4.3 %all-to-all-start.1 = ((bf16[16,112,256]{2,1,0:T(8,128)(2,1)}), bf16[16,112,256]{2,1,0:T(8,128)(2,1)}, u32[]{:S(2)}, u32[]{:S(2)}) async-start(bf16[16,112,256]{2,1,0:T(8,128)(2,1)} %get-tuple-element.24), calls=%async_computation.1 | async-start | bytes 1835008 | tf_op jit(solution)/shard_map/all_to_all | solution.py:49
  35.8 1.8 collective-permute-start.6
  37.9 1.1 fusion.3
  39.0 2.2 pad_maximum_fusion.refs_0_
  41.1 1.7 collective-permute-start.3
  42.8 1.1 pad_maximum_fusion.1.refs_1_
  43.9 1.6 collective-permute-start.4
  46.8 6.6 %collective-permute-done.6.refs_6_ = bf16[16,96,256]{2,1,0:T(8,128)(2,1)S(1)} collective-permute-done((bf16[16,96,256]{2,1,0:T(8,128)(2,1)S(1)}, bf16[16,96,256]{2,1,0:T(8,128)(2,1)S(1)}, u32[]{:S(2)}, u32[]{:S(2)}) %collective-permute-start.6) | collective-permute-done | bytes 786464 | tf_op jit(solution)/shard_map/ppermute | solution.py:29
  53.4 3.0 %collective-permute-start.8 = (bf16[8,96,256]{2,1,0:T(8,128)(2,1)S(1)}, bf16[8,96,256]{2,1,0:T(8,128)(2,1)S(1)}, u32[]{:S(2)}, u32[]{:S(2)}) collective-permute-start(bf16[8,96,256]{2,1,0:T(8,128)(2,1)S(1)} %slice.48), channel_id=1, source_target_pairs={{0,96},{16,112},{32,0},{48,16},{64,32},{80,48},{96,64},{112,80},{1... | collective-permute-start | bytes 1179656 | tf_op jit(solution)/shard_map/ppermute | solution.py:29
  56.4 0.8 slice.47
  57.2 1.4 slice_convert_fusion
  58.6 1.7 multiply_reduce_fusion.1
  60.3 1.3 mul.77
  61.6 1.0 copy.14
  62.6 0.8 multiply_reduce_fusion
  63.5 0.8 select_reduce_fusion
  64.3 1.4 copy.15
  65.7 1.3 reduce_sum.32
  67.6 3.6 %collective-permute-done.3.refs_2_ = bf16[4,2,64,1024]{3,2,1,0:T(8,128)(2,1)} collective-permute-done((bf16[4,2,64,1024]{3,2,1,0:T(8,128)(2,1)}, bf16[4,2,64,1024]{3,2,1,0:T(8,128)(2,1)}, u32[]{:S(2)}, u32[]{:S(2)}) %collective-permute-start.3) | collective-permute-done | bytes 1048608 | tf_op jit(solution)/shard_map/ppermute | solution.py:39
  71.2 7.3 %gradient_partials.2 = (bf16[16,96,512]{2,1,0:T(8,128)(2,1)}, bf16[16,96,512]{2,1,0:T(8,128)(2,1)}) custom-call(s32[2]{0:T(128)S(1)} %pad_add_fusion.here_ref, bf16[4,2,64,1024]{3,2,1,0:T(8,128)(2,1)} %pad_maximum_fusion.refs_0_, bf16[4,2,64,1024]{3,2,1,0:T(8,128)(2,1)} %pad_maximum_fusion.1.refs_1_, ...), custom_call_target="tpu_custom_call" | custom-call | bytes 1024 | tf_op jit(solution)/shard_map/gradient_partials/pallas_call | solution.py:144
  78.6 1.3 slice.49.refs_4_
  79.9 2.0 collective-permute-start.12
  82.0 1.1 collective-permute-start.11
  83.0 1.0 collective-permute-start.10
  84.0 2.6 deal_to_slots.2
  86.6 4.6 %all-to-all-start.2 = ((bf16[128,16,512]{2,1,0:T(8,128)(2,1)}), bf16[128,16,512]{2,1,0:T(8,128)(2,1)}, u32[]{:S(2)}, u32[]{:S(2)}) async-start(bf16[128,16,512]{2,1,0:T(8,128)(2,1)} %deal_to_slots.2), calls=%async_computation.2 | async-start | bytes 4194304 | tf_op jit(solution)/shard_map/all_to_all | solution.py:49
  91.2 10.8 %collective-permute-done.12.refs_7_ = bf16[16,96,256]{2,1,0:T(8,128)(2,1)S(1)} collective-permute-done((bf16[16,96,256]{2,1,0:T(8,128)(2,1)S(1)}, bf16[16,96,256]{2,1,0:T(8,128)(2,1)S(1)}, u32[]{:S(2)}, u32[]{:S(2)}) %collective-permute-start.12) | collective-permute-done | bytes 786464 | tf_op jit(solution)/shard_map/ppermute | solution.py:29
  102.0 15.4 %collective-permute-done.11.refs_6_ = bf16[16,96,256]{2,1,0:T(8,128)(2,1)S(1)} collective-permute-done((bf16[16,96,256]{2,1,0:T(8,128)(2,1)S(1)}, bf16[16,96,256]{2,1,0:T(8,128)(2,1)S(1)}, u32[]{:S(2)}, u32[]{:S(2)}) %collective-permute-start.11) | collective-permute-done | bytes 786464 | tf_op jit(solution)/shard_map/ppermute | solution.py:29
  117.3 0.9 collective-permute-done.10.refs_5_
  118.2 7.2 %gradient_partials.3 = (bf16[16,96,512]{2,1,0:T(8,128)(2,1)}, bf16[16,96,512]{2,1,0:T(8,128)(2,1)}) custom-call(s32[2]{0:T(128)S(1)} %pad_add_fusion.here_ref, bf16[4,2,64,1024]{3,2,1,0:T(8,128)(2,1)} %pad_maximum_fusion.refs_0_, bf16[4,2,64,1024]{3,2,1,0:T(8,128)(2,1)} %pad_maximum_fusion.1.refs_1_, ...), custom_call_target="tpu_custom_call" | custom-call | bytes 1024 | tf_op jit(solution)/shard_map/gradient_partials/pallas_call | solution.py:144
  125.7 3.5 %collective-permute-done.13.got_ref = bf16[16,96,512]{2,1,0:T(8,128)(2,1)S(1)} collective-permute-done((bf16[16,96,512]{2,1,0:T(8,128)(2,1)}, bf16[16,96,512]{2,1,0:T(8,128)(2,1)S(1)}, u32[]{:S(2)}, u32[]{:S(2)}) %collective-permute-start.13) | collective-permute-done | bytes 1572896 | tf_op jit(solution)/shard_map/ppermute | solution.py:34
  129.2 1.4 copy-done.2
  130.6 1.2 deal_to_slots.3
  131.8 32.9 %all_to_all.25 = bf16[128,16,512]{2,1,0:T(8,128)(2,1)} all-to-all(bf16[128,16,512]{2,1,0:T(8,128)(2,1)S(1)} %deal_to_slots.3), channel_id=1, replica_groups=mesh['dp'=8,'mp'=16] {'mp'}, dimensions={0} | all-to-all | bytes 4194304 | tf_op jit(solution)/shard_map/all_to_all | solution.py:49
  164.7 12.8 %work_on_slots.1 = (bf16[16,512,512]{2,1,0:T(8,128)(2,1)}, bf16[8,512,512]{2,1,0:T(8,128)(2,1)}, bf16[8,512,512]{2,1,0:T(8,128)(2,1)}) custom-call(s32[8]{0:T(128)S(1)} %compare_select_fusion.source_ref, bf16[8,512,512]{2,1,0:T(8,128)(2,1)} %bitcast.35, bf16[8,512,512]{2,1,0:T(8,128)(2,1)} %bitcast.36, bf16[16,8,16,512]{3,2,1,0:T(8,128)(2,1)} %bitcast.16.first_ref, ...), custom_call_target="tpu_custom_call" | custom-call | flops 8589934592 | bytes 25165824 | tf_op jit(solution)/shard_map/work_on_slots/pallas_call | solution.py:244
  177.5 99.0 %all_to_all.26.returned_ref = bf16[16,512,512]{2,1,0:T(8,128)(2,1)S(1)} all-to-all(bf16[16,512,512]{2,1,0:T(8,128)(2,1)} %get-tuple-element.36), channel_id=1, replica_groups=mesh['dp'=8,'mp'=16] {'mp'}, dimensions={0} | all-to-all | bytes 16777216 | tf_op jit(solution)/shard_map/all_to_all | solution.py:49
  276.5 2.5 place_blocks.1
  (30 shorter events, 2.1 us)
Async XLA Ops:
  2.5 5.1 %copy-start = (bf16[2,256,1536]{2,1,0:T(8,128)(2,1)S(1)}, bf16[2,256,1536]{2,1,0:T(8,128)(2,1)}, u32[]{:S(2)}) copy-start(bf16[2,256,1536]{2,1,0:T(8,128)(2,1)} %cot_ref) | copy-start | bytes 4718596
  2.5 5.1 %copy-start.3 = (s32[1,1,6]{2,1,0:T(1,128)S(1)}, s32[1,1,6]{2,1,0:T(1,128)}, u32[]{:S(2)}) copy-start(s32[1,1,6]{2,1,0:T(1,128)} %param.11) | copy-start | bytes 76
  3.3 16.4 %collective-permute-start = (bf16[2,2,64,1024]{3,2,1,0:T(8,128)(2,1)}, bf16[2,2,64,1024]{3,2,1,0:T(8,128)(2,1)S(1)}, u32[]{:S(2)}, u32[]{:S(2)}) collective-permute-start(bf16[2,2,64,1024]{3,2,1,0:T(8,128)(2,1)} %pad_maximum_fusion.2), channel_id=1, source_target_pairs={{0,32},{16,48},{32,64},{48,80},{64,96},{80,112},{96,0},{112,16},{1... | collective-permute-start | bytes 1572872 | tf_op jit(solution)/shard_map/ppermute | solution.py:29
  5.0 15.4 %collective-permute-start.1 = (bf16[2,2,64,1024]{3,2,1,0:T(8,128)(2,1)S(1)}, bf16[2,2,64,1024]{3,2,1,0:T(8,128)(2,1)S(1)}, u32[]{:S(2)}, u32[]{:S(2)}) collective-permute-start(bf16[2,2,64,1024]{3,2,1,0:T(8,128)(2,1)S(1)} %pad_maximum_fusion.3), channel_id=1, source_target_pairs={{0,96},{16,112},{32,0},{48,16},{64,32},{80,48},{96,64},{112,80},{1... | collective-permute-start | bytes 1572872 | tf_op jit(solution)/shard_map/ppermute | solution.py:29
  9.7 21.8 %all-to-all-start = ((bf16[16,96,256]{2,1,0:T(8,128)(2,1)}), bf16[16,96,256]{2,1,0:T(8,128)(2,1)S(1)}, u32[]{:S(2)}, u32[]{:S(2)}) async-start(bf16[16,96,256]{2,1,0:T(8,128)(2,1)} %get-tuple-element.23), calls=%async_computation | async-start | bytes 1572864 | tf_op jit(solution)/shard_map/all_to_all | solution.py:49
  17.7 20.2 %collective-permute-start.2 = (bf16[2,2,64,1024]{3,2,1,0:T(8,128)(2,1)}, bf16[2,2,64,1024]{3,2,1,0:T(8,128)(2,1)}, u32[]{:S(2)}, u32[]{:S(2)}) collective-permute-start(bf16[2,2,64,1024]{3,2,1,0:T(8,128)(2,1)} %pad_maximum_fusion.4), channel_id=1, source_target_pairs={{0,64},{16,80},{32,96},{48,112},{64,0},{80,16},{96,32},{112,48},{1... | collective-permute-start | bytes 1572872 | tf_op jit(solution)/shard_map/ppermute | solution.py:29
  31.5 25.7 %all-to-all-start.1 = ((bf16[16,112,256]{2,1,0:T(8,128)(2,1)}), bf16[16,112,256]{2,1,0:T(8,128)(2,1)}, u32[]{:S(2)}, u32[]{:S(2)}) async-start(bf16[16,112,256]{2,1,0:T(8,128)(2,1)} %get-tuple-element.24), calls=%async_computation.1 | async-start | bytes 1835008 | tf_op jit(solution)/shard_map/all_to_all | solution.py:49
  35.8 17.6 %collective-permute-start.6 = (bf16[16,96,256]{2,1,0:T(8,128)(2,1)S(1)}, bf16[16,96,256]{2,1,0:T(8,128)(2,1)S(1)}, u32[]{:S(2)}, u32[]{:S(2)}) collective-permute-start(bf16[16,96,256]{2,1,0:T(8,128)(2,1)S(1)} %all-to-all-done.refs_4_), channel_id=1, source_target_pairs={{0,96},{16,112},{32,0},{48,16},{64,32},{80,48},{96,64},{112,80},{1... | collective-permute-start | bytes 2359304 | tf_op jit(solution)/shard_map/ppermute | solution.py:29
  37.6 18.8 %collective-permute-start.5 = (bf16[16,96,256]{2,1,0:T(8,128)(2,1)S(1)}, bf16[16,96,256]{2,1,0:T(8,128)(2,1)S(1)}, u32[]{:S(2)}, u32[]{:S(2)}) collective-permute-start(bf16[16,96,256]{2,1,0:T(8,128)(2,1)S(1)} %all-to-all-done.refs_4_), channel_id=1, source_target_pairs={{0,32},{16,48},{32,64},{48,80},{64,96},{80,112},{96,0},{112,16},{1... | collective-permute-start | bytes 2359304 | tf_op jit(solution)/shard_map/ppermute | solution.py:29
  39.0 7.8 %copy-start.4 = (s32[1,1,8]{2,1,0:T(1,128)S(1)}, s32[1,1,8]{2,1,0:T(1,128)}, u32[]{:S(2)}) copy-start(s32[1,1,8]{2,1,0:T(1,128)} %param.12) | copy-start | bytes 100
  41.1 30.1 %collective-permute-start.3 = (bf16[4,2,64,1024]{3,2,1,0:T(8,128)(2,1)}, bf16[4,2,64,1024]{3,2,1,0:T(8,128)(2,1)}, u32[]{:S(2)}, u32[]{:S(2)}) collective-permute-start(bf16[4,2,64,1024]{3,2,1,0:T(8,128)(2,1)} %pad_maximum_fusion.refs_0_), channel_id=1, source_target_pairs={{0,1},{1,2},{2,3},{3,0},{4,5},{5,6},{6,7},{7,4},{8,9},{9,10},{10,1... | collective-permute-start | bytes 3145736 | tf_op jit(solution)/shard_map/ppermute | solution.py:39
  43.9 27.3 %collective-permute-start.4 = (bf16[4,2,64,1024]{3,2,1,0:T(8,128)(2,1)}, bf16[4,2,64,1024]{3,2,1,0:T(8,128)(2,1)}, u32[]{:S(2)}, u32[]{:S(2)}) collective-permute-start(bf16[4,2,64,1024]{3,2,1,0:T(8,128)(2,1)} %pad_maximum_fusion.1.refs_1_), channel_id=1, source_target_pairs={{0,3},{1,0},{2,1},{3,2},{4,7},{5,4},{6,5},{7,6},{8,11},{9,8},{10,9... | collective-permute-start | bytes 3145736 | tf_op jit(solution)/shard_map/ppermute | solution.py:39
  53.4 17.9 %collective-permute-start.8 = (bf16[8,96,256]{2,1,0:T(8,128)(2,1)S(1)}, bf16[8,96,256]{2,1,0:T(8,128)(2,1)S(1)}, u32[]{:S(2)}, u32[]{:S(2)}) collective-permute-start(bf16[8,96,256]{2,1,0:T(8,128)(2,1)S(1)} %slice.48), channel_id=1, source_target_pairs={{0,96},{16,112},{32,0},{48,16},{64,32},{80,48},{96,64},{112,80},{1... | collective-permute-start | bytes 1179656 | tf_op jit(solution)/shard_map/ppermute | solution.py:29
  57.2 14.1 %collective-permute-start.7 = (bf16[8,96,256]{2,1,0:T(8,128)(2,1)}, bf16[8,96,256]{2,1,0:T(8,128)(2,1)S(1)}, u32[]{:S(2)}, u32[]{:S(2)}) collective-permute-start(bf16[8,96,256]{2,1,0:T(8,128)(2,1)} %slice.47), channel_id=1, source_target_pairs={{0,32},{16,48},{32,64},{48,80},{64,96},{80,112},{96,0},{112,16},{1... | collective-permute-start | bytes 1179656 | tf_op jit(solution)/shard_map/ppermute | solution.py:29
  78.5 5.5 %copy-start.1 = (bf16[16,96,512]{2,1,0:T(8,128)(2,1)S(1)}, bf16[16,96,512]{2,1,0:T(8,128)(2,1)}, u32[]{:S(2)}) copy-start(bf16[16,96,512]{2,1,0:T(8,128)(2,1)} %get-tuple-element.28.kept_ref) | copy-start | bytes 4718596
  78.6 5.4 %collective-permute-start.9 = (bf16[16,96,512]{2,1,0:T(8,128)(2,1)}, bf16[16,96,512]{2,1,0:T(8,128)(2,1)S(1)}, u32[]{:S(2)}, u32[]{:S(2)}) collective-permute-start(bf16[16,96,512]{2,1,0:T(8,128)(2,1)} %get-tuple-element.29), channel_id=1, source_target_pairs={{0,16},{16,0},{32,48},{48,32},{64,80},{80,64},{96,112},{112,96},{1... | collective-permute-start | bytes 4718600 | tf_op jit(solution)/shard_map/ppermute | solution.py:34
  79.9 22.0 %collective-permute-start.12 = (bf16[16,96,256]{2,1,0:T(8,128)(2,1)S(1)}, bf16[16,96,256]{2,1,0:T(8,128)(2,1)S(1)}, u32[]{:S(2)}, u32[]{:S(2)}) collective-permute-start(bf16[16,96,256]{2,1,0:T(8,128)(2,1)S(1)} %slice.49.refs_4_), channel_id=1, source_target_pairs={{0,64},{16,80},{32,96},{48,112},{64,0},{80,16},{96,32},{112,48},{1... | collective-permute-start | bytes 2359304 | tf_op jit(solution)/shard_map/ppermute | solution.py:29
  82.0 35.4 %collective-permute-start.11 = (bf16[16,96,256]{2,1,0:T(8,128)(2,1)S(1)}, bf16[16,96,256]{2,1,0:T(8,128)(2,1)S(1)}, u32[]{:S(2)}, u32[]{:S(2)}) collective-permute-start(bf16[16,96,256]{2,1,0:T(8,128)(2,1)S(1)} %slice.49.refs_4_), channel_id=1, source_target_pairs={{0,96},{16,112},{32,0},{48,16},{64,32},{80,48},{96,64},{112,80},{1... | collective-permute-start | bytes 2359304 | tf_op jit(solution)/shard_map/ppermute | solution.py:29
  83.0 35.2 %collective-permute-start.10 = (bf16[16,96,256]{2,1,0:T(8,128)(2,1)S(1)}, bf16[16,96,256]{2,1,0:T(8,128)(2,1)S(1)}, u32[]{:S(2)}, u32[]{:S(2)}) collective-permute-start(bf16[16,96,256]{2,1,0:T(8,128)(2,1)S(1)} %slice.49.refs_4_), channel_id=1, source_target_pairs={{0,32},{16,48},{32,64},{48,80},{64,96},{80,112},{96,0},{112,16},{1... | collective-permute-start | bytes 2359304 | tf_op jit(solution)/shard_map/ppermute | solution.py:29
  86.6 45.3 %all-to-all-start.2 = ((bf16[128,16,512]{2,1,0:T(8,128)(2,1)}), bf16[128,16,512]{2,1,0:T(8,128)(2,1)}, u32[]{:S(2)}, u32[]{:S(2)}) async-start(bf16[128,16,512]{2,1,0:T(8,128)(2,1)} %deal_to_slots.2), calls=%async_computation.2 | async-start | bytes 4194304 | tf_op jit(solution)/shard_map/all_to_all | solution.py:49
  125.5 3.7 %collective-permute-start.13 = (bf16[16,96,512]{2,1,0:T(8,128)(2,1)}, bf16[16,96,512]{2,1,0:T(8,128)(2,1)S(1)}, u32[]{:S(2)}, u32[]{:S(2)}) collective-permute-start(bf16[16,96,512]{2,1,0:T(8,128)(2,1)} %get-tuple-element.33), channel_id=1, source_target_pairs={{0,16},{16,0},{32,48},{48,32},{64,80},{80,64},{96,112},{112,96},{1... | collective-permute-start | bytes 4718600 | tf_op jit(solution)/shard_map/ppermute | solution.py:34
  129.2 1.4 copy-start.2

commit v4 on v3

--- a/solution.py
+++ b/solution.py
@@ -360,8 +360,6 @@
     first_parts = ring_in_two(first, along_y)
     pieces = (halves[0], halves[1], along_z(halves[0], 1), along_z(halves[1], -1))
     owner_of = second[:, base : base + blocks, 0].astype(jnp.int32)
-    second = after(second[:, :base], *first_parts)
-    second_parts = (second, along_y(second, 1), along_y(second, -1), along_y(second, 2))
 
     all_owners = jnp.arange(owner_total, dtype=jnp.int32)
     named = (owner_of[:, :, None] == all_owners).astype(jnp.int32)
@@ -377,7 +375,10 @@
     slot_range = jnp.arange(slot_total, dtype=jnp.int32)
     sources = jnp.where(slot_range < owner_counts.reshape(()), owned_sources.reshape(-1), -1)
     here = jnp.stack((core, parity)).astype(jnp.int32)
-    here, slots, sources = lax.optimization_barrier((here, slots, sources))
+    here, slots, sources, second = lax.optimization_barrier(
+        (here, slots, sources, second[:, :base], first_parts[1:3])
+    )[:4]
+    second_parts = (second, along_y(second, 1), along_y(second, -1), along_y(second, 2))
     dealt = sliced_slots(here, first_parts)
     arrived = exchange(dealt)
     dealt = sliced_slots(after(here, dealt), second_parts)

time: 280 us -> 279 us (level)
  waiting for transfers between devices: 51 us -> 56.1 us
  other arithmetic: 11.2 us -> 6.61 us
    ppermute x2, waiting for transfers between devices: 3.62 us -> 9.47 us  [along_z(): return lax.ppermute(value, 'mp', pairs)]
  transfers between devices with their start and end apart: 17 -> 17, of which waited for: 7 -> 7; matrix products, arithmetic and copies ran while one was open for 7% -> 4% of each run, Pallas kernels for 5% -> 5%
where the time goes in v4:
time: 279 us; the launch traced here: 277 us
  blocking collectives  132 us (47%)
  waiting for transfers between devices  56.1 us (20%)
  Pallas kernels  35.8 us (13%)
  starting transfers between devices  34.9 us (13%)
  local copies, waits for them, and re-layouts  10.3 us (4%)
  other arithmetic  6.61 us (2%)
    all_to_all x2, blocking collectives, exchange(): return lax.all_to_all(value, 'mp', split_axis=0, concat_axis=0, tiled=True)  132 us
    ppermute x10, waiting for transfers between devices, along_y(): return lax.ppermute(value, 'dp', pairs)  32.8 us
    all_to_all x3, starting transfers between devices, exchange(): return lax.all_to_all(value, 'mp', split_axis=0, concat_axis=0, tiled=True)  16.9 us
    pallas_call x2, Pallas kernels, gradient_partials(): pl.pallas_call(partial_kernel, in_specs=[pl.BlockSpec(memory_space=pltpu....  14.6 us
    ppermute x10, starting transfers between devices, along_y(): return lax.ppermute(value, 'dp', pairs)  14.5 us
    pallas_call x1, Pallas kernels, work_on_slots(): pl.pallas_call(slot_kernel, grid_spec=pltpu.PrefetchScalarGridSpec(num_sc...  12.8 us
    all_to_all x3, waiting for transfers between devices, exchange(): return lax.all_to_all(value, 'mp', split_axis=0, concat_axis=0, tiled=True)  10.3 us
    ppermute x2, waiting for transfers between devices, along_z(): return lax.ppermute(value, 'mp', pairs)  9.47 us
  transfers between devices with their start and end apart: 17, of which 7 were waited for; matrix products, arithmetic and copies ran while one was open for 4% of the time, Pallas kernels for 5%

profile of v4, /device:TPU:0, one launch (start us, length us, event | category | flops | bytes accessed | tf_op | source)
XLA Modules:
  0.0 277.0 jit_solution(8520601391237040119)
XLA Ops:
  0.7 1.8 dynamic-slice_bitcast_fusion
  2.6 1.7 collective-permute-start.2
  4.3 1.6 collective-permute-start.3
  6.0 0.8 pad_maximum_fusion.4
  6.8 2.2 split_cotangents.1
  9.0 8.0 %all-to-all-start = ((bf16[16,96,256]{2,1,0:T(8,128)(2,1)}), bf16[16,96,256]{2,1,0:T(8,128)(2,1)S(1)}, u32[]{:S(2)}, u32[]{:S(2)}) async-start(bf16[16,96,256]{2,1,0:T(8,128)(2,1)} %get-tuple-element.23), calls=%async_computation | async-start | bytes 1572864 | tf_op jit(solution)/shard_map/all_to_all | solution.py:49
  17.0 2.1 collective-permute-start.4
  19.0 0.7 fusion.1
  19.8 0.7 fusion.2
  20.5 10.3 %all-to-all-done.refs_4_ = bf16[16,96,256]{2,1,0:T(8,128)(2,1)S(1)} async-done(((bf16[16,96,256]{2,1,0:T(8,128)(2,1)}), bf16[16,96,256]{2,1,0:T(8,128)(2,1)S(1)}, u32[]{:S(2)}, u32[]{:S(2)}) %all-to-all-start) | async-done | bytes 786464 | tf_op jit(solution)/shard_map/all_to_all | solution.py:49
  30.8 4.3 %all-to-all-start.1 = ((bf16[16,112,256]{2,1,0:T(8,128)(2,1)}), bf16[16,112,256]{2,1,0:T(8,128)(2,1)}, u32[]{:S(2)}, u32[]{:S(2)}) async-start(bf16[16,112,256]{2,1,0:T(8,128)(2,1)} %get-tuple-element.24), calls=%async_computation.1 | async-start | bytes 1835008 | tf_op jit(solution)/shard_map/all_to_all | solution.py:49
  35.1 1.8 collective-permute-start.1
  36.9 0.3 collective-permute-start
  37.2 1.1 fusion.3
  38.3 2.2 pad_maximum_fusion.refs_0_
  40.4 1.7 collective-permute-start.5
  42.1 1.1 pad_maximum_fusion.1.refs_1_
  43.2 1.6 collective-permute-start.6
  45.5 7.1 %collective-permute-done.1.refs_6_ = bf16[16,96,256]{2,1,0:T(8,128)(2,1)S(1)} collective-permute-done((bf16[16,96,256]{2,1,0:T(8,128)(2,1)S(1)}, bf16[16,96,256]{2,1,0:T(8,128)(2,1)S(1)}, u32[]{:S(2)}, u32[]{:S(2)}) %collective-permute-start.1) | collective-permute-done | bytes 786464 | tf_op jit(solution)/shard_map/ppermute | solution.py:29
  52.6 0.8 slice.49
  53.4 2.9 %collective-permute-start.8 = (bf16[8,96,256]{2,1,0:T(8,128)(2,1)}, bf16[8,96,256]{2,1,0:T(8,128)(2,1)S(1)}, u32[]{:S(2)}, u32[]{:S(2)}) collective-permute-start(bf16[8,96,256]{2,1,0:T(8,128)(2,1)} %slice.49), channel_id=1, source_target_pairs={{0,96},{16,112},{32,0},{48,16},{64,32},{80,48},{96,64},{112,80},{1... | collective-permute-start | bytes 1179656 | tf_op jit(solution)/shard_map/ppermute | solution.py:29
  56.4 0.8 slice.48
  57.1 0.8 slice_convert_fusion
  57.9 1.1 multiply_reduce_fusion.1
  59.1 0.1 copy.14
  59.3 0.1 multiply_reduce_fusion
  59.4 0.2 select_reduce_fusion
  59.9 1.2 slice.41.refs_4_
  61.1 9.5 %collective-permute-done.5.refs_2_ = bf16[4,2,64,1024]{3,2,1,0:T(8,128)(2,1)} collective-permute-done((bf16[4,2,64,1024]{3,2,1,0:T(8,128)(2,1)}, bf16[4,2,64,1024]{3,2,1,0:T(8,128)(2,1)}, u32[]{:S(2)}, u32[]{:S(2)}) %collective-permute-start.5) | collective-permute-done | bytes 1048608 | tf_op jit(solution)/shard_map/ppermute | solution.py:39
  70.6 7.3 %gradient_partials.2 = (bf16[16,96,512]{2,1,0:T(8,128)(2,1)}, bf16[16,96,512]{2,1,0:T(8,128)(2,1)}) custom-call(s32[2]{0:T(128)S(1)} %pad_add_fusion.here_ref, bf16[4,2,64,1024]{3,2,1,0:T(8,128)(2,1)} %pad_maximum_fusion.refs_0_, bf16[4,2,64,1024]{3,2,1,0:T(8,128)(2,1)} %pad_maximum_fusion.1.refs_1_, ...), custom_call_target="tpu_custom_call" | custom-call | bytes 1024 | tf_op jit(solution)/shard_map/gradient_partials/pallas_call | solution.py:144
  78.0 2.0 collective-permute-start.12
  80.0 1.1 collective-permute-start.11
  81.0 1.0 collective-permute-start.10
  82.0 1.4 copy-done.1
  83.4 2.6 deal_to_slots.2
  86.0 4.6 %all-to-all-start.2 = ((bf16[128,16,512]{2,1,0:T(8,128)(2,1)}), bf16[128,16,512]{2,1,0:T(8,128)(2,1)}, u32[]{:S(2)}, u32[]{:S(2)}) async-start(bf16[128,16,512]{2,1,0:T(8,128)(2,1)} %deal_to_slots.2), calls=%async_computation.2 | async-start | bytes 4194304 | tf_op jit(solution)/shard_map/all_to_all | solution.py:49
  90.6 9.4 %collective-permute-done.12.refs_7_ = bf16[16,96,256]{2,1,0:T(8,128)(2,1)S(1)} collective-permute-done((bf16[16,96,256]{2,1,0:T(8,128)(2,1)S(1)}, bf16[16,96,256]{2,1,0:T(8,128)(2,1)S(1)}, u32[]{:S(2)}, u32[]{:S(2)}) %collective-permute-start.12) | collective-permute-done | bytes 786464 | tf_op jit(solution)/shard_map/ppermute | solution.py:29
  100.0 15.4 %collective-permute-done.11.refs_6_ = bf16[16,96,256]{2,1,0:T(8,128)(2,1)S(1)} collective-permute-done((bf16[16,96,256]{2,1,0:T(8,128)(2,1)S(1)}, bf16[16,96,256]{2,1,0:T(8,128)(2,1)S(1)}, u32[]{:S(2)}, u32[]{:S(2)}) %collective-permute-start.11) | collective-permute-done | bytes 786464 | tf_op jit(solution)/shard_map/ppermute | solution.py:29
  115.4 0.9 collective-permute-done.10.refs_5_
  116.3 7.2 %gradient_partials.3 = (bf16[16,96,512]{2,1,0:T(8,128)(2,1)}, bf16[16,96,512]{2,1,0:T(8,128)(2,1)}) custom-call(s32[2]{0:T(128)S(1)} %pad_add_fusion.here_ref, bf16[4,2,64,1024]{3,2,1,0:T(8,128)(2,1)} %pad_maximum_fusion.refs_0_, bf16[4,2,64,1024]{3,2,1,0:T(8,128)(2,1)} %pad_maximum_fusion.1.refs_1_, ...), custom_call_target="tpu_custom_call" | custom-call | bytes 1024 | tf_op jit(solution)/shard_map/gradient_partials/pallas_call | solution.py:144
  123.5 0.2 collective-permute-start.13
  123.8 3.5 %collective-permute-done.13.got_ref = bf16[16,96,512]{2,1,0:T(8,128)(2,1)S(1)} collective-permute-done((bf16[16,96,512]{2,1,0:T(8,128)(2,1)}, bf16[16,96,512]{2,1,0:T(8,128)(2,1)S(1)}, u32[]{:S(2)}, u32[]{:S(2)}) %collective-permute-start.13) | collective-permute-done | bytes 1572896 | tf_op jit(solution)/shard_map/ppermute | solution.py:34
  127.3 1.4 copy-done.2
  128.7 1.2 deal_to_slots.3
  129.9 32.9 %all_to_all.25 = bf16[128,16,512]{2,1,0:T(8,128)(2,1)} all-to-all(bf16[128,16,512]{2,1,0:T(8,128)(2,1)S(1)} %deal_to_slots.3), channel_id=1, replica_groups=mesh['dp'=8,'mp'=16] {'mp'}, dimensions={0} | all-to-all | bytes 4194304 | tf_op jit(solution)/shard_map/all_to_all | solution.py:49
  162.8 12.8 %work_on_slots.1 = (bf16[16,512,512]{2,1,0:T(8,128)(2,1)}, bf16[8,512,512]{2,1,0:T(8,128)(2,1)}, bf16[8,512,512]{2,1,0:T(8,128)(2,1)}) custom-call(s32[8]{0:T(128)S(1)} %compare_select_fusion.source_ref, bf16[8,512,512]{2,1,0:T(8,128)(2,1)} %bitcast.35, bf16[8,512,512]{2,1,0:T(8,128)(2,1)} %bitcast.36, bf16[16,8,16,512]{3,2,1,0:T(8,128)(2,1)} %bitcast.16.first_ref, ...), custom_call_target="tpu_custom_call" | custom-call | flops 8589934592 | bytes 25165824 | tf_op jit(solution)/shard_map/work_on_slots/pallas_call | solution.py:244
  175.6 98.7 %all_to_all.26.returned_ref = bf16[16,512,512]{2,1,0:T(8,128)(2,1)S(1)} all-to-all(bf16[16,512,512]{2,1,0:T(8,128)(2,1)} %get-tuple-element.36), channel_id=1, replica_groups=mesh['dp'=8,'mp'=16] {'mp'}, dimensions={0} | all-to-all | bytes 16777216 | tf_op jit(solution)/shard_map/all_to_all | solution.py:49
  274.3 2.5 place_blocks.1
  (30 shorter events, 0.7 us)
Async XLA Ops:
  2.5 4.4 %copy-start = (bf16[2,256,1536]{2,1,0:T(8,128)(2,1)S(1)}, bf16[2,256,1536]{2,1,0:T(8,128)(2,1)}, u32[]{:S(2)}) copy-start(bf16[2,256,1536]{2,1,0:T(8,128)(2,1)} %cot_ref) | copy-start | bytes 4718596
  2.5 4.3 %copy-start.3 = (s32[1,1,6]{2,1,0:T(1,128)S(1)}, s32[1,1,6]{2,1,0:T(1,128)}, u32[]{:S(2)}) copy-start(s32[1,1,6]{2,1,0:T(1,128)} %param.11) | copy-start | bytes 76
  2.6 16.5 %collective-permute-start.2 = (bf16[2,2,64,1024]{3,2,1,0:T(8,128)(2,1)S(1)}, bf16[2,2,64,1024]{3,2,1,0:T(8,128)(2,1)S(1)}, u32[]{:S(2)}, u32[]{:S(2)}) collective-permute-start(bf16[2,2,64,1024]{3,2,1,0:T(8,128)(2,1)S(1)} %pad_maximum_fusion.2), channel_id=1, source_target_pairs={{0,32},{16,48},{32,64},{48,80},{64,96},{80,112},{96,0},{112,16},{1... | collective-permute-start | bytes 1572872 | tf_op jit(solution)/shard_map/ppermute | solution.py:29
  4.3 15.4 %collective-permute-start.3 = (bf16[2,2,64,1024]{3,2,1,0:T(8,128)(2,1)S(1)}, bf16[2,2,64,1024]{3,2,1,0:T(8,128)(2,1)S(1)}, u32[]{:S(2)}, u32[]{:S(2)}) collective-permute-start(bf16[2,2,64,1024]{3,2,1,0:T(8,128)(2,1)S(1)} %pad_maximum_fusion.3), channel_id=1, source_target_pairs={{0,96},{16,112},{32,0},{48,16},{64,32},{80,48},{96,64},{112,80},{1... | collective-permute-start | bytes 1572872 | tf_op jit(solution)/shard_map/ppermute | solution.py:29
  9.0 21.8 %all-to-all-start = ((bf16[16,96,256]{2,1,0:T(8,128)(2,1)}), bf16[16,96,256]{2,1,0:T(8,128)(2,1)S(1)}, u32[]{:S(2)}, u32[]{:S(2)}) async-start(bf16[16,96,256]{2,1,0:T(8,128)(2,1)} %get-tuple-element.23), calls=%async_computation | async-start | bytes 1572864 | tf_op jit(solution)/shard_map/all_to_all | solution.py:49
  17.0 20.2 %collective-permute-start.4 = (bf16[2,2,64,1024]{3,2,1,0:T(8,128)(2,1)}, bf16[2,2,64,1024]{3,2,1,0:T(8,128)(2,1)}, u32[]{:S(2)}, u32[]{:S(2)}) collective-permute-start(bf16[2,2,64,1024]{3,2,1,0:T(8,128)(2,1)} %pad_maximum_fusion.4), channel_id=1, source_target_pairs={{0,64},{16,80},{32,96},{48,112},{64,0},{80,16},{96,32},{112,48},{1... | collective-permute-start | bytes 1572872 | tf_op jit(solution)/shard_map/ppermute | solution.py:29
  30.8 26.4 %all-to-all-start.1 = ((bf16[16,112,256]{2,1,0:T(8,128)(2,1)}), bf16[16,112,256]{2,1,0:T(8,128)(2,1)}, u32[]{:S(2)}, u32[]{:S(2)}) async-start(bf16[16,112,256]{2,1,0:T(8,128)(2,1)} %get-tuple-element.24), calls=%async_computation.1 | async-start | bytes 1835008 | tf_op jit(solution)/shard_map/all_to_all | solution.py:49
  35.1 17.6 %collective-permute-start.1 = (bf16[16,96,256]{2,1,0:T(8,128)(2,1)S(1)}, bf16[16,96,256]{2,1,0:T(8,128)(2,1)S(1)}, u32[]{:S(2)}, u32[]{:S(2)}) collective-permute-start(bf16[16,96,256]{2,1,0:T(8,128)(2,1)S(1)} %all-to-all-done.refs_4_), channel_id=1, source_target_pairs={{0,96},{16,112},{32,0},{48,16},{64,32},{80,48},{96,64},{112,80},{1... | collective-permute-start | bytes 2359304 | tf_op jit(solution)/shard_map/ppermute | solution.py:29
  36.9 19.5 %collective-permute-start = (bf16[16,96,256]{2,1,0:T(8,128)(2,1)S(1)}, bf16[16,96,256]{2,1,0:T(8,128)(2,1)S(1)}, u32[]{:S(2)}, u32[]{:S(2)}) collective-permute-start(bf16[16,96,256]{2,1,0:T(8,128)(2,1)S(1)} %all-to-all-done.refs_4_), channel_id=1, source_target_pairs={{0,32},{16,48},{32,64},{48,80},{64,96},{80,112},{96,0},{112,16},{1... | collective-permute-start | bytes 2359304 | tf_op jit(solution)/shard_map/ppermute | solution.py:29
  38.3 7.3 %copy-start.4 = (s32[1,1,8]{2,1,0:T(1,128)S(1)}, s32[1,1,8]{2,1,0:T(1,128)}, u32[]{:S(2)}) copy-start(s32[1,1,8]{2,1,0:T(1,128)} %param.12) | copy-start | bytes 100
  40.4 30.1 %collective-permute-start.5 = (bf16[4,2,64,1024]{3,2,1,0:T(8,128)(2,1)}, bf16[4,2,64,1024]{3,2,1,0:T(8,128)(2,1)}, u32[]{:S(2)}, u32[]{:S(2)}) collective-permute-start(bf16[4,2,64,1024]{3,2,1,0:T(8,128)(2,1)} %pad_maximum_fusion.refs_0_), channel_id=1, source_target_pairs={{0,1},{1,2},{2,3},{3,0},{4,5},{5,6},{6,7},{7,4},{8,9},{9,10},{10,1... | collective-permute-start | bytes 3145736 | tf_op jit(solution)/shard_map/ppermute | solution.py:39
  43.2 27.3 %collective-permute-start.6 = (bf16[4,2,64,1024]{3,2,1,0:T(8,128)(2,1)}, bf16[4,2,64,1024]{3,2,1,0:T(8,128)(2,1)}, u32[]{:S(2)}, u32[]{:S(2)}) collective-permute-start(bf16[4,2,64,1024]{3,2,1,0:T(8,128)(2,1)} %pad_maximum_fusion.1.refs_1_), channel_id=1, source_target_pairs={{0,3},{1,0},{2,1},{3,2},{4,7},{5,4},{6,5},{7,6},{8,11},{9,8},{10,9... | collective-permute-start | bytes 3145736 | tf_op jit(solution)/shard_map/ppermute | solution.py:39
  53.4 17.1 %collective-permute-start.8 = (bf16[8,96,256]{2,1,0:T(8,128)(2,1)}, bf16[8,96,256]{2,1,0:T(8,128)(2,1)S(1)}, u32[]{:S(2)}, u32[]{:S(2)}) collective-permute-start(bf16[8,96,256]{2,1,0:T(8,128)(2,1)} %slice.49), channel_id=1, source_target_pairs={{0,96},{16,112},{32,0},{48,16},{64,32},{80,48},{96,64},{112,80},{1... | collective-permute-start | bytes 1179656 | tf_op jit(solution)/shard_map/ppermute | solution.py:29
  57.1 13.4 %collective-permute-start.7 = (bf16[8,96,256]{2,1,0:T(8,128)(2,1)}, bf16[8,96,256]{2,1,0:T(8,128)(2,1)}, u32[]{:S(2)}, u32[]{:S(2)}) collective-permute-start(bf16[8,96,256]{2,1,0:T(8,128)(2,1)} %slice.48), channel_id=1, source_target_pairs={{0,32},{16,48},{32,64},{48,80},{64,96},{80,112},{96,0},{112,16},{1... | collective-permute-start | bytes 1179656 | tf_op jit(solution)/shard_map/ppermute | solution.py:29
  77.9 4.1 %collective-permute-start.9 = (bf16[16,96,512]{2,1,0:T(8,128)(2,1)}, bf16[16,96,512]{2,1,0:T(8,128)(2,1)S(1)}, u32[]{:S(2)}, u32[]{:S(2)}) collective-permute-start(bf16[16,96,512]{2,1,0:T(8,128)(2,1)} %get-tuple-element.29), channel_id=1, source_target_pairs={{0,16},{16,0},{32,48},{48,32},{64,80},{80,64},{96,112},{112,96},{1... | collective-permute-start | bytes 4718600 | tf_op jit(solution)/shard_map/ppermute | solution.py:34
  78.0 22.0 %collective-permute-start.12 = (bf16[16,96,256]{2,1,0:T(8,128)(2,1)S(1)}, bf16[16,96,256]{2,1,0:T(8,128)(2,1)S(1)}, u32[]{:S(2)}, u32[]{:S(2)}) collective-permute-start(bf16[16,96,256]{2,1,0:T(8,128)(2,1)S(1)} %slice.41.refs_4_), channel_id=1, source_target_pairs={{0,64},{16,80},{32,96},{48,112},{64,0},{80,16},{96,32},{112,48},{1... | collective-permute-start | bytes 2359304 | tf_op jit(solution)/shard_map/ppermute | solution.py:29
  80.0 35.4 %collective-permute-start.11 = (bf16[16,96,256]{2,1,0:T(8,128)(2,1)S(1)}, bf16[16,96,256]{2,1,0:T(8,128)(2,1)S(1)}, u32[]{:S(2)}, u32[]{:S(2)}) collective-permute-start(bf16[16,96,256]{2,1,0:T(8,128)(2,1)S(1)} %slice.41.refs_4_), channel_id=1, source_target_pairs={{0,96},{16,112},{32,0},{48,16},{64,32},{80,48},{96,64},{112,80},{1... | collective-permute-start | bytes 2359304 | tf_op jit(solution)/shard_map/ppermute | solution.py:29
  81.0 35.3 %collective-permute-start.10 = (bf16[16,96,256]{2,1,0:T(8,128)(2,1)S(1)}, bf16[16,96,256]{2,1,0:T(8,128)(2,1)S(1)}, u32[]{:S(2)}, u32[]{:S(2)}) collective-permute-start(bf16[16,96,256]{2,1,0:T(8,128)(2,1)S(1)} %slice.41.refs_4_), channel_id=1, source_target_pairs={{0,32},{16,48},{32,64},{48,80},{64,96},{80,112},{96,0},{112,16},{1... | collective-permute-start | bytes 2359304 | tf_op jit(solution)/shard_map/ppermute | solution.py:29
  82.0 1.4 copy-start.1
  86.0 44.0 %all-to-all-start.2 = ((bf16[128,16,512]{2,1,0:T(8,128)(2,1)}), bf16[128,16,512]{2,1,0:T(8,128)(2,1)}, u32[]{:S(2)}, u32[]{:S(2)}) async-start(bf16[128,16,512]{2,1,0:T(8,128)(2,1)} %deal_to_slots.2), calls=%async_computation.2 | async-start | bytes 4194304 | tf_op jit(solution)/shard_map/all_to_all | solution.py:49
  123.5 3.7 %collective-permute-start.13 = (bf16[16,96,512]{2,1,0:T(8,128)(2,1)}, bf16[16,96,512]{2,1,0:T(8,128)(2,1)S(1)}, u32[]{:S(2)}, u32[]{:S(2)}) collective-permute-start(bf16[16,96,512]{2,1,0:T(8,128)(2,1)} %get-tuple-element.33), channel_id=1, source_target_pairs={{0,16},{16,0},{32,48},{48,32},{64,80},{80,64},{96,112},{112,96},{1... | collective-permute-start | bytes 4718600 | tf_op jit(solution)/shard_map/ppermute | solution.py:34
  127.2 1.4 copy-start.2

commit v5 on v4

--- a/solution.py
+++ b/solution.py
@@ -152,7 +152,7 @@
             pltpu.SemaphoreType.DMA((layers, inputs)),
         ],
         out_shape=[shape, shape],
-        compiler_params=pltpu.CompilerParams(vmem_limit_bytes=50 * MIB),
+        compiler_params=pltpu.CompilerParams(vmem_limit_bytes=36 * MIB),
         cost_estimate=pl.CostEstimate(flops=0, bytes_accessed=1024, transcendentals=0),
         name="gradient_partials",
     )(here, *pieces, *parts)

time: 279 us -> 279 us (level)
  waiting for transfers between devices: 56.1 us -> 45.5 us
  starting transfers between devices: 34.9 us -> 41.7 us
  Pallas kernels: 35.8 us -> 30.4 us
  local copies, waits for them, and re-layouts: 10.3 us -> 15 us
  blocking collectives: 132 us -> 135 us
    ppermute x2, waiting for transfers between devices: 9.47 us -> 0.01 us  [along_z(): return lax.ppermute(value, 'mp', pairs)]
    ppermute x10, starting transfers between devices: 14.5 us -> 19 us  [along_y(): return lax.ppermute(value, 'dp', pairs)]
    all_to_all x2, blocking collectives: 132 us -> 135 us  [exchange(): return lax.all_to_all(value, 'mp', split_axis=0, concat_axis=0, tiled=True)]
    pallas_call x2, Pallas kernels: 14.6 us -> 11.5 us  [gradient_partials(): pl.pallas_call(partial_kernel, in_specs=[pl.BlockSpec(memory_space=pltpu....]
    another operation x2, other arithmetic: 3.26 us -> 0.27 us  [on_device(): halves = [jnp.stack([piece[u] for piece in from_chips]) for u in range(2)]]
  transfers between devices with their start and end apart: 17 -> 17, of which waited for: 7 -> 5; matrix products, arithmetic and copies ran while one was open for 4% -> 6% of each run, Pallas kernels for 5% -> 4%
where the time goes in v5:
time: 279 us; the launch traced here: 277 us
  blocking collectives  135 us (48%)
  waiting for transfers between devices  45.5 us (16%)
  starting transfers between devices  41.7 us (15%)
  Pallas kernels  30.4 us (11%)
  local copies, waits for them, and re-layouts  15 us (5%)
  other arithmetic  7.5 us (3%)
    all_to_all x2, blocking collectives, exchange(): return lax.all_to_all(value, 'mp', split_axis=0, concat_axis=0, tiled=True)  135 us
    ppermute x10, waiting for transfers between devices, along_y(): return lax.ppermute(value, 'dp', pairs)  31.8 us
    all_to_all x3, starting transfers between devices, exchange(): return lax.all_to_all(value, 'mp', split_axis=0, concat_axis=0, tiled=True)  19.2 us
    ppermute x10, starting transfers between devices, along_y(): return lax.ppermute(value, 'dp', pairs)  19 us
    pallas_call x1, Pallas kernels, work_on_slots(): pl.pallas_call(slot_kernel, grid_spec=pltpu.PrefetchScalarGridSpec(num_sc...  11.8 us
    pallas_call x2, Pallas kernels, gradient_partials(): pl.pallas_call(partial_kernel, in_specs=[pl.BlockSpec(memory_space=pltpu....  11.5 us
    all_to_all x3, waiting for transfers between devices, exchange(): return lax.all_to_all(value, 'mp', split_axis=0, concat_axis=0, tiled=True)  10.3 us
  transfers between devices with their start and end apart: 17, of which 5 were waited for; matrix products, arithmetic and copies ran while one was open for 6% of the time, Pallas kernels for 4%

profile of v5, /device:TPU:0, one launch (start us, length us, event | category | flops | bytes accessed | tf_op | source)
XLA Modules:
  0.0 277.0 jit_solution(10565696802607646514)
XLA Ops:
  0.7 1.8 dynamic-slice_bitcast_fusion
  2.6 1.7 collective-permute-start.2
  4.3 0.8 pad_maximum_fusion.3
  5.1 1.6 collective-permute-start.3
  6.8 2.2 split_cotangents.1
  8.9 8.0 %all-to-all-start = ((bf16[16,96,256]{2,1,0:T(8,128)(2,1)}), bf16[16,96,256]{2,1,0:T(8,128)(2,1)}, u32[]{:S(2)}, u32[]{:S(2)}) async-start(bf16[16,96,256]{2,1,0:T(8,128)(2,1)} %get-tuple-element.23), calls=%async_computation | async-start | bytes 1572864 | tf_op jit(solution)/shard_map/all_to_all | solution.py:49
  17.0 2.1 collective-permute-start.4
  19.0 0.7 fusion.1
  19.8 0.7 fusion.2
  20.5 10.3 %all-to-all-done.refs_4_ = bf16[16,96,256]{2,1,0:T(8,128)(2,1)} async-done(((bf16[16,96,256]{2,1,0:T(8,128)(2,1)}), bf16[16,96,256]{2,1,0:T(8,128)(2,1)}, u32[]{:S(2)}, u32[]{:S(2)}) %all-to-all-start) | async-done | bytes 786464 | tf_op jit(solution)/shard_map/all_to_all | solution.py:49
  30.8 4.3 %all-to-all-start.1 = ((bf16[16,112,256]{2,1,0:T(8,128)(2,1)}), bf16[16,112,256]{2,1,0:T(8,128)(2,1)}, u32[]{:S(2)}, u32[]{:S(2)}) async-start(bf16[16,112,256]{2,1,0:T(8,128)(2,1)} %get-tuple-element.24), calls=%async_computation.1 | async-start | bytes 1835008 | tf_op jit(solution)/shard_map/all_to_all | solution.py:49
  35.2 6.5 %collective-permute-start.1 = (bf16[16,96,256]{2,1,0:T(8,128)(2,1)}, bf16[16,96,256]{2,1,0:T(8,128)(2,1)S(1)}, u32[]{:S(2)}, u32[]{:S(2)}) collective-permute-start(bf16[16,96,256]{2,1,0:T(8,128)(2,1)} %all-to-all-done.refs_4_), channel_id=1, source_target_pairs={{0,96},{16,112},{32,0},{48,16},{64,32},{80,48},{96,64},{112,80},{1... | collective-permute-start | bytes 2359304 | tf_op jit(solution)/shard_map/ppermute | solution.py:29
  41.7 0.1 pad_maximum_fusion.refs_0_
  41.9 1.9 collective-permute-start.5
  44.0 1.4 collective-permute-start.6
  46.1 0.6 fusion
  46.7 6.2 %collective-permute-done.1.refs_6_ = bf16[16,96,256]{2,1,0:T(8,128)(2,1)S(1)} collective-permute-done((bf16[16,96,256]{2,1,0:T(8,128)(2,1)}, bf16[16,96,256]{2,1,0:T(8,128)(2,1)S(1)}, u32[]{:S(2)}, u32[]{:S(2)}) %collective-permute-start.1) | collective-permute-done | bytes 786464 | tf_op jit(solution)/shard_map/ppermute | solution.py:29
  52.9 0.8 slice.49
  53.7 0.9 copy-done.1
  54.6 2.9 %collective-permute-start.8 = (bf16[8,96,256]{2,1,0:T(8,128)(2,1)}, bf16[8,96,256]{2,1,0:T(8,128)(2,1)S(1)}, u32[]{:S(2)}, u32[]{:S(2)}) collective-permute-start(bf16[8,96,256]{2,1,0:T(8,128)(2,1)} %slice.49), channel_id=1, source_target_pairs={{0,96},{16,112},{32,0},{48,16},{64,32},{80,48},{96,64},{112,80},{1... | collective-permute-start | bytes 1179656 | tf_op jit(solution)/shard_map/ppermute | solution.py:29
  57.5 0.8 slice.48
  58.3 0.9 copy-done.3
  59.2 1.4 slice_convert_fusion
  60.6 1.7 multiply_reduce_fusion.1
  62.3 1.4 mul.77
  63.7 1.0 copy.14
  64.7 0.8 multiply_reduce_fusion
  65.5 0.8 select_reduce_fusion
  66.4 1.4 copy.15
  67.7 1.3 reduce_sum.32
  69.0 0.8 add.60.slot_ref
  69.8 2.1 slice.41.refs_4_
  71.9 5.7 %gradient_partials.2 = (bf16[16,96,512]{2,1,0:T(8,128)(2,1)S(1)}, bf16[16,96,512]{2,1,0:T(8,128)(2,1)S(1)}) custom-call(s32[2]{0:T(128)S(1)} %pad_add_fusion.here_ref, bf16[4,2,64,1024]{3,2,1,0:T(8,128)(2,1)S(1)} %pad_maximum_fusion.refs_0_, bf16[4,2,64,1024]{3,2,1,0:T(8,128)(2,1)S(1)} %pad_maximum_fusion.1.refs_1_, ...), custom_call_target="tpu_custom_call" | custom-call | bytes 1024 | tf_op jit(solution)/shard_map/gradient_partials/pallas_call | solution.py:144
  77.7 1.5 collective-permute-start.12
  79.2 1.9 collective-permute-start.11
  81.1 0.8 collective-permute-start.10
  81.8 1.3 deal_to_slots.2
  83.1 1.3 copy-done
  84.4 6.9 %all-to-all-start.2 = ((bf16[128,16,512]{2,1,0:T(8,128)(2,1)}), bf16[128,16,512]{2,1,0:T(8,128)(2,1)}, u32[]{:S(2)}, u32[]{:S(2)}) async-start(bf16[128,16,512]{2,1,0:T(8,128)(2,1)} %copy-done), calls=%async_computation.2 | async-start | bytes 4194304 | tf_op jit(solution)/shard_map/all_to_all | solution.py:49
  91.3 8.6 %collective-permute-done.12.refs_7_ = bf16[16,96,256]{2,1,0:T(8,128)(2,1)} collective-permute-done((bf16[16,96,256]{2,1,0:T(8,128)(2,1)}, bf16[16,96,256]{2,1,0:T(8,128)(2,1)}, u32[]{:S(2)}, u32[]{:S(2)}) %collective-permute-start.12) | collective-permute-done | bytes 786464 | tf_op jit(solution)/shard_map/ppermute | solution.py:29
  100.0 16.9 %collective-permute-done.11.refs_6_ = bf16[16,96,256]{2,1,0:T(8,128)(2,1)} collective-permute-done((bf16[16,96,256]{2,1,0:T(8,128)(2,1)}, bf16[16,96,256]{2,1,0:T(8,128)(2,1)}, u32[]{:S(2)}, u32[]{:S(2)}) %collective-permute-start.11) | collective-permute-done | bytes 786464 | tf_op jit(solution)/shard_map/ppermute | solution.py:29
  116.9 5.9 %gradient_partials.3 = (bf16[16,96,512]{2,1,0:T(8,128)(2,1)S(1)}, bf16[16,96,512]{2,1,0:T(8,128)(2,1)S(1)}) custom-call(s32[2]{0:T(128)S(1)} %pad_add_fusion.here_ref, bf16[4,2,64,1024]{3,2,1,0:T(8,128)(2,1)S(1)} %pad_maximum_fusion.refs_0_, bf16[4,2,64,1024]{3,2,1,0:T(8,128)(2,1)S(1)} %pad_maximum_fusion.1.refs_1_, ...), custom_call_target="tpu_custom_call" | custom-call | bytes 1024 | tf_op jit(solution)/shard_map/gradient_partials/pallas_call | solution.py:144
  122.9 3.4 %collective-permute-done.13.got_ref = bf16[16,96,512]{2,1,0:T(8,128)(2,1)S(1)} collective-permute-done((bf16[16,96,512]{2,1,0:T(8,128)(2,1)S(1)}, bf16[16,96,512]{2,1,0:T(8,128)(2,1)S(1)}, u32[]{:S(2)}, u32[]{:S(2)}) %collective-permute-start.13) | collective-permute-done | bytes 1572896 | tf_op jit(solution)/shard_map/ppermute | solution.py:34
  126.3 1.2 deal_to_slots.3
  127.5 35.4 %all_to_all.25 = bf16[128,16,512]{2,1,0:T(8,128)(2,1)} all-to-all(bf16[128,16,512]{2,1,0:T(8,128)(2,1)S(1)} %deal_to_slots.3), channel_id=1, replica_groups=mesh['dp'=8,'mp'=16] {'mp'}, dimensions={0} | all-to-all | bytes 4194304 | tf_op jit(solution)/shard_map/all_to_all | solution.py:49
  162.9 11.8 %work_on_slots.1 = (bf16[16,512,512]{2,1,0:T(8,128)(2,1)}, bf16[8,512,512]{2,1,0:T(8,128)(2,1)}, bf16[8,512,512]{2,1,0:T(8,128)(2,1)}) custom-call(s32[8]{0:T(128)S(1)} %compare_select_fusion.source_ref, bf16[8,512,512]{2,1,0:T(8,128)(2,1)} %bitcast.35, bf16[8,512,512]{2,1,0:T(8,128)(2,1)} %bitcast.36, bf16[16,8,16,512]{3,2,1,0:T(8,128)(2,1)} %bitcast.16.first_ref, ...), custom_call_target="tpu_custom_call" | custom-call | flops 8589934592 | bytes 25165824 | tf_op jit(solution)/shard_map/work_on_slots/pallas_call | solution.py:244
  174.7 99.7 %all_to_all.26.returned_ref = bf16[16,512,512]{2,1,0:T(8,128)(2,1)S(1)} all-to-all(bf16[16,512,512]{2,1,0:T(8,128)(2,1)} %get-tuple-element.36), channel_id=1, replica_groups=mesh['dp'=8,'mp'=16] {'mp'}, dimensions={0} | all-to-all | bytes 16777216 | tf_op jit(solution)/shard_map/all_to_all | solution.py:49
  274.3 2.5 place_blocks.1
  (40 shorter events, 0.7 us)
Async XLA Ops:
  2.5 4.3 %copy-start.5 = (bf16[2,256,1536]{2,1,0:T(8,128)(2,1)S(1)}, bf16[2,256,1536]{2,1,0:T(8,128)(2,1)}, u32[]{:S(2)}) copy-start(bf16[2,256,1536]{2,1,0:T(8,128)(2,1)} %cot_ref) | copy-start | bytes 4718596
  2.5 4.3 %copy-start.6 = (s32[1,1,6]{2,1,0:T(1,128)S(1)}, s32[1,1,6]{2,1,0:T(1,128)}, u32[]{:S(2)}) copy-start(s32[1,1,6]{2,1,0:T(1,128)} %param.11) | copy-start | bytes 76
  2.6 16.5 %collective-permute-start.2 = (bf16[2,2,64,1024]{3,2,1,0:T(8,128)(2,1)S(1)}, bf16[2,2,64,1024]{3,2,1,0:T(8,128)(2,1)S(1)}, u32[]{:S(2)}, u32[]{:S(2)}) collective-permute-start(bf16[2,2,64,1024]{3,2,1,0:T(8,128)(2,1)S(1)} %pad_maximum_fusion.2), channel_id=1, source_target_pairs={{0,32},{16,48},{32,64},{48,80},{64,96},{80,112},{96,0},{112,16},{1... | collective-permute-start | bytes 1572872 | tf_op jit(solution)/shard_map/ppermute | solution.py:29
  5.1 14.6 %collective-permute-start.3 = (bf16[2,2,64,1024]{3,2,1,0:T(8,128)(2,1)}, bf16[2,2,64,1024]{3,2,1,0:T(8,128)(2,1)S(1)}, u32[]{:S(2)}, u32[]{:S(2)}) collective-permute-start(bf16[2,2,64,1024]{3,2,1,0:T(8,128)(2,1)} %pad_maximum_fusion.3), channel_id=1, source_target_pairs={{0,96},{16,112},{32,0},{48,16},{64,32},{80,48},{96,64},{112,80},{1... | collective-permute-start | bytes 1572872 | tf_op jit(solution)/shard_map/ppermute | solution.py:29
  8.9 21.9 %all-to-all-start = ((bf16[16,96,256]{2,1,0:T(8,128)(2,1)}), bf16[16,96,256]{2,1,0:T(8,128)(2,1)}, u32[]{:S(2)}, u32[]{:S(2)}) async-start(bf16[16,96,256]{2,1,0:T(8,128)(2,1)} %get-tuple-element.23), calls=%async_computation | async-start | bytes 1572864 | tf_op jit(solution)/shard_map/all_to_all | solution.py:49
  17.0 24.7 %collective-permute-start.4 = (bf16[2,2,64,1024]{3,2,1,0:T(8,128)(2,1)S(1)}, bf16[2,2,64,1024]{3,2,1,0:T(8,128)(2,1)S(1)}, u32[]{:S(2)}, u32[]{:S(2)}) collective-permute-start(bf16[2,2,64,1024]{3,2,1,0:T(8,128)(2,1)S(1)} %pad_maximum_fusion.4), channel_id=1, source_target_pairs={{0,64},{16,80},{32,96},{48,112},{64,0},{80,16},{96,32},{112,48},{1... | collective-permute-start | bytes 1572872 | tf_op jit(solution)/shard_map/ppermute | solution.py:29
  30.8 28.4 %all-to-all-start.1 = ((bf16[16,112,256]{2,1,0:T(8,128)(2,1)}), bf16[16,112,256]{2,1,0:T(8,128)(2,1)}, u32[]{:S(2)}, u32[]{:S(2)}) async-start(bf16[16,112,256]{2,1,0:T(8,128)(2,1)} %get-tuple-element.24), calls=%async_computation.1 | async-start | bytes 1835008 | tf_op jit(solution)/shard_map/all_to_all | solution.py:49
  35.2 8.7 %copy-start.7 = (bf16[1,2,64,1024]{3,2,1,0:T(8,128)(2,1)S(1)}, bf16[1,2,64,1024]{3,2,1,0:T(8,128)(2,1)}, u32[]{:S(2)}) copy-start(bf16[1,2,64,1024]{3,2,1,0:T(8,128)(2,1)} %get-tuple-element.47) | copy-start | bytes 786436
  35.2 8.7 %copy-start.8 = (bf16[1,2,64,1024]{3,2,1,0:T(8,128)(2,1)S(1)}, bf16[1,2,64,1024]{3,2,1,0:T(8,128)(2,1)}, u32[]{:S(2)}) copy-start(bf16[1,2,64,1024]{3,2,1,0:T(8,128)(2,1)} %get-tuple-element.49) | copy-start | bytes 786436
  35.2 17.8 %collective-permute-start.1 = (bf16[16,96,256]{2,1,0:T(8,128)(2,1)}, bf16[16,96,256]{2,1,0:T(8,128)(2,1)S(1)}, u32[]{:S(2)}, u32[]{:S(2)}) collective-permute-start(bf16[16,96,256]{2,1,0:T(8,128)(2,1)} %all-to-all-done.refs_4_), channel_id=1, source_target_pairs={{0,96},{16,112},{32,0},{48,16},{64,32},{80,48},{96,64},{112,80},{1... | collective-permute-start | bytes 2359304 | tf_op jit(solution)/shard_map/ppermute | solution.py:29
  41.7 15.9 %collective-permute-start = (bf16[16,96,256]{2,1,0:T(8,128)(2,1)}, bf16[16,96,256]{2,1,0:T(8,128)(2,1)S(1)}, u32[]{:S(2)}, u32[]{:S(2)}) collective-permute-start(bf16[16,96,256]{2,1,0:T(8,128)(2,1)} %all-to-all-done.refs_4_), channel_id=1, source_target_pairs={{0,32},{16,48},{32,64},{48,80},{64,96},{80,112},{96,0},{112,16},{1... | collective-permute-start | bytes 2359304 | tf_op jit(solution)/shard_map/ppermute | solution.py:29
  41.7 5.0 %copy-start.9 = (s32[1,1,8]{2,1,0:T(1,128)S(1)}, s32[1,1,8]{2,1,0:T(1,128)}, u32[]{:S(2)}) copy-start(s32[1,1,8]{2,1,0:T(1,128)} %param.12) | copy-start | bytes 100
  41.9 30.0 %collective-permute-start.5 = (bf16[4,2,64,1024]{3,2,1,0:T(8,128)(2,1)S(1)}, bf16[4,2,64,1024]{3,2,1,0:T(8,128)(2,1)S(1)}, u32[]{:S(2)}, u32[]{:S(2)}) collective-permute-start(bf16[4,2,64,1024]{3,2,1,0:T(8,128)(2,1)S(1)} %pad_maximum_fusion.refs_0_), channel_id=1, source_target_pairs={{0,1},{1,2},{2,3},{3,0},{4,5},{5,6},{6,7},{7,4},{8,9},{9,10},{10,1... | collective-permute-start | bytes 3145736 | tf_op jit(solution)/shard_map/ppermute | solution.py:39
  44.0 27.9 %collective-permute-start.6 = (bf16[4,2,64,1024]{3,2,1,0:T(8,128)(2,1)S(1)}, bf16[4,2,64,1024]{3,2,1,0:T(8,128)(2,1)}, u32[]{:S(2)}, u32[]{:S(2)}) collective-permute-start(bf16[4,2,64,1024]{3,2,1,0:T(8,128)(2,1)S(1)} %pad_maximum_fusion.1.refs_1_), channel_id=1, source_target_pairs={{0,3},{1,0},{2,1},{3,2},{4,7},{5,4},{6,5},{7,6},{8,11},{9,8},{10,9... | collective-permute-start | bytes 3145736 | tf_op jit(solution)/shard_map/ppermute | solution.py:39
  53.7 0.9 copy-start.1
  54.6 17.3 %collective-permute-start.8 = (bf16[8,96,256]{2,1,0:T(8,128)(2,1)}, bf16[8,96,256]{2,1,0:T(8,128)(2,1)S(1)}, u32[]{:S(2)}, u32[]{:S(2)}) collective-permute-start(bf16[8,96,256]{2,1,0:T(8,128)(2,1)} %slice.49), channel_id=1, source_target_pairs={{0,96},{16,112},{32,0},{48,16},{64,32},{80,48},{96,64},{112,80},{1... | collective-permute-start | bytes 1179656 | tf_op jit(solution)/shard_map/ppermute | solution.py:29
  58.3 0.9 copy-start.3
  59.2 12.7 %collective-permute-start.7 = (bf16[8,96,256]{2,1,0:T(8,128)(2,1)}, bf16[8,96,256]{2,1,0:T(8,128)(2,1)}, u32[]{:S(2)}, u32[]{:S(2)}) collective-permute-start(bf16[8,96,256]{2,1,0:T(8,128)(2,1)} %slice.48), channel_id=1, source_target_pairs={{0,32},{16,48},{32,64},{48,80},{64,96},{80,112},{96,0},{112,16},{1... | collective-permute-start | bytes 1179656 | tf_op jit(solution)/shard_map/ppermute | solution.py:29
  69.0 2.9 %copy-start.2 = (bf16[16,96,256]{2,1,0:T(8,128)(2,1)S(1)}, bf16[16,96,256]{2,1,0:T(8,128)(2,1)}, u32[]{:S(2)}) copy-start(bf16[16,96,256]{2,1,0:T(8,128)(2,1)} %copy-done.1) | copy-start | bytes 2359300
  69.0 2.9 %copy-start.4 = (bf16[16,96,256]{2,1,0:T(8,128)(2,1)S(1)}, bf16[16,96,256]{2,1,0:T(8,128)(2,1)}, u32[]{:S(2)}) copy-start(bf16[16,96,256]{2,1,0:T(8,128)(2,1)} %copy-done.3) | copy-start | bytes 2359300
  77.6 4.3 %collective-permute-start.9 = (bf16[16,96,512]{2,1,0:T(8,128)(2,1)S(1)}, bf16[16,96,512]{2,1,0:T(8,128)(2,1)S(1)}, u32[]{:S(2)}, u32[]{:S(2)}) collective-permute-start(bf16[16,96,512]{2,1,0:T(8,128)(2,1)S(1)} %get-tuple-element.29), channel_id=1, source_target_pairs={{0,16},{16,0},{32,48},{48,32},{64,80},{80,64},{96,112},{112,96},{1... | collective-permute-start | bytes 4718600 | tf_op jit(solution)/shard_map/ppermute | solution.py:34
  77.7 22.3 %collective-permute-start.12 = (bf16[16,96,256]{2,1,0:T(8,128)(2,1)}, bf16[16,96,256]{2,1,0:T(8,128)(2,1)}, u32[]{:S(2)}, u32[]{:S(2)}) collective-permute-start(bf16[16,96,256]{2,1,0:T(8,128)(2,1)} %slice.41.refs_4_), channel_id=1, source_target_pairs={{0,64},{16,80},{32,96},{48,112},{64,0},{80,16},{96,32},{112,48},{1... | collective-permute-start | bytes 2359304 | tf_op jit(solution)/shard_map/ppermute | solution.py:29
  79.2 37.7 %collective-permute-start.11 = (bf16[16,96,256]{2,1,0:T(8,128)(2,1)}, bf16[16,96,256]{2,1,0:T(8,128)(2,1)}, u32[]{:S(2)}, u32[]{:S(2)}) collective-permute-start(bf16[16,96,256]{2,1,0:T(8,128)(2,1)} %slice.41.refs_4_), channel_id=1, source_target_pairs={{0,96},{16,112},{32,0},{48,16},{64,32},{80,48},{96,64},{112,80},{1... | collective-permute-start | bytes 2359304 | tf_op jit(solution)/shard_map/ppermute | solution.py:29
  81.1 35.8 %collective-permute-start.10 = (bf16[16,96,256]{2,1,0:T(8,128)(2,1)}, bf16[16,96,256]{2,1,0:T(8,128)(2,1)}, u32[]{:S(2)}, u32[]{:S(2)}) collective-permute-start(bf16[16,96,256]{2,1,0:T(8,128)(2,1)} %slice.41.refs_4_), channel_id=1, source_target_pairs={{0,32},{16,48},{32,64},{48,80},{64,96},{80,112},{96,0},{112,16},{1... | collective-permute-start | bytes 2359304 | tf_op jit(solution)/shard_map/ppermute | solution.py:29
  83.1 1.3 copy-start
  84.4 43.1 %all-to-all-start.2 = ((bf16[128,16,512]{2,1,0:T(8,128)(2,1)}), bf16[128,16,512]{2,1,0:T(8,128)(2,1)}, u32[]{:S(2)}, u32[]{:S(2)}) async-start(bf16[128,16,512]{2,1,0:T(8,128)(2,1)} %copy-done), calls=%async_computation.2 | async-start | bytes 4194304 | tf_op jit(solution)/shard_map/all_to_all | solution.py:49
  122.8 3.5 %collective-permute-start.13 = (bf16[16,96,512]{2,1,0:T(8,128)(2,1)S(1)}, bf16[16,96,512]{2,1,0:T(8,128)(2,1)S(1)}, u32[]{:S(2)}, u32[]{:S(2)}) collective-permute-start(bf16[16,96,512]{2,1,0:T(8,128)(2,1)S(1)} %get-tuple-element.33), channel_id=1, source_target_pairs={{0,16},{16,0},{32,48},{48,32},{64,80},{80,64},{96,112},{112,96},{1... | collective-permute-start | bytes 4718600 | tf_op jit(solution)/shard_map/ppermute | solution.py:34

commit v6 on v4

--- a/solution.py
+++ b/solution.py
@@ -260,7 +260,7 @@
             ],
         ),
         out_shape=[jax.ShapeDtypeStruct((owner_total, size, size), kind), stats, stats],
-        compiler_params=pltpu.CompilerParams(vmem_limit_bytes=50 * MIB),
+        compiler_params=pltpu.CompilerParams(vmem_limit_bytes=36 * MIB),
         cost_estimate=pl.CostEstimate(
             flops=8 * slot_total * size**3,
             bytes_accessed=12 * slot_total * size * size,

time: 279 us -> 280 us (level)
  no operation moved by 1% of the time
where the time goes in v6:
time: 280 us; the launch traced here: 279 us
  blocking collectives  132 us (47%)
  waiting for transfers between devices  56.1 us (20%)
  Pallas kernels  35.4 us (13%)
  starting transfers between devices  34.9 us (12%)
  local copies, waits for them, and re-layouts  12.5 us (4%)
  other arithmetic  6.6 us (2%)
    all_to_all x2, blocking collectives, exchange(): return lax.all_to_all(value, 'mp', split_axis=0, concat_axis=0, tiled=True)  132 us
    ppermute x10, waiting for transfers between devices, along_y(): return lax.ppermute(value, 'dp', pairs)  32.9 us
    all_to_all x3, starting transfers between devices, exchange(): return lax.all_to_all(value, 'mp', split_axis=0, concat_axis=0, tiled=True)  16.9 us
    pallas_call x2, Pallas kernels, gradient_partials(): pl.pallas_call(partial_kernel, in_specs=[pl.BlockSpec(memory_space=pltpu....  14.6 us
    ppermute x10, starting transfers between devices, along_y(): return lax.ppermute(value, 'dp', pairs)  14.5 us
    pallas_call x1, Pallas kernels, work_on_slots(): pl.pallas_call(slot_kernel, grid_spec=pltpu.PrefetchScalarGridSpec(num_sc...  12.3 us
    all_to_all x3, waiting for transfers between devices, exchange(): return lax.all_to_all(value, 'mp', split_axis=0, concat_axis=0, tiled=True)  10.3 us
    ppermute x2, waiting for transfers between devices, along_z(): return lax.ppermute(value, 'mp', pairs)  9.47 us
  transfers between devices with their start and end apart: 17, of which 7 were waited for; matrix products, arithmetic and copies ran while one was open for 4% of the time, Pallas kernels for 5%

profile of v6, /device:TPU:0, one launch (start us, length us, event | category | flops | bytes accessed | tf_op | source)
XLA Modules:
  0.0 279.1 jit_solution(17694012323894810603)
XLA Ops:
  0.7 1.8 dynamic-slice_bitcast_fusion
  2.6 1.7 collective-permute-start.2
  4.3 1.6 collective-permute-start.3
  6.0 0.8 pad_maximum_fusion.4
  6.8 2.2 split_cotangents.1
  9.0 8.0 %all-to-all-start = ((bf16[16,96,256]{2,1,0:T(8,128)(2,1)}), bf16[16,96,256]{2,1,0:T(8,128)(2,1)S(1)}, u32[]{:S(2)}, u32[]{:S(2)}) async-start(bf16[16,96,256]{2,1,0:T(8,128)(2,1)} %get-tuple-element.23), calls=%async_computation | async-start | bytes 1572864 | tf_op jit(solution)/shard_map/all_to_all | solution.py:49
  17.0 2.1 collective-permute-start.4
  19.0 0.7 fusion.1
  19.8 0.7 fusion.2
  20.5 10.3 %all-to-all-done.refs_4_ = bf16[16,96,256]{2,1,0:T(8,128)(2,1)S(1)} async-done(((bf16[16,96,256]{2,1,0:T(8,128)(2,1)}), bf16[16,96,256]{2,1,0:T(8,128)(2,1)S(1)}, u32[]{:S(2)}, u32[]{:S(2)}) %all-to-all-start) | async-done | bytes 786464 | tf_op jit(solution)/shard_map/all_to_all | solution.py:49
  30.8 4.3 %all-to-all-start.1 = ((bf16[16,112,256]{2,1,0:T(8,128)(2,1)}), bf16[16,112,256]{2,1,0:T(8,128)(2,1)}, u32[]{:S(2)}, u32[]{:S(2)}) async-start(bf16[16,112,256]{2,1,0:T(8,128)(2,1)} %get-tuple-element.24), calls=%async_computation.1 | async-start | bytes 1835008 | tf_op jit(solution)/shard_map/all_to_all | solution.py:49
  35.1 1.8 collective-permute-start.1
  36.9 0.3 collective-permute-start
  37.2 1.1 fusion.3
  38.3 2.2 pad_maximum_fusion.refs_0_
  40.4 1.7 collective-permute-start.5
  42.1 1.1 pad_maximum_fusion.1.refs_1_
  43.2 1.6 collective-permute-start.6
  45.5 7.1 %collective-permute-done.1.refs_6_ = bf16[16,96,256]{2,1,0:T(8,128)(2,1)S(1)} collective-permute-done((bf16[16,96,256]{2,1,0:T(8,128)(2,1)S(1)}, bf16[16,96,256]{2,1,0:T(8,128)(2,1)S(1)}, u32[]{:S(2)}, u32[]{:S(2)}) %collective-permute-start.1) | collective-permute-done | bytes 786464 | tf_op jit(solution)/shard_map/ppermute | solution.py:29
  52.6 0.8 slice.49
  53.4 2.9 %collective-permute-start.8 = (bf16[8,96,256]{2,1,0:T(8,128)(2,1)}, bf16[8,96,256]{2,1,0:T(8,128)(2,1)S(1)}, u32[]{:S(2)}, u32[]{:S(2)}) collective-permute-start(bf16[8,96,256]{2,1,0:T(8,128)(2,1)} %slice.49), channel_id=1, source_target_pairs={{0,96},{16,112},{32,0},{48,16},{64,32},{80,48},{96,64},{112,80},{1... | collective-permute-start | bytes 1179656 | tf_op jit(solution)/shard_map/ppermute | solution.py:29
  56.4 0.8 slice.48
  57.1 0.8 slice_convert_fusion
  57.9 1.1 multiply_reduce_fusion.1
  59.1 0.1 copy.14
  59.4 0.2 select_reduce_fusion
  59.9 1.2 slice.41.refs_4_
  61.1 9.5 %collective-permute-done.5.refs_2_ = bf16[4,2,64,1024]{3,2,1,0:T(8,128)(2,1)} collective-permute-done((bf16[4,2,64,1024]{3,2,1,0:T(8,128)(2,1)}, bf16[4,2,64,1024]{3,2,1,0:T(8,128)(2,1)}, u32[]{:S(2)}, u32[]{:S(2)}) %collective-permute-start.5) | collective-permute-done | bytes 1048608 | tf_op jit(solution)/shard_map/ppermute | solution.py:39
  70.6 7.3 %gradient_partials.2 = (bf16[16,96,512]{2,1,0:T(8,128)(2,1)}, bf16[16,96,512]{2,1,0:T(8,128)(2,1)}) custom-call(s32[2]{0:T(128)S(1)} %pad_add_fusion.here_ref, bf16[4,2,64,1024]{3,2,1,0:T(8,128)(2,1)} %pad_maximum_fusion.refs_0_, bf16[4,2,64,1024]{3,2,1,0:T(8,128)(2,1)} %pad_maximum_fusion.1.refs_1_, ...), custom_call_target="tpu_custom_call" | custom-call | bytes 1024 | tf_op jit(solution)/shard_map/gradient_partials/pallas_call | solution.py:144
  78.0 2.0 collective-permute-start.12
  80.0 1.1 collective-permute-start.11
  81.0 1.0 collective-permute-start.10
  82.0 1.4 copy-done.1
  83.4 2.6 deal_to_slots.2
  86.0 4.6 %all-to-all-start.2 = ((bf16[128,16,512]{2,1,0:T(8,128)(2,1)}), bf16[128,16,512]{2,1,0:T(8,128)(2,1)}, u32[]{:S(2)}, u32[]{:S(2)}) async-start(bf16[128,16,512]{2,1,0:T(8,128)(2,1)} %deal_to_slots.2), calls=%async_computation.2 | async-start | bytes 4194304 | tf_op jit(solution)/shard_map/all_to_all | solution.py:49
  90.6 9.4 %collective-permute-done.12.refs_7_ = bf16[16,96,256]{2,1,0:T(8,128)(2,1)S(1)} collective-permute-done((bf16[16,96,256]{2,1,0:T(8,128)(2,1)S(1)}, bf16[16,96,256]{2,1,0:T(8,128)(2,1)S(1)}, u32[]{:S(2)}, u32[]{:S(2)}) %collective-permute-start.12) | collective-permute-done | bytes 786464 | tf_op jit(solution)/shard_map/ppermute | solution.py:29
  100.0 15.4 %collective-permute-done.11.refs_6_ = bf16[16,96,256]{2,1,0:T(8,128)(2,1)S(1)} collective-permute-done((bf16[16,96,256]{2,1,0:T(8,128)(2,1)S(1)}, bf16[16,96,256]{2,1,0:T(8,128)(2,1)S(1)}, u32[]{:S(2)}, u32[]{:S(2)}) %collective-permute-start.11) | collective-permute-done | bytes 786464 | tf_op jit(solution)/shard_map/ppermute | solution.py:29
  115.4 0.9 collective-permute-done.10.refs_5_
  116.3 7.2 %gradient_partials.3 = (bf16[16,96,512]{2,1,0:T(8,128)(2,1)}, bf16[16,96,512]{2,1,0:T(8,128)(2,1)}) custom-call(s32[2]{0:T(128)S(1)} %pad_add_fusion.here_ref, bf16[4,2,64,1024]{3,2,1,0:T(8,128)(2,1)} %pad_maximum_fusion.refs_0_, bf16[4,2,64,1024]{3,2,1,0:T(8,128)(2,1)} %pad_maximum_fusion.1.refs_1_, ...), custom_call_target="tpu_custom_call" | custom-call | bytes 1024 | tf_op jit(solution)/shard_map/gradient_partials/pallas_call | solution.py:144
  123.6 0.2 collective-permute-start.13
  123.8 3.5 %collective-permute-done.13.got_ref = bf16[16,96,512]{2,1,0:T(8,128)(2,1)S(1)} collective-permute-done((bf16[16,96,512]{2,1,0:T(8,128)(2,1)}, bf16[16,96,512]{2,1,0:T(8,128)(2,1)S(1)}, u32[]{:S(2)}, u32[]{:S(2)}) %collective-permute-start.13) | collective-permute-done | bytes 1572896 | tf_op jit(solution)/shard_map/ppermute | solution.py:34
  127.3 1.4 copy-done.2
  128.7 1.2 deal_to_slots.3
  129.9 33.0 %all_to_all.25 = bf16[128,16,512]{2,1,0:T(8,128)(2,1)S(1)} all-to-all(bf16[128,16,512]{2,1,0:T(8,128)(2,1)S(1)} %deal_to_slots.3), channel_id=1, replica_groups=mesh['dp'=8,'mp'=16] {'mp'}, dimensions={0} | all-to-all | bytes 4194304 | tf_op jit(solution)/shard_map/all_to_all | solution.py:49
  163.0 2.2 copy-done.5
  165.2 12.3 %work_on_slots.1 = (bf16[16,512,512]{2,1,0:T(8,128)(2,1)}, bf16[8,512,512]{2,1,0:T(8,128)(2,1)}, bf16[8,512,512]{2,1,0:T(8,128)(2,1)}) custom-call(s32[8]{0:T(128)S(1)} %compare_select_fusion.source_ref, bf16[8,512,512]{2,1,0:T(8,128)(2,1)S(1)} %bitcast.33, bf16[8,512,512]{2,1,0:T(8,128)(2,1)S(1)} %bitcast.34, bf16[16,8,16,512]{3,2,1,0:T(8,128)(2,1)} %bitcast.16.first_ref, ...), custom_call_target="tpu_custom_call" | custom-call | flops 8589934592 | bytes 25165824 | tf_op jit(solution)/shard_map/work_on_slots/pallas_call | solution.py:244
  177.5 98.9 %all_to_all.26.returned_ref = bf16[16,512,512]{2,1,0:T(8,128)(2,1)S(1)} all-to-all(bf16[16,512,512]{2,1,0:T(8,128)(2,1)} %get-tuple-element.36), channel_id=1, replica_groups=mesh['dp'=8,'mp'=16] {'mp'}, dimensions={0} | all-to-all | bytes 16777216 | tf_op jit(solution)/shard_map/all_to_all | solution.py:49
  276.4 2.5 place_blocks.1
  (34 shorter events, 0.8 us)
Async XLA Ops:
  2.5 4.4 %copy-start = (bf16[2,256,1536]{2,1,0:T(8,128)(2,1)S(1)}, bf16[2,256,1536]{2,1,0:T(8,128)(2,1)}, u32[]{:S(2)}) copy-start(bf16[2,256,1536]{2,1,0:T(8,128)(2,1)} %cot_ref) | copy-start | bytes 4718596
  2.5 4.3 %copy-start.3 = (s32[1,1,6]{2,1,0:T(1,128)S(1)}, s32[1,1,6]{2,1,0:T(1,128)}, u32[]{:S(2)}) copy-start(s32[1,1,6]{2,1,0:T(1,128)} %param.11) | copy-start | bytes 76
  2.6 16.5 %collective-permute-start.2 = (bf16[2,2,64,1024]{3,2,1,0:T(8,128)(2,1)S(1)}, bf16[2,2,64,1024]{3,2,1,0:T(8,128)(2,1)S(1)}, u32[]{:S(2)}, u32[]{:S(2)}) collective-permute-start(bf16[2,2,64,1024]{3,2,1,0:T(8,128)(2,1)S(1)} %pad_maximum_fusion.2), channel_id=1, source_target_pairs={{0,32},{16,48},{32,64},{48,80},{64,96},{80,112},{96,0},{112,16},{1... | collective-permute-start | bytes 1572872 | tf_op jit(solution)/shard_map/ppermute | solution.py:29
  4.3 15.4 %collective-permute-start.3 = (bf16[2,2,64,1024]{3,2,1,0:T(8,128)(2,1)S(1)}, bf16[2,2,64,1024]{3,2,1,0:T(8,128)(2,1)S(1)}, u32[]{:S(2)}, u32[]{:S(2)}) collective-permute-start(bf16[2,2,64,1024]{3,2,1,0:T(8,128)(2,1)S(1)} %pad_maximum_fusion.3), channel_id=1, source_target_pairs={{0,96},{16,112},{32,0},{48,16},{64,32},{80,48},{96,64},{112,80},{1... | collective-permute-start | bytes 1572872 | tf_op jit(solution)/shard_map/ppermute | solution.py:29
  9.0 21.8 %all-to-all-start = ((bf16[16,96,256]{2,1,0:T(8,128)(2,1)}), bf16[16,96,256]{2,1,0:T(8,128)(2,1)S(1)}, u32[]{:S(2)}, u32[]{:S(2)}) async-start(bf16[16,96,256]{2,1,0:T(8,128)(2,1)} %get-tuple-element.23), calls=%async_computation | async-start | bytes 1572864 | tf_op jit(solution)/shard_map/all_to_all | solution.py:49
  17.0 20.2 %collective-permute-start.4 = (bf16[2,2,64,1024]{3,2,1,0:T(8,128)(2,1)}, bf16[2,2,64,1024]{3,2,1,0:T(8,128)(2,1)}, u32[]{:S(2)}, u32[]{:S(2)}) collective-permute-start(bf16[2,2,64,1024]{3,2,1,0:T(8,128)(2,1)} %pad_maximum_fusion.4), channel_id=1, source_target_pairs={{0,64},{16,80},{32,96},{48,112},{64,0},{80,16},{96,32},{112,48},{1... | collective-permute-start | bytes 1572872 | tf_op jit(solution)/shard_map/ppermute | solution.py:29
  30.8 26.4 %all-to-all-start.1 = ((bf16[16,112,256]{2,1,0:T(8,128)(2,1)}), bf16[16,112,256]{2,1,0:T(8,128)(2,1)}, u32[]{:S(2)}, u32[]{:S(2)}) async-start(bf16[16,112,256]{2,1,0:T(8,128)(2,1)} %get-tuple-element.24), calls=%async_computation.1 | async-start | bytes 1835008 | tf_op jit(solution)/shard_map/all_to_all | solution.py:49
  35.1 17.6 %collective-permute-start.1 = (bf16[16,96,256]{2,1,0:T(8,128)(2,1)S(1)}, bf16[16,96,256]{2,1,0:T(8,128)(2,1)S(1)}, u32[]{:S(2)}, u32[]{:S(2)}) collective-permute-start(bf16[16,96,256]{2,1,0:T(8,128)(2,1)S(1)} %all-to-all-done.refs_4_), channel_id=1, source_target_pairs={{0,96},{16,112},{32,0},{48,16},{64,32},{80,48},{96,64},{112,80},{1... | collective-permute-start | bytes 2359304 | tf_op jit(solution)/shard_map/ppermute | solution.py:29
  36.9 19.5 %collective-permute-start = (bf16[16,96,256]{2,1,0:T(8,128)(2,1)S(1)}, bf16[16,96,256]{2,1,0:T(8,128)(2,1)S(1)}, u32[]{:S(2)}, u32[]{:S(2)}) collective-permute-start(bf16[16,96,256]{2,1,0:T(8,128)(2,1)S(1)} %all-to-all-done.refs_4_), channel_id=1, source_target_pairs={{0,32},{16,48},{32,64},{48,80},{64,96},{80,112},{96,0},{112,16},{1... | collective-permute-start | bytes 2359304 | tf_op jit(solution)/shard_map/ppermute | solution.py:29
  38.3 7.2 %copy-start.6 = (s32[1,1,8]{2,1,0:T(1,128)S(1)}, s32[1,1,8]{2,1,0:T(1,128)}, u32[]{:S(2)}) copy-start(s32[1,1,8]{2,1,0:T(1,128)} %param.12) | copy-start | bytes 100
  40.4 30.1 %collective-permute-start.5 = (bf16[4,2,64,1024]{3,2,1,0:T(8,128)(2,1)}, bf16[4,2,64,1024]{3,2,1,0:T(8,128)(2,1)}, u32[]{:S(2)}, u32[]{:S(2)}) collective-permute-start(bf16[4,2,64,1024]{3,2,1,0:T(8,128)(2,1)} %pad_maximum_fusion.refs_0_), channel_id=1, source_target_pairs={{0,1},{1,2},{2,3},{3,0},{4,5},{5,6},{6,7},{7,4},{8,9},{9,10},{10,1... | collective-permute-start | bytes 3145736 | tf_op jit(solution)/shard_map/ppermute | solution.py:39
  43.2 27.3 %collective-permute-start.6 = (bf16[4,2,64,1024]{3,2,1,0:T(8,128)(2,1)}, bf16[4,2,64,1024]{3,2,1,0:T(8,128)(2,1)}, u32[]{:S(2)}, u32[]{:S(2)}) collective-permute-start(bf16[4,2,64,1024]{3,2,1,0:T(8,128)(2,1)} %pad_maximum_fusion.1.refs_1_), channel_id=1, source_target_pairs={{0,3},{1,0},{2,1},{3,2},{4,7},{5,4},{6,5},{7,6},{8,11},{9,8},{10,9... | collective-permute-start | bytes 3145736 | tf_op jit(solution)/shard_map/ppermute | solution.py:39
  53.4 17.1 %collective-permute-start.8 = (bf16[8,96,256]{2,1,0:T(8,128)(2,1)}, bf16[8,96,256]{2,1,0:T(8,128)(2,1)S(1)}, u32[]{:S(2)}, u32[]{:S(2)}) collective-permute-start(bf16[8,96,256]{2,1,0:T(8,128)(2,1)} %slice.49), channel_id=1, source_target_pairs={{0,96},{16,112},{32,0},{48,16},{64,32},{80,48},{96,64},{112,80},{1... | collective-permute-start | bytes 1179656 | tf_op jit(solution)/shard_map/ppermute | solution.py:29
  57.1 13.4 %collective-permute-start.7 = (bf16[8,96,256]{2,1,0:T(8,128)(2,1)}, bf16[8,96,256]{2,1,0:T(8,128)(2,1)}, u32[]{:S(2)}, u32[]{:S(2)}) collective-permute-start(bf16[8,96,256]{2,1,0:T(8,128)(2,1)} %slice.48), channel_id=1, source_target_pairs={{0,32},{16,48},{32,64},{48,80},{64,96},{80,112},{96,0},{112,16},{1... | collective-permute-start | bytes 1179656 | tf_op jit(solution)/shard_map/ppermute | solution.py:29
  77.9 4.1 %collective-permute-start.9 = (bf16[16,96,512]{2,1,0:T(8,128)(2,1)}, bf16[16,96,512]{2,1,0:T(8,128)(2,1)S(1)}, u32[]{:S(2)}, u32[]{:S(2)}) collective-permute-start(bf16[16,96,512]{2,1,0:T(8,128)(2,1)} %get-tuple-element.29), channel_id=1, source_target_pairs={{0,16},{16,0},{32,48},{48,32},{64,80},{80,64},{96,112},{112,96},{1... | collective-permute-start | bytes 4718600 | tf_op jit(solution)/shard_map/ppermute | solution.py:34
  78.0 22.0 %collective-permute-start.12 = (bf16[16,96,256]{2,1,0:T(8,128)(2,1)S(1)}, bf16[16,96,256]{2,1,0:T(8,128)(2,1)S(1)}, u32[]{:S(2)}, u32[]{:S(2)}) collective-permute-start(bf16[16,96,256]{2,1,0:T(8,128)(2,1)S(1)} %slice.41.refs_4_), channel_id=1, source_target_pairs={{0,64},{16,80},{32,96},{48,112},{64,0},{80,16},{96,32},{112,48},{1... | collective-permute-start | bytes 2359304 | tf_op jit(solution)/shard_map/ppermute | solution.py:29
  80.0 35.4 %collective-permute-start.11 = (bf16[16,96,256]{2,1,0:T(8,128)(2,1)S(1)}, bf16[16,96,256]{2,1,0:T(8,128)(2,1)S(1)}, u32[]{:S(2)}, u32[]{:S(2)}) collective-permute-start(bf16[16,96,256]{2,1,0:T(8,128)(2,1)S(1)} %slice.41.refs_4_), channel_id=1, source_target_pairs={{0,96},{16,112},{32,0},{48,16},{64,32},{80,48},{96,64},{112,80},{1... | collective-permute-start | bytes 2359304 | tf_op jit(solution)/shard_map/ppermute | solution.py:29
  81.0 35.3 %collective-permute-start.10 = (bf16[16,96,256]{2,1,0:T(8,128)(2,1)S(1)}, bf16[16,96,256]{2,1,0:T(8,128)(2,1)S(1)}, u32[]{:S(2)}, u32[]{:S(2)}) collective-permute-start(bf16[16,96,256]{2,1,0:T(8,128)(2,1)S(1)} %slice.41.refs_4_), channel_id=1, source_target_pairs={{0,32},{16,48},{32,64},{48,80},{64,96},{80,112},{96,0},{112,16},{1... | collective-permute-start | bytes 2359304 | tf_op jit(solution)/shard_map/ppermute | solution.py:29
  82.0 1.4 copy-start.1
  86.0 44.0 %all-to-all-start.2 = ((bf16[128,16,512]{2,1,0:T(8,128)(2,1)}), bf16[128,16,512]{2,1,0:T(8,128)(2,1)}, u32[]{:S(2)}, u32[]{:S(2)}) async-start(bf16[128,16,512]{2,1,0:T(8,128)(2,1)} %deal_to_slots.2), calls=%async_computation.2 | async-start | bytes 4194304 | tf_op jit(solution)/shard_map/all_to_all | solution.py:49
  123.6 3.7 %collective-permute-start.13 = (bf16[16,96,512]{2,1,0:T(8,128)(2,1)}, bf16[16,96,512]{2,1,0:T(8,128)(2,1)S(1)}, u32[]{:S(2)}, u32[]{:S(2)}) collective-permute-start(bf16[16,96,512]{2,1,0:T(8,128)(2,1)} %get-tuple-element.33), channel_id=1, source_target_pairs={{0,16},{16,0},{32,48},{48,32},{64,80},{80,64},{96,112},{112,96},{1... | collective-permute-start | bytes 4718600 | tf_op jit(solution)/shard_map/ppermute | solution.py:34
  127.3 1.4 copy-start.2
  129.9 33.1 %copy-start.4 = (bf16[1,1,8,512,512]{4,3,2,1,0:T(8,128)(2,1)S(1)}, bf16[1,1,8,512,512]{4,3,2,1,0:T(8,128)(2,1)}, u32[]{:S(2)}) copy-start(bf16[1,1,8,512,512]{4,3,2,1,0:T(8,128)(2,1)} %param.9) | copy-start | bytes 12582916
  163.0 2.2 copy-start.5
